TPU v7x, 32 devices: a whole 2x2x4 slice. The times are simulated.
32 devices in a mesh: dp: 8 (over z, x), tensor: 4 (over y, core).
Axes of the slice: x: 2, y: 2, z: 4, core: 2. Of those that a mesh axis runs over, the one named last changes fastest.
Arguments:
- tokens: bfloat16 [16384, 1024], P('dp'), may hold values from -6 to 6
- cotangent: bfloat16 [16384, 1024], P('dp'), may hold values from -6 to 6
- lengths: int32 [8], P('dp'), may hold values from 200 to 2048, as said below
- joint_weight: float32 [1024, 3072], P('dp', 'tensor'), as said below
- output_weight: float32 [1024, 1024], P('tensor', 'dp'), as said below
- widen_weight: float32 [1024, 4096], P('dp', 'tensor'), as said below
- narrow_weight: float32 [4096, 1024], P('tensor', 'dp'), as said below
- shared_vectors: float32 [6, 1024], P(None, 'dp'), as said below
- split_vectors: float32 [4, 1536], P('tensor', 'dp'), may hold values from -1.75 to 1.75
- joint_first: float32 [1024, 3072], P('dp', 'tensor'), may hold values from -0.00018310547 to 0.00018310547
- joint_second: float32 [1024, 3072], P('dp', 'tensor'), may hold values from 4.207952e-09 to 1.6673019e-08
- output_first: float32 [1024, 1024], P('tensor', 'dp'), may hold values from -0.00018310547 to 0.00018310547
- output_second: float32 [1024, 1024], P('tensor', 'dp'), may hold values from 4.207952e-09 to 1.6673019e-08
- widen_first: float32 [1024, 4096], P('dp', 'tensor'), may hold values from -0.00018310547 to 0.00018310547
- widen_second: float32 [1024, 4096], P('dp', 'tensor'), may hold values from 4.207952e-09 to 1.6673019e-08
- narrow_first: float32 [4096, 1024], P('tensor', 'dp'), may hold values from -0.00018310547 to 0.00018310547
- narrow_second: float32 [4096, 1024], P('tensor', 'dp'), may hold values from 4.207952e-09 to 1.6673019e-08
- shared_first: float32 [6, 1024], P(None, 'dp'), may hold values from -0.00048828125 to 0.00048828125
- shared_second: float32 [6, 1024], P(None, 'dp'), may hold values from 3.7315804e-08 to 1.5085112e-07
- split_first: float32 [4, 1536], P('tensor', 'dp'), may hold values from -0.00048828125 to 0.00048828125
- split_second: float32 [4, 1536], P('tensor', 'dp'), may hold values from 3.7315804e-08 to 1.5085112e-07
Outputs:
- layer_output: bfloat16 [16384, 1024], P('dp')
- input_grad: bfloat16 [16384, 1024], P('dp')
- grad_norm: float32 [], replicated
- joint_master: float32 [1024, 3072], P('dp', 'tensor')
- joint_moment: float32 [1024, 3072], P('dp', 'tensor')
- joint_variance: float32 [1024, 3072], P('dp', 'tensor')
- output_master: float32 [1024, 1024], P('tensor', 'dp')
- output_moment: float32 [1024, 1024], P('tensor', 'dp')
- output_variance: float32 [1024, 1024], P('tensor', 'dp')
- widen_master: float32 [1024, 4096], P('dp', 'tensor')
- widen_moment: float32 [1024, 4096], P('dp', 'tensor')
- widen_variance: float32 [1024, 4096], P('dp', 'tensor')
- narrow_master: float32 [4096, 1024], P('tensor', 'dp')
- narrow_moment: float32 [4096, 1024], P('tensor', 'dp')
- narrow_variance: float32 [4096, 1024], P('tensor', 'dp')
- shared_master: float32 [6, 1024], P(None, 'dp')
- shared_moment: float32 [6, 1024], P(None, 'dp')
- shared_variance: float32 [6, 1024], P(None, 'dp')
- split_master: float32 [4, 1536], P('tensor', 'dp')
- split_moment: float32 [4, 1536], P('tensor', 'dp')
- split_variance: float32 [4, 1536], P('tensor', 'dp')
Inputs may be any that keep to these rules, and one draw needn't show every extreme that they name: `lengths`: one sequence's length in its row of 2048 slots. `joint_weight`: master weights. `output_weight`: master weights. `widen_weight`: master weights. `narrow_weight`: master weights. `shared_vectors`: gains and shifts.
All inputs are finite; a program needn't handle non-finite values.
Results may differ from a plain program's by a relative error of at most 0.02.
The roundings to bfloat16 on the way count: a program that leaves them out, or rounds other values in their place, can miss the bound.
Values may be sent and summed in bfloat16 or wider, within the bound.
A program may use at most 256 MiB of HBM per device.

v0:
```python
import math

import jax
import jax.numpy as jnp
from jax import lax
from jax.sharding import PartitionSpec as P

D = 1024
HEADS = 16
STEP = 10


NORM_EPSILON = 1e-05
CLIP_LIMIT = 1.0
BETA_FIRST = 0.9
BETA_SECOND = 0.95
ADAM_EPSILON = 1e-08
MATRIX_RATE = 0.05
OUTPUT_RATE = 0.2
VECTOR_RATE = 0.6
MATRIX_DECAY = 0.1
MASKED_SCORE = -1e30


def normalize(values):
    centred = values - jnp.mean(values, axis=-1, keepdims=True)
    inverse = lax.rsqrt(jnp.mean(centred * centred, axis=-1, keepdims=True) + NORM_EPSILON)
    return (centred * inverse, inverse)


def normalize_back(incoming, normed, inverse, gain):
    scaled = incoming * gain
    return inverse * (
        scaled
        - jnp.mean(scaled, axis=-1, keepdims=True)
        - normed * jnp.mean(scaled * normed, axis=-1, keepdims=True)
    )


def over_rows(left, right):
    return lax.dot_general(
        left, right, (((0,), (0,)), ((), ())), preferred_element_type=jnp.float32
    )


def against_rows(left, right):
    return lax.dot_general(
        left, right, (((1,), (1,)), ((), ())), preferred_element_type=jnp.float32
    )


def gelu_tanh(values):
    return jax.nn.gelu(values, approximate=True)


def adam_step(master, moment, variance, gradient, rate, decay):
    moment_new = BETA_FIRST * moment + (1.0 - BETA_FIRST) * gradient
    variance_new = BETA_SECOND * variance + (1.0 - BETA_SECOND) * gradient * gradient
    moment_hat = moment_new / (1.0 - BETA_FIRST**STEP)
    variance_hat = variance_new / (1.0 - BETA_SECOND**STEP)
    master_new = master - rate * (
        moment_hat / (jnp.sqrt(variance_hat) + ADAM_EPSILON) + decay * master
    )
    return (master_new, moment_new, variance_new)


def on_device(
    tokens,
    cotangent,
    lengths,
    joint_weight,
    output_weight,
    widen_weight,
    narrow_weight,
    shared_vectors,
    split_vectors,
    joint_first,
    joint_second,
    output_first,
    output_second,
    widen_first,
    widen_second,
    narrow_first,
    narrow_second,
    shared_first,
    shared_second,
    split_first,
    split_second,
):
    gathered = (
        lax.all_gather(joint_weight.astype(jnp.bfloat16), "dp", axis=0, tiled=True),
        lax.all_gather(output_weight.astype(jnp.bfloat16), "dp", axis=1, tiled=True),
        lax.all_gather(widen_weight.astype(jnp.bfloat16), "dp", axis=0, tiled=True),
        lax.all_gather(narrow_weight.astype(jnp.bfloat16), "dp", axis=1, tiled=True),
        lax.all_gather(shared_vectors.astype(jnp.bfloat16), "dp", axis=1, tiled=True),
        lax.all_gather(split_vectors.astype(jnp.bfloat16), "dp", axis=1, tiled=True),
    )
    joint_work, output_work, widen_work, narrow_work, shared_work, split_work = gathered
    shared_float = shared_work.astype(jnp.float32)
    split_float = split_work.astype(jnp.float32)[0]
    head_size = D // HEADS
    head_cols = output_work.shape[0]
    local_heads = head_cols // head_size
    tensor_rank = lax.axis_index("tensor")
    query_bias = split_float[:head_cols].reshape(local_heads, head_size)
    value_bias = split_float[head_cols : 2 * head_cols].reshape(local_heads, head_size)
    widen_bias = split_float[2 * head_cols :]
    total_rows = tokens.shape[0]
    seq_count = lengths.shape[0]
    seq_len = total_rows // seq_count
    block_rows = min(512, seq_len)
    block_count = seq_len // block_rows
    score_scale = 1.0 / math.sqrt(head_size)
    positions = jnp.arange(seq_len, dtype=jnp.int32)
    row_lengths = jnp.repeat(lengths, seq_len, total_repeat_length=total_rows)
    live_rows = (jnp.tile(positions, seq_count) < row_lengths).astype(jnp.float32)[:, None]
    head_ids = tensor_rank * local_heads + jnp.arange(local_heads, dtype=jnp.int32)
    slopes = jnp.exp2(-8.0 * (head_ids + 1).astype(jnp.float32) / HEADS)
    block_limits = [block_count] * seq_count

    def block_scores(block_queries, seq_keys, first_row, seq_length):
        scores = (
            jnp.einsum("qhd,khd->hqk", block_queries, seq_keys, preferred_element_type=jnp.float32)
            * score_scale
        )
        row_ids = first_row + jnp.arange(block_rows, dtype=jnp.int32)
        offset = (positions[None, :] - row_ids[:, None]).astype(jnp.float32)
        scores = scores + slopes[:, None, None] * offset[None]
        allowed = (positions[None, :] <= row_ids[:, None]) & (positions[None, :] < seq_length)
        return jnp.where(allowed[None], scores, MASKED_SCORE)

    inputs = tokens.astype(jnp.float32)
    normed_one, inverse_one = normalize(inputs)
    attn_input = (normed_one * shared_float[0] + shared_float[1]).astype(jnp.bfloat16)
    joint = jnp.dot(attn_input, joint_work, preferred_element_type=jnp.float32).reshape(
        total_rows, local_heads, 3, head_size
    )
    queries = (joint[:, :, 0] + query_bias).astype(jnp.bfloat16)
    keys_all = joint[:, :, 1].astype(jnp.bfloat16)
    values_all = (joint[:, :, 2] + value_bias).astype(jnp.bfloat16)
    heads_out = jnp.zeros((total_rows, local_heads, head_size), jnp.bfloat16)
    lse_rows = jnp.zeros((total_rows, local_heads), jnp.float32)
    seq_index = 0
    base_row = seq_index * seq_len
    seq_queries = queries
    seq_keys = keys_all
    seq_values = values_all
    seq_length = lengths[seq_index]

    def forward_block(block_index, carry):
        out_buffer, lse_buffer = carry
        first_row = block_index * block_rows
        block_queries = lax.dynamic_slice_in_dim(seq_queries, first_row, block_rows, 0)
        scores = block_scores(block_queries, seq_keys, first_row, seq_length)
        highest = jnp.max(scores, axis=-1, keepdims=True)
        weights = jnp.exp(scores - highest)
        totals = jnp.sum(weights, axis=-1, keepdims=True)
        probabilities = (weights / totals).astype(jnp.bfloat16)
        block_out = jnp.einsum(
            "hqk,khd->qhd", probabilities, seq_values, preferred_element_type=jnp.float32
        )
        out_buffer = lax.dynamic_update_slice_in_dim(
            out_buffer, block_out.astype(jnp.bfloat16), base_row + first_row, 0
        )
        lse_buffer = lax.dynamic_update_slice_in_dim(
            lse_buffer, (highest + jnp.log(totals))[:, :, 0].T, base_row + first_row, 0
        )
        return (out_buffer, lse_buffer)

    heads_out, lse_rows = lax.fori_loop(
        0, block_limits[seq_index], forward_block, (heads_out, lse_rows)
    )
    heads_flat = heads_out.reshape(total_rows, head_cols)
    attn_sum = lax.psum(
        jnp.dot(heads_flat, output_work, preferred_element_type=jnp.float32).astype(jnp.bfloat16),
        "tensor",
    ).astype(jnp.float32)
    hidden_one = inputs + attn_sum + shared_float[4]
    normed_two, inverse_two = normalize(hidden_one)
    mlp_input = (normed_two * shared_float[2] + shared_float[3]).astype(jnp.bfloat16)
    widened = jnp.dot(mlp_input, widen_work, preferred_element_type=jnp.float32) + widen_bias
    activated, gelu_pull = jax.vjp(gelu_tanh, widened)
    activated_low = activated.astype(jnp.bfloat16)
    mlp_sum = lax.psum(
        jnp.dot(activated_low, narrow_work, preferred_element_type=jnp.float32).astype(
            jnp.bfloat16
        ),
        "tensor",
    ).astype(jnp.float32)
    result = hidden_one + mlp_sum + shared_float[5]
    layer_output = (result * live_rows).astype(jnp.bfloat16)
    grad_out = cotangent.astype(jnp.float32) * live_rows
    grad_out_low = grad_out.astype(jnp.bfloat16)
    grad_narrow = over_rows(activated_low, grad_out_low)
    grad_widened = gelu_pull(against_rows(grad_out_low, narrow_work))[0].astype(jnp.bfloat16)
    grad_widen = over_rows(mlp_input, grad_widened)
    grad_mlp_in = lax.psum(
        against_rows(grad_widened, widen_work).astype(jnp.bfloat16), "tensor"
    ).astype(jnp.float32)
    grad_hidden = grad_out + normalize_back(grad_mlp_in, normed_two, inverse_two, shared_float[2])
    grad_hidden_low = grad_hidden.astype(jnp.bfloat16)
    grad_output = over_rows(heads_flat, grad_hidden_low)
    grad_heads = (
        against_rows(grad_hidden_low, output_work)
        .astype(jnp.bfloat16)
        .reshape(total_rows, local_heads, head_size)
    )
    grad_queries = jnp.zeros((total_rows, local_heads, head_size), jnp.bfloat16)
    seq_index = 0
    base_row = seq_index * seq_len
    seq_queries = queries
    seq_keys = keys_all
    seq_values = values_all
    seq_lse = lse_rows
    seq_length = lengths[seq_index]

    def backward_block(block_index, carry):
        query_buffer, grad_keys, grad_values = carry
        first_row = block_index * block_rows
        block_queries = lax.dynamic_slice_in_dim(seq_queries, first_row, block_rows, 0)
        block_grad = lax.dynamic_slice_in_dim(grad_heads, first_row, block_rows, 0)
        block_lse = lax.dynamic_slice_in_dim(seq_lse, first_row, block_rows, 0).T
        scores = block_scores(block_queries, seq_keys, first_row, seq_length)
        probabilities = jnp.exp(scores - block_lse[:, :, None])
        grad_probs = jnp.einsum(
            "qhd,khd->hqk", block_grad, seq_values, preferred_element_type=jnp.float32
        )
        row_inner = jnp.sum(probabilities * grad_probs, axis=-1, keepdims=True)
        grad_scores = (probabilities * (grad_probs - row_inner)).astype(jnp.bfloat16)
        block_grad_q = (
            jnp.einsum("hqk,khd->qhd", grad_scores, seq_keys, preferred_element_type=jnp.float32)
            * score_scale
        )
        grad_keys = (
            grad_keys
            + jnp.einsum(
                "hqk,qhd->khd", grad_scores, block_queries, preferred_element_type=jnp.float32
            )
            * score_scale
        )
        grad_values = grad_values + jnp.einsum(
            "hqk,qhd->khd",
            probabilities.astype(jnp.bfloat16),
            block_grad,
            preferred_element_type=jnp.float32,
        )
        query_buffer = lax.dynamic_update_slice_in_dim(
            query_buffer, block_grad_q.astype(jnp.bfloat16), base_row + first_row, 0
        )
        return (query_buffer, grad_keys, grad_values)

    zero_seq = jnp.zeros((seq_len, local_heads, head_size), jnp.float32)
    grad_queries, seq_key_grad, seq_value_grad = lax.fori_loop(
        0, block_limits[seq_index], backward_block, (grad_queries, zero_seq, zero_seq)
    )
    key_parts = seq_key_grad.astype(jnp.bfloat16)
    value_parts = seq_value_grad.astype(jnp.bfloat16)
    grad_joint_act = jnp.stack([grad_queries, key_parts, value_parts], axis=2).reshape(
        total_rows, 3 * head_cols
    )
    grad_query_bias = jnp.sum(grad_queries, axis=0, dtype=jnp.float32).reshape(head_cols)
    grad_value_bias = jnp.sum(value_parts, axis=0, dtype=jnp.float32).reshape(head_cols)
    grad_joint = over_rows(attn_input, grad_joint_act)
    grad_attn_in = lax.psum(
        against_rows(grad_joint_act, joint_work).astype(jnp.bfloat16), "tensor"
    ).astype(jnp.float32)
    input_grad = (
        grad_hidden + normalize_back(grad_attn_in, normed_one, inverse_one, shared_float[0])
    ).astype(jnp.bfloat16)
    grad_shared = jnp.stack(
        [
            jnp.sum(grad_attn_in * normed_one, axis=0),
            jnp.sum(grad_attn_in, axis=0),
            jnp.sum(grad_mlp_in * normed_two, axis=0),
            jnp.sum(grad_mlp_in, axis=0),
            jnp.sum(grad_hidden, axis=0),
            jnp.sum(grad_out, axis=0),
        ]
    )
    grad_split = jnp.concatenate(
        [grad_query_bias, grad_value_bias, jnp.sum(grad_widened, axis=0, dtype=jnp.float32)]
    )[None]
    joint_sum, output_sum, widen_sum, narrow_sum, shared_sum, split_sum = (
        lax.psum_scatter(grad_joint, "dp", scatter_dimension=0, tiled=True),
        lax.psum_scatter(grad_output, "dp", scatter_dimension=1, tiled=True),
        lax.psum_scatter(grad_widen, "dp", scatter_dimension=0, tiled=True),
        lax.psum_scatter(grad_narrow, "dp", scatter_dimension=1, tiled=True),
        lax.psum_scatter(grad_shared, "dp", scatter_dimension=1, tiled=True),
        lax.psum_scatter(grad_split, "dp", scatter_dimension=1, tiled=True),
    )
    local_square = jnp.sum(joint_sum * joint_sum) + jnp.sum(output_sum * output_sum)
    local_square = local_square + jnp.sum(widen_sum * widen_sum) + jnp.sum(narrow_sum * narrow_sum)
    local_square = local_square + jnp.sum(split_sum * split_sum)
    local_square = local_square + jnp.where(
        tensor_rank == 0, jnp.sum(shared_sum * shared_sum), jnp.float32(0.0)
    )
    total_square = lax.psum(local_square, ("dp", "tensor"))
    grad_norm = jnp.sqrt(total_square)
    factor = jnp.minimum(1.0, CLIP_LIMIT / (grad_norm + 1e-06))
    joint_new = adam_step(
        joint_weight, joint_first, joint_second, factor * joint_sum, MATRIX_RATE, MATRIX_DECAY
    )
    output_new = adam_step(
        output_weight, output_first, output_second, factor * output_sum, OUTPUT_RATE, MATRIX_DECAY
    )
    widen_new = adam_step(
        widen_weight, widen_first, widen_second, factor * widen_sum, MATRIX_RATE, MATRIX_DECAY
    )
    narrow_new = adam_step(
        narrow_weight, narrow_first, narrow_second, factor * narrow_sum, MATRIX_RATE, MATRIX_DECAY
    )
    shared_new = adam_step(
        shared_vectors, shared_first, shared_second, factor * shared_sum, VECTOR_RATE, 0.0
    )
    split_new = adam_step(
        split_vectors, split_first, split_second, factor * split_sum, VECTOR_RATE, 0.0
    )
    return (
        layer_output,
        input_grad,
        grad_norm,
        joint_new[0],
        joint_new[1],
        joint_new[2],
        output_new[0],
        output_new[1],
        output_new[2],
        widen_new[0],
        widen_new[1],
        widen_new[2],
        narrow_new[0],
        narrow_new[1],
        narrow_new[2],
        shared_new[0],
        shared_new[1],
        shared_new[2],
        split_new[0],
        split_new[1],
        split_new[2],
    )


def solution(mesh):
    in_specs = (
        P("dp", None),
        P("dp", None),
        P("dp"),
        P("dp", "tensor"),
        P("tensor", "dp"),
        P("dp", "tensor"),
        P("tensor", "dp"),
        P(None, "dp"),
        P("tensor", "dp"),
        P("dp", "tensor"),
        P("dp", "tensor"),
        P("tensor", "dp"),
        P("tensor", "dp"),
        P("dp", "tensor"),
        P("dp", "tensor"),
        P("tensor", "dp"),
        P("tensor", "dp"),
        P(None, "dp"),
        P(None, "dp"),
        P("tensor", "dp"),
        P("tensor", "dp"),
    )
    out_specs = (
        P("dp", None),
        P("dp", None),
        P(),
        P("dp", "tensor"),
        P("dp", "tensor"),
        P("dp", "tensor"),
        P("tensor", "dp"),
        P("tensor", "dp"),
        P("tensor", "dp"),
        P("dp", "tensor"),
        P("dp", "tensor"),
        P("dp", "tensor"),
        P("tensor", "dp"),
        P("tensor", "dp"),
        P("tensor", "dp"),
        P(None, "dp"),
        P(None, "dp"),
        P(None, "dp"),
        P("tensor", "dp"),
        P("tensor", "dp"),
        P("tensor", "dp"),
    )
    return jax.shard_map(
        on_device, mesh=mesh, in_specs=in_specs, out_specs=out_specs, check_vma=False
    )
```

profile of v0, /device:TPU:0, one launch (start us, length us, event | category | flops | bytes accessed | tf_op | source)
XLA Modules:
  0.0 1432.6 jit_solution(12050288936933223811)
XLA Ops:
  12.6 23.1 %all-reduce = bf16[1536]{0:T(1024)(128)(2,1)S(1)} all-reduce(bf16[1536]{0:T(1024)(128)(2,1)S(1)} %dynamic-update-slice.4), channel_id=1, replica_groups=mesh['dp'=8,'tensor'=4] {'dp'}, use_global_device_ids=true, to_apply=%add | all-reduce | flops 1536 | bytes 6144
  37.4 26.3 %all_gather.18 = bf16[6,1024]{1,0:T(8,128)(2,1)S(1)} all-gather(bf16[6,128]{1,0:T(8,128)(2,1)S(1)} %convert_element_type.180), channel_id=1, replica_groups=mesh['dp'=8,'tensor'=4] {'dp'}, dimensions={1}, use_global_device_ids=true | all-gather | bytes 13824 | tf_op jit(solution)/shard_map/all_gather | solution.py:95
  70.1 28.1 %all_gather.21 = bf16[256,1024]{1,0:T(8,128)(2,1)} all-gather(bf16[256,128]{1,0:T(8,128)(2,1)S(1)} %convert_element_type.190), channel_id=1, replica_groups=mesh['dp'=8,'tensor'=4] {'dp'}, dimensions={1}, use_global_device_ids=true | all-gather | bytes 589824 | tf_op jit(solution)/shard_map/all_gather | solution.py:92
  98.2 6.4 fusion.103
  108.4 96.8 %while.38 = (s32[]{:T(128)}, bf16[2048,4,64]{0,2,1:T(8,128)(2,1)S(1)}, f32[2048,4]{0,1:T(4,128)}, s32[]{:T(128)}, bf16[2048,4,64]{0,2,1:T(8,128)(2,1)}, /*index=...) while((s32[]{:T(128)}, ...), condition=%wide.region_5.6_spmd.clone.clone, body=%wide.region_2.5_spmd.clone.clone.sunk | while | flops 1153565184 | bytes 90778360 | solution.py:170
  110.4 7.2 fusion.167
  117.6 5.8 fusion.168
  123.4 8.8 fusion.169
  134.6 7.2 fusion.167
  141.8 5.8 fusion.168
  147.6 8.8 fusion.169
  158.7 7.2 fusion.167
  165.9 5.8 fusion.168
  171.7 8.8 fusion.169
  182.9 7.2 fusion.167
  190.1 5.8 fusion.168
  195.8 8.8 fusion.169
  211.0 81.1 %all-reduce.6.cloned.1.call-done = bf16[2048,1024]{1,0:T(8,128)(2,1)} async-done(((bf16[2048,1024]{1,0:T(8,128)(2,1)}), bf16[2048,1024]{1,0:T(8,128)(2,1)}) %all-reduce.6.cloned.1.call-update) | async-done | bytes 4194320 | tf_op jit(solution)/shard_map/psum | solution.py:174
  292.1 5.0 fusion.79
  304.3 40.2 %all-gather.6.cloned.1.call-done = bf16[1024,1024]{1,0:T(8,128)(2,1)} async-done(((bf16[128,1024]{1,0:T(8,128)(2,1)}), bf16[1024,1024]{1,0:T(8,128)(2,1)}) %all-gather.6.cloned.1.call-update) | async-done | bytes 2097168 | tf_op jit(solution)/shard_map/all_gather | solution.py:93
  344.5 10.6 fusion.115
  355.1 41.7 %all-gather.8.cloned.1.call-done = bf16[1024,1024]{1,0:T(8,128)(2,1)} async-done(((bf16[1024,128]{1,0:T(8,128)(2,1)}), bf16[1024,1024]{1,0:T(8,128)(2,1)}) %all-gather.8.cloned.1.call-update) | async-done | bytes 2097168 | tf_op jit(solution)/shard_map/all_gather | solution.py:94
  396.8 14.4 %convert_reduce_fusion.3 = (f32[1024]{0:T(1024)}, bf16[2048,1024]{1,0:T(8,128)(2,1)S(1)}) fusion(f32[2048,1024]{1,0:T(8,128)} %fusion.115, f32[1024]{0:T(1024)S(1)} %bitcast.142, bf16[1024,1024]{1,0:T(8,128)(2,1)} %all-gather.8.cloned.1.call-done, bf16[2048,1024]{1,0:T(8,128)(2,1)} %param.30, f32[2048]{0:T(1024)S(1)} %fusion.98), kind=kOutput, calls=%fused_computation.100 | convolution fusion | flops 4349492224 | bytes 18890752 | tf_op jit(solution)/shard_map/dot_general | solution.py:47
  413.1 6.3 convolution_convert_fusion.2
  419.5 12.0 convolution_convert_fusion.3
  431.5 71.7 %all-reduce.8.cloned.1.call-done = bf16[2048,1024]{1,0:T(8,128)(2,1)} async-done(((bf16[2048,1024]{1,0:T(8,128)(2,1)}), bf16[2048,1024]{1,0:T(8,128)(2,1)}) %all-reduce.8.cloned.1.call-update) | async-done | bytes 4194320 | tf_op jit(solution)/shard_map/psum | solution.py:197
  503.3 9.4 fusion.75
  512.7 7.9 fusion.111
  525.2 214.5 %while.39 = (s32[]{:T(128)}, bf16[2048,4,64]{0,2,1:T(8,128)(2,1)}, f32[2048,4,64]{0,2,1:T(8,128)S(1)}, f32[2048,4,64]{0,2,1:T(8,128)}, s32[]{:T(128)}, /*index=5...) while((s32[]{:T(128)}, bf16[2048,4,64]{0,2,1:T(8,128)(2,1)}, ...), condition=%wide.region_15.16_spmd.clone.clone, body=%wide.region_13.15_spmd.clone.clone.sunk | while | flops 2737570304 | bytes 216320304 | solution.py:253
  528.0 9.4 fusion.179
  537.4 14.4 %multiply_reduce_fusion.9 = (f32[4,512]{1,0:T(4,128)S(1)}, f32[4,512,2048]{2,1,0:T(8,128)}) fusion(f32[4,512,2048]{2,1,0:T(8,128)} %fusion.179, f32[4,512]{1,0:T(4,128)S(1)} %dynamic-slice_bitcast_fusion.2, f32[512,2048]{1,0:T(8,128)S(1)} %fusion.180, f32[4]{0:T(128)S(1)} %multiply_exponential_fusion.5, ...), kind=kOutput, calls=%fused_computation.27.clone.1 | convolution fusion | flops 566228992 | bytes 40124436 | tf_op jit(solution)/shard_map/while/body/eval_jaxpr/qhd,khd->hqk/dot_general | solution.py:123
  551.9 11.5 multiply_convert_fusion.6
  563.3 3.9 copy-done
  571.1 4.6 fusion.182
  581.0 9.4 fusion.179
  590.4 14.4 %multiply_reduce_fusion.9 = (f32[4,512]{1,0:T(4,128)S(1)}, f32[4,512,2048]{2,1,0:T(8,128)}) fusion(f32[4,512,2048]{2,1,0:T(8,128)} %fusion.179, f32[4,512]{1,0:T(4,128)S(1)} %dynamic-slice_bitcast_fusion.2, f32[512,2048]{1,0:T(8,128)S(1)} %fusion.180, f32[4]{0:T(128)S(1)} %multiply_exponential_fusion.5, ...), kind=kOutput, calls=%fused_computation.27.clone.1 | convolution fusion | flops 566228992 | bytes 40124436 | tf_op jit(solution)/shard_map/while/body/eval_jaxpr/qhd,khd->hqk/dot_general | solution.py:123
  604.8 11.5 multiply_convert_fusion.6
  620.2 4.6 fusion.184
  624.8 4.6 fusion.182
  634.6 9.4 fusion.179
  644.1 14.4 %multiply_reduce_fusion.9 = (f32[4,512]{1,0:T(4,128)S(1)}, f32[4,512,2048]{2,1,0:T(8,128)}) fusion(f32[4,512,2048]{2,1,0:T(8,128)} %fusion.179, f32[4,512]{1,0:T(4,128)S(1)} %dynamic-slice_bitcast_fusion.2, f32[512,2048]{1,0:T(8,128)S(1)} %fusion.180, f32[4]{0:T(128)S(1)} %multiply_exponential_fusion.5, ...), kind=kOutput, calls=%fused_computation.27.clone.1 | convolution fusion | flops 566228992 | bytes 40124436 | tf_op jit(solution)/shard_map/while/body/eval_jaxpr/qhd,khd->hqk/dot_general | solution.py:123
  658.5 11.5 multiply_convert_fusion.6
  673.9 4.6 fusion.184
  678.5 4.6 fusion.182
  688.3 9.4 fusion.179
  697.7 14.4 %multiply_reduce_fusion.9 = (f32[4,512]{1,0:T(4,128)S(1)}, f32[4,512,2048]{2,1,0:T(8,128)}) fusion(f32[4,512,2048]{2,1,0:T(8,128)} %fusion.179, f32[4,512]{1,0:T(4,128)S(1)} %dynamic-slice_bitcast_fusion.2, f32[512,2048]{1,0:T(8,128)S(1)} %fusion.180, f32[4]{0:T(128)S(1)} %multiply_exponential_fusion.5, ...), kind=kOutput, calls=%fused_computation.27.clone.1 | convolution fusion | flops 566228992 | bytes 40124436 | tf_op jit(solution)/shard_map/while/body/eval_jaxpr/qhd,khd->hqk/dot_general | solution.py:123
  712.1 11.5 multiply_convert_fusion.6
  727.5 4.6 fusion.184
  732.1 4.6 fusion.182
  745.1 5.1 convolution_convert_fusion.1
  753.1 6.1 fusion.84
  759.3 144.5 %all-reduce.10.cloned.1.call-done = (bf16[2048,1024]{1,0:T(8,128)(2,1)}, bf16[2048,1024]{1,0:T(8,128)(2,1)}) async-done(((bf16[2048,1024]{1,0:T(8,128)(2,1)}, bf16[2048,1024]{1,0:T(8,128)(2,1)}), (bf16[2048,1024]{1,0:T(8,128)(2,1)}, bf16[2048,1024]{1,0:T(8,128)(2,1)})) %all-reduce.10.cloned.1.call-update) | async-done | bytes 8388624 | tf_op jit(solution)/shard_map/psum | solution.py:184
  903.8 6.1 fusion.76
  910.7 8.2 fusion.101
  919.0 10.1 fusion.116
  929.4 13.3 fusion.87
  942.7 27.0 %reduce-scatter.19.cloned.1.call-done = f32[192,1]{1,0:T(8,128)} async-done(((f32[1536,1]{1,0:T(8,128)}), f32[192,1]{1,0:T(8,128)}) %reduce-scatter.19.cloned.1.call-update) | async-done | bytes 784
  971.3 65.1 %reduce-scatter.11.cloned.1.call-done = f32[256,128]{1,0:T(8,128)} async-done(((f32[256,1024]{1,0:T(8,128)}), f32[256,128]{1,0:T(8,128)}) %reduce-scatter.11.cloned.1.call-update) | async-done | bytes 131088 | tf_op jit(solution)/shard_map/reduce_scatter | solution.py:285
  1039.1 53.5 %reduce-scatter.17.cloned.1.call-done = f32[6,128]{1,0:T(8,128)} async-done(((f32[6,1024]{1,0:T(8,128)}), f32[6,128]{1,0:T(8,128)}) %reduce-scatter.17.cloned.1.call-update) | async-done | bytes 3088 | tf_op jit(solution)/shard_map/reduce_scatter | solution.py:288
  1094.6 75.0 %reduce-scatter.9.cloned.1.call-done = f32[128,768]{1,0:T(8,128)} async-done(((f32[1024,768]{1,0:T(8,128)}), f32[128,768]{1,0:T(8,128)}) %reduce-scatter.9.cloned.1.call-update) | async-done | bytes 393232 | tf_op jit(solution)/shard_map/reduce_scatter | solution.py:284
  1172.5 88.2 %reduce-scatter.13.cloned.1.call-done = f32[128,1024]{1,0:T(8,128)} async-done(((f32[1024,1024]{1,0:T(8,128)}), f32[128,1024]{1,0:T(8,128)}) %reduce-scatter.13.cloned.1.call-update) | async-done | bytes 524304 | tf_op jit(solution)/shard_map/reduce_scatter | solution.py:286
  1263.2 90.3 %reduce-scatter.15.cloned.1.call-done = f32[1024,128]{1,0:T(8,128)} async-done(((f32[1024,1024]{1,0:T(8,128)}), f32[1024,128]{1,0:T(8,128)}) %reduce-scatter.15.cloned.1.call-update) | async-done | bytes 524304 | tf_op jit(solution)/shard_map/reduce_scatter | solution.py:287
  1356.7 14.8 %fusion.60 = (bf16[2048,1024]{1,0:T(8,128)(2,1)}, bf16[2048,1024]{1,0:T(8,128)(2,1)}) fusion(f32[2048,1024]{1,0:T(8,128)} %copy-done.4, bf16[2048,1024]{1,0:T(8,128)(2,1)} %param.29, bf16[2048,1024]{1,0:T(8,128)(2,1)} %get-tuple-element.580, f32[2048]{0:T(1024)} %broadcast_multiply_fusion, f32[2048]{0:T(1024)} %broadcast_multiply_fusion.1, ...), kind=kLoop, calls=%fused_computation.83 | loop fusion | flops 39845888 | bytes 33607680 | tf_op jit(solution)/shard_map/convert_element_type | solution.py:269
  1371.5 40.3 %psum.39 = f32[]{:T(128)} all-reduce(f32[]{:T(128)S(6)} %add.435), channel_id=1, replica_groups=mesh['dp'=8,'tensor'=4] {'dp','tensor'}, use_global_device_ids=true, to_apply=%region_40.41 | all-reduce | flops 1 | bytes 8 | tf_op jit(solution)/shard_map/psum | solution.py:297
  (255 shorter events, 113.1 us)
Async XLA Ops:
  7.2 91.0 %all-gather.4.cloned.1.call-start = ((), (), s32[]{:S(2)}) async-start(), calls=%async_computation.6 | async-start | bytes 1769472 | tf_op jit(solution)/shard_map/all_gather | solution.py:91
  9.0 283.1 %all-reduce.6.cloned.1.call-start = ((), (), s32[]{:S(2)}) async-start(), calls=%async_computation.7 | async-start | bytes 8388608 | tf_op jit(solution)/shard_map/psum | solution.py:174
  66.5 38.2 %copy-start.28 = (f32[2048]{0:T(1024)}, f32[2048]{0:T(1024)S(1)}, u32[]{:S(2)}) copy-start(f32[2048]{0:T(1024)S(1)} %broadcast_multiply_fusion.5) | copy-start | bytes 24580
  69.5 35.2 %copy-start.32 = (f32[2048]{0:T(1024)}, f32[2048]{0:T(1024)S(1)}, u32[]{:S(2)}) copy-start(f32[2048]{0:T(1024)S(1)} %add_rsqrt_fusion.1) | copy-start | bytes 24580
  70.1 34.6 %copy-start.35 = (f32[1,1024]{1,0:T(1,128)}, f32[1,1024]{1,0:T(1,128)S(1)}, u32[]{:S(2)}) copy-start(f32[1,1024]{1,0:T(1,128)S(1)} %get-tuple-element.613) | copy-start | bytes 12292
  70.1 34.6 %copy-start.45 = (f32[1,1024]{1,0:T(1,128)}, f32[1,1024]{1,0:T(1,128)S(1)}, u32[]{:S(2)}) copy-start(f32[1,1024]{1,0:T(1,128)S(1)} %get-tuple-element.614) | copy-start | bytes 12292
  108.4 96.8 %copy-start.11 = (bf16[256,1024]{1,0:T(8,128)(2,1)S(1)}, bf16[256,1024]{1,0:T(8,128)(2,1)}, u32[]{:S(2)}) copy-start(bf16[256,1024]{1,0:T(8,128)(2,1)} %all_gather.21) | copy-start | bytes 1572868
  110.4 7.2 copy-start.1
  134.6 7.2 copy-start.1
  158.7 7.2 copy-start.1
  182.9 7.2 copy-start.1
  205.2 91.9 %copy-start.8 = (bf16[2048,4,64]{0,2,1:T(8,128)(2,1)}, bf16[2048,4,64]{0,2,1:T(8,128)(2,1)S(1)}, u32[]{:S(2)}) copy-start(bf16[2048,4,64]{0,2,1:T(8,128)(2,1)S(1)} %get-tuple-element.413) | copy-start | bytes 3145732
  205.2 4.2 copy-start.15
  205.2 5.7 copy-start.38
  205.2 86.9 %copy-start.26 = (f32[1,1024]{1,0:T(1,128)S(1)}, f32[1,1024]{1,0:T(1,128)}, u32[]{:S(2)}) copy-start(f32[1,1024]{1,0:T(1,128)} %get-tuple-element.615) | copy-start | bytes 12292
  208.6 135.9 %all-gather.6.cloned.1.call-start = ((), (), s32[]{:S(2)}) async-start(), calls=%async_computation.8 | async-start | bytes 2359296 | tf_op jit(solution)/shard_map/all_gather | solution.py:93
  209.4 187.3 %all-gather.8.cloned.1.call-start = ((), (), s32[]{:S(2)}) async-start(), calls=%async_computation.9 | async-start | bytes 2359296 | tf_op jit(solution)/shard_map/all_gather | solution.py:94
  210.2 293.0 %all-reduce.8.cloned.1.call-start = ((), (), s32[]{:S(2)}) async-start(), calls=%async_computation.10 | async-start | bytes 8388608 | tf_op jit(solution)/shard_map/psum | solution.py:197
  211.0 208.5 %copy-start.48 = (f32[1,1024]{1,0:T(1,128)}, f32[1,1024]{1,0:T(1,128)S(1)}, u32[]{:S(2)}) copy-start(f32[1,1024]{1,0:T(1,128)S(1)} %slice.85) | copy-start | bytes 12292
  211.0 301.6 %copy-start.30 = (f32[2048]{0:T(1024)}, f32[2048]{0:T(1024)S(1)}, u32[]{:S(2)}) copy-start(f32[2048]{0:T(1024)S(1)} %fusion.98) | copy-start | bytes 24580
  292.1 5.1 copy-start.2
  292.1 5.9 copy-start.5
  292.1 8.4 copy-start.34
  292.1 8.4 copy-start.39
  396.8 16.4 %copy-start.50 = (bf16[1024,1024]{1,0:T(8,128)(2,1)S(1)}, bf16[1024,1024]{1,0:T(8,128)(2,1)}, u32[]{:S(2)}) copy-start(bf16[1024,1024]{1,0:T(8,128)(2,1)} %all-gather.6.cloned.1.call-done) | copy-start | bytes 6291460
  419.4 484.3 %all-reduce.10.cloned.1.call-start = ((), (), s32[]{:S(2)}) async-start(), calls=%async_computation.17 | async-start | bytes 16777216 | tf_op jit(solution)/shard_map/psum | solution.py:184
  503.3 9.4 copy-start.3
  503.3 9.4 copy-start.6
  503.3 9.4 copy-start.7
  512.6 7.9 copy-start.12
  520.5 3.5 copy-start.4
  551.9 15.4 %copy-start = (f32[4,512,2048]{2,1,0:T(8,128)S(1)}, f32[4,512,2048]{2,1,0:T(8,128)}, u32[]{:S(2)}) copy-start(f32[4,512,2048]{2,1,0:T(8,128)} %get-tuple-element.744) | copy-start | bytes 50331652 | tf_op jit(solution)/shard_map/while
  604.8 15.4 %copy-start = (f32[4,512,2048]{2,1,0:T(8,128)S(1)}, f32[4,512,2048]{2,1,0:T(8,128)}, u32[]{:S(2)}) copy-start(f32[4,512,2048]{2,1,0:T(8,128)} %get-tuple-element.744) | copy-start | bytes 50331652 | tf_op jit(solution)/shard_map/while
  658.5 15.4 %copy-start = (f32[4,512,2048]{2,1,0:T(8,128)S(1)}, f32[4,512,2048]{2,1,0:T(8,128)}, u32[]{:S(2)}) copy-start(f32[4,512,2048]{2,1,0:T(8,128)} %get-tuple-element.744) | copy-start | bytes 50331652 | tf_op jit(solution)/shard_map/while
  712.1 15.4 %copy-start = (f32[4,512,2048]{2,1,0:T(8,128)S(1)}, f32[4,512,2048]{2,1,0:T(8,128)}, u32[]{:S(2)}) copy-start(f32[4,512,2048]{2,1,0:T(8,128)} %get-tuple-element.744) | copy-start | bytes 50331652 | tf_op jit(solution)/shard_map/while
  739.7 5.4 copy-start.51
  750.2 153.5 %copy-start.29 = (f32[2048]{0:T(1024)S(1)}, f32[2048]{0:T(1024)}, u32[]{:S(2)}) copy-start(f32[2048]{0:T(1024)} %copy-done.28) | copy-start | bytes 24580
  750.2 153.5 %copy-start.33 = (f32[2048]{0:T(1024)S(1)}, f32[2048]{0:T(1024)}, u32[]{:S(2)}) copy-start(f32[2048]{0:T(1024)} %copy-done.32) | copy-start | bytes 24580
  750.3 153.5 %copy-start.36 = (f32[1,1024]{1,0:T(1,128)S(1)}, f32[1,1024]{1,0:T(1,128)}, u32[]{:S(2)}) copy-start(f32[1,1024]{1,0:T(1,128)} %copy-done.35) | copy-start | bytes 12292
  750.3 219.4 %reduce-scatter.19.cloned.1.call-start = ((), (), s32[]{:S(2)}) async-start(), calls=%async_computation.16 | async-start | bytes 884736
  752.9 156.9 %copy-start.40 = (f32[1024]{0:T(1024)S(1)}, f32[1024]{0:T(1024)}, u32[]{:S(2)}) copy-start(f32[1024]{0:T(1024)} %get-tuple-element.531) | copy-start | bytes 12292
  753.0 156.9 %copy-start.41 = (f32[1024]{0:T(1024)S(1)}, f32[1024]{0:T(1024)}, u32[]{:S(2)}) copy-start(f32[1024]{0:T(1024)} %get-tuple-element.537) | copy-start | bytes 12292
  753.0 156.9 %copy-start.42 = (f32[1024]{0:T(1024)S(1)}, f32[1024]{0:T(1024)}, u32[]{:S(2)}) copy-start(f32[1024]{0:T(1024)} %get-tuple-element.599) | copy-start | bytes 12292
  753.0 156.9 %copy-start.43 = (f32[1024]{0:T(1024)S(1)}, f32[1024]{0:T(1024)}, u32[]{:S(2)}) copy-start(f32[1024]{0:T(1024)} %get-tuple-element.607) | copy-start | bytes 12292
  753.0 157.7 %copy-start.46 = (f32[1,1024]{1,0:T(1,128)S(1)}, f32[1,1024]{1,0:T(1,128)}, u32[]{:S(2)}) copy-start(f32[1,1024]{1,0:T(1,128)} %copy-done.45) | copy-start | bytes 12292
  753.0 283.4 %reduce-scatter.11.cloned.1.call-start = ((), (), s32[]{:S(2)}) async-start(), calls=%async_computation.12 | async-start | bytes 1179648 | tf_op jit(solution)/shard_map/reduce_scatter | solution.py:285
  759.2 151.4 %copy-start.14 = (bf16[2048,4,3,64]{0,3,2,1:T(8,128)(2,1)S(1)}, bf16[2048,4,3,64]{0,3,2,1:T(8,128)(2,1)}, u32[]{:S(2)}) copy-start(bf16[2048,4,3,64]{0,3,2,1:T(8,128)(2,1)} %copy-done.13) | copy-start | bytes 9437188
  759.2 333.4 %reduce-scatter.17.cloned.1.call-start = ((), (), s32[]{:S(2)}) async-start(), calls=%async_computation.15 | async-start | bytes 36864 | tf_op jit(solution)/shard_map/reduce_scatter | solution.py:288
  910.6 259.0 %reduce-scatter.9.cloned.1.call-start = ((), (), s32[]{:S(2)}) async-start(), calls=%async_computation.11 | async-start | bytes 3538944 | tf_op jit(solution)/shard_map/reduce_scatter | solution.py:284
  918.9 10.4 copy-start.31
  918.9 10.4 copy-start.49
  918.9 341.9 %reduce-scatter.13.cloned.1.call-start = ((), (), s32[]{:S(2)}) async-start(), calls=%async_computation.13 | async-start | bytes 4718592 | tf_op jit(solution)/shard_map/reduce_scatter | solution.py:286
  929.1 427.6 %copy-start.27 = (f32[1,1024]{1,0:T(1,128)S(1)}, f32[1,1024]{1,0:T(1,128)}, u32[]{:S(2)}) copy-start(f32[1,1024]{1,0:T(1,128)} %get-tuple-element.615) | copy-start | bytes 12292
  929.1 424.5 %reduce-scatter.15.cloned.1.call-start = ((), (), s32[]{:S(2)}) async-start(), calls=%async_computation.14 | async-start | bytes 4718592 | tf_op jit(solution)/shard_map/reduce_scatter | solution.py:287
  970.7 385.9 %copy-start.44 = (f32[1,192]{1,0:T(1,128)}, f32[1,192]{1,0:T(1,128)S(1)}, u32[]{:S(2)}) copy-start(f32[1,192]{1,0:T(1,128)S(1)} %copy.52) | copy-start | bytes 2308
  1356.6 58.6 %copy-start.23 = (f32[256,128]{1,0:T(8,128)S(1)}, f32[256,128]{1,0:T(8,128)}, u32[]{:S(2)}) copy-start(f32[256,128]{1,0:T(8,128)} %param.33) | copy-start | bytes 393220
  1356.6 58.5 %copy-start.24 = (f32[256,128]{1,0:T(8,128)S(1)}, f32[256,128]{1,0:T(8,128)}, u32[]{:S(2)}) copy-start(f32[256,128]{1,0:T(8,128)} %reduce-scatter.11.cloned.1.call-done) | copy-start | bytes 393220
  1356.7 60.3 %copy-start.21 = (f32[128,768]{1,0:T(8,128)S(1)}, f32[128,768]{1,0:T(8,128)}, u32[]{:S(2)}) copy-start(f32[128,768]{1,0:T(8,128)} %param.32) | copy-start | bytes 1179652
  1356.7 60.3 %copy-start.22 = (f32[128,768]{1,0:T(8,128)S(1)}, f32[128,768]{1,0:T(8,128)}, u32[]{:S(2)}) copy-start(f32[128,768]{1,0:T(8,128)} %reduce-scatter.9.cloned.1.call-done) | copy-start | bytes 1179652
  1356.7 60.3 %copy-start.25 = (f32[128,768]{1,0:T(8,128)S(1)}, f32[128,768]{1,0:T(8,128)}, u32[]{:S(2)}) copy-start(f32[128,768]{1,0:T(8,128)} %param.38) | copy-start | bytes 1179652
  1356.7 62.5 %copy-start.16 = (f32[1024,128]{1,0:T(8,128)S(1)}, f32[1024,128]{1,0:T(8,128)}, u32[]{:S(2)}) copy-start(f32[1024,128]{1,0:T(8,128)} %param.35) | copy-start | bytes 1572868
  1356.7 62.5 %copy-start.20 = (f32[1024,128]{1,0:T(8,128)S(1)}, f32[1024,128]{1,0:T(8,128)}, u32[]{:S(2)}) copy-start(f32[1024,128]{1,0:T(8,128)} %reduce-scatter.15.cloned.1.call-done) | copy-start | bytes 1572868
  1356.7 65.0 %copy-start.18 = (f32[128,1024]{1,0:T(8,128)S(1)}, f32[128,1024]{1,0:T(8,128)}, u32[]{:S(2)}) copy-start(f32[128,1024]{1,0:T(8,128)} %param.34) | copy-start | bytes 1572868
  1356.7 65.0 %copy-start.19 = (f32[128,1024]{1,0:T(8,128)S(1)}, f32[128,1024]{1,0:T(8,128)}, u32[]{:S(2)}) copy-start(f32[128,1024]{1,0:T(8,128)} %reduce-scatter.13.cloned.1.call-done) | copy-start | bytes 1572868
  (7 other events, 13.3 us)
Sparse Core Ops, SparseCore 0:
  10.8 47.0 all-gather.3
  208.7 83.3 all-reduce.5
  295.0 49.4 all-gather.5
  347.2 49.5 all-gather.7
  419.5 83.6 all-reduce.7
  750.3 153.3 all-reduce.9
  907.1 62.6 reduce-scatter.18
  973.5 62.8 reduce-scatter.10
  1040.1 52.4 reduce-scatter.16
  1096.1 73.4 reduce-scatter.8
  1173.8 86.9 reduce-scatter.12
  1265.3 88.2 reduce-scatter.14
where the time goes:
time: 1440 us; the launch traced here: 1430 us
  waiting for transfers between devices  779 us (54%)
  matrix products  305 us (21%)
  other arithmetic  173 us (12%)
  blocking collectives  118 us (8%)
  local copies, waits for them, and re-layouts  33.9 us (2%)
  between operations  22.2 us (2%)
    psum x1, waiting for transfers between devices, on_device(): lax.psum(jnp.dot(activated_low, narrow_work, preferred_element_type=jnp.f...  144 us
    reduce_scatter x1, waiting for transfers between devices, on_device(): lax.psum_scatter(grad_narrow, 'dp', scatter_dimension=1, tiled=True)  90.3 us
    reduce_scatter x1, waiting for transfers between devices, on_device(): lax.psum_scatter(grad_widen, 'dp', scatter_dimension=0, tiled=True)  88.2 us
    dot_general x8, matrix products, block_scores(): jnp.einsum('qhd,khd->hqk', block_queries, seq_keys, preferred_element_typ...  86.3 us
    psum x1, waiting for transfers between devices, on_device(): lax.psum(jnp.dot(heads_flat, output_work, preferred_element_type=jnp.floa...  81.1 us
    reduce_scatter x1, waiting for transfers between devices, on_device(): lax.psum_scatter(grad_joint, 'dp', scatter_dimension=0, tiled=True)  75 us
    psum x1, waiting for transfers between devices, on_device(): lax.psum(against_rows(grad_widened, widen_work).astype(jnp.bfloat16), 'te...  71.7 us
    reduce_scatter x1, waiting for transfers between devices, on_device(): lax.psum_scatter(grad_output, 'dp', scatter_dimension=1, tiled=True)  65.1 us
  transfers between devices with their start and end apart: 12, of which 11 were waited for; matrix products, arithmetic and copies ran while one was open for 7% of the time, Pallas kernels for 0%

commit v1 on v0

v1 whole, which is shorter than its diff:
```python
import functools
import math

import jax
import jax.numpy as jnp
from jax import lax
from jax.experimental import pallas as pl
from jax.experimental.pallas import tpu as pltpu
from jax.sharding import PartitionSpec as P

F32, BF = jnp.float32, jnp.bfloat16

D = 1024
HEADS = 16
STEP = 10


NORM_EPSILON = 1e-05
CLIP_LIMIT = 1.0
BETA_FIRST = 0.9
BETA_SECOND = 0.95
ADAM_EPSILON = 1e-08
MATRIX_RATE = 0.05
OUTPUT_RATE = 0.2
VECTOR_RATE = 0.6
MATRIX_DECAY = 0.1


def by_kind(values):
    rows, cols = values.shape
    size = D // HEADS
    return jnp.swapaxes(values.reshape(rows, cols // (3 * size), 3, size), 1, 2).reshape(rows, cols)


def by_head(values):
    rows, cols = values.shape
    size = D // HEADS
    return jnp.swapaxes(values.reshape(rows, 3, cols // (3 * size), size), 1, 2).reshape(rows, cols)


NN = (((1,), (0,)), ((), ()))
NT = (((1,), (1,)), ((), ()))
TN = (((0,), (0,)), ((), ()))
LOW = -1e30


def dot(left, right, dims=NN):
    return lax.dot_general(left, right, dims, preferred_element_type=F32)


def three(values):
    high = values.astype(BF).astype(F32)
    rest = values - high
    middle = rest.astype(BF).astype(F32)
    return high, middle, rest - middle


def stack_rows(shape, rows):
    ids = lax.broadcasted_iota(jnp.int32, shape, 0)
    out = jnp.zeros(shape, F32)
    for at, row in enumerate(rows):
        out = jnp.where(ids == at, row, out)
    return out.astype(BF)


def head_tile(ref, rows, col, head, d):
    lane = col + (head // 2) * 128
    tile = ref[rows, lane:lane + 128].astype(F32)
    if head % 2:
        tile = pltpu.roll(tile, 64, 1)
    return tile


def fill_keys(qkv_ref, ka_ref, heads, d, slope_of, first, count):
    rows = pl.ds(first, count)
    lanes = lax.broadcasted_iota(jnp.int32, (count, 128), 1)
    position = (lax.broadcasted_iota(jnp.int32, (count, 128), 0) + first).astype(F32)
    for head in range(heads):
        high, middle, low = three(position * slope_of(head))
        tile = head_tile(qkv_ref, rows, heads * d, head, d)
        for at, part in enumerate((high, middle, low, 1.0, 1.0, 1.0)):
            tile = jnp.where(lanes == d + at, part, tile)
        ka_ref[head, rows, :] = jnp.where(lanes < d + 6, tile, 0.0).astype(BF)


def causal(scores, bk, bq):
    kid = lax.broadcasted_iota(jnp.int32, (bk, bq), 0)
    qid = lax.broadcasted_iota(jnp.int32, (bk, bq), 1)
    return jnp.where(kid <= qid, scores, LOW)


def slope_fn(heads, total_heads):
    rank = lax.axis_index("tensor")
    def slope_of(head):
        index = jnp.full((1, 128), rank * heads + head + 1, jnp.int32).astype(F32)
        return jnp.exp2(index * (-8.0 / total_heads))
    return slope_of


def attend_kernel(heads, d, total_heads, bq, qkv_ref, wo_ref, part_ref, ot_ref, lse_ref, ka_ref, vt_ref):
    i = pl.program_id(0)
    blocks = pl.num_programs(0)
    width = heads * d

    rows_i = pl.ds(pl.multiple_of(i * bq, bq), bq)
    fill_keys(qkv_ref, ka_ref, heads, d, slope_fn(heads, total_heads), pl.multiple_of(i * bq, bq), bq)
    vt_ref[i] = qkv_ref[rows_i, 2 * width:3 * width].T
    qt = qkv_ref[rows_i, 0:width].T
    ones = stack_rows((128 - d, bq), (1.0, 1.0, 1.0))
    queries = [jnp.concatenate([qt[h * d:(h + 1) * d], ones], axis=0) for h in range(heads)]

    def block(j, carry, last):
        out = []
        kr = pl.ds(pl.multiple_of(j * bq, bq), bq)
        for h in range(heads):
            m, l, acc = carry[h]
            s = dot(ka_ref[h, kr, :], queries[h])
            if last:
                s = causal(s, bq, bq)
            top = jnp.maximum(m, jnp.max(s, axis=0, keepdims=True))
            p = jnp.exp(s - top)
            scale = jnp.exp(m - top)
            l = l * scale + jnp.sum(p, axis=0, keepdims=True)
            acc = acc * scale + dot(vt_ref[j, h * d:(h + 1) * d, :], p.astype(BF))
            out.append((top, l, acc))
        return tuple(out)

    start = (jnp.full((1, bq), LOW, F32), jnp.zeros((1, bq), F32), jnp.zeros((d, bq), F32))
    carry = lax.fori_loop(0, i, lambda j, c: block(j, c, False), (start,) * heads)
    carry = block(i, carry, True)
    for h in range(heads):
        m, l, acc = carry[h]
        ot_ref[h * d:(h + 1) * d, :] = acc / l
        lse_ref[0, h:h + 1, :] = m + jnp.log(l)
    part_ref[...] = dot(ot_ref[...].astype(BF), wo_ref[...], TN).astype(BF)


def attend(qkv, wo, heads, d, total_heads, bq=512):
    n, width = qkv.shape[0], heads * d
    bq = min(bq, n)
    nb = n // bq
    feats = wo.shape[1]
    return pl.pallas_call(
        functools.partial(attend_kernel, heads, d, total_heads, bq),
        grid=(nb,),
        in_specs=[pl.BlockSpec(qkv.shape, lambda i: (0, 0)), pl.BlockSpec(wo.shape, lambda i: (0, 0))],
        out_specs=[pl.BlockSpec((bq, feats), lambda i: (i, 0)), pl.BlockSpec((width, bq), lambda i: (0, i)),
                   pl.BlockSpec((1, heads, bq), lambda i: (i, 0, 0))],
        out_shape=[jax.ShapeDtypeStruct((n, feats), BF), jax.ShapeDtypeStruct((width, n), F32),
                   jax.ShapeDtypeStruct((nb, heads, bq), F32)],
        scratch_shapes=[pltpu.VMEM((heads, n, 128), BF), pltpu.VMEM((nb, width, bq), BF)],
        compiler_params=pltpu.CompilerParams(vmem_limit_bytes=48 * 2**20),
        name="attend",
    )(qkv, wo)


def attend_back_kernel(heads, d, total_heads, bq, qkv_ref, wo_ref, gh_ref, ot_ref, lse_ref, out_ref,
                       ka_ref, kt_ref, va_ref, dk_ref, dv_ref):
    g = pl.program_id(0)
    nb = pl.num_programs(0)
    i = nb - 1 - g
    width = heads * d

    @pl.when(g == 0)
    def _():
        dk_ref[...] = jnp.zeros_like(dk_ref)
        dv_ref[...] = jnp.zeros_like(dv_ref)
        lanes = lax.broadcasted_iota(jnp.int32, (bq, 128), 1)
        def fill(b, c):
            first = pl.multiple_of(b * bq, bq)
            fill_keys(qkv_ref, ka_ref, heads, d, slope_fn(heads, total_heads), first, bq)
            rows = pl.ds(first, bq)
            kt_ref[b] = (qkv_ref[rows, width:2 * width].astype(F32) * (1.0 / d ** 0.5)).astype(BF).T
            for h in range(heads):
                tile = head_tile(qkv_ref, rows, 2 * width, h, d)
                va_ref[h, rows, :] = jnp.where(lanes < d, tile, jnp.where(lanes < d + 3, 1.0, 0.0)).astype(BF)
            return c
        lax.fori_loop(0, nb, fill, 0)

    rows_i = pl.ds(pl.multiple_of(i * bq, bq), bq)
    grad_o = dot(gh_ref[...], wo_ref[...], NT).astype(BF)
    grad_t = grad_o.T
    q_nat = qkv_ref[rows_i, 0:width]
    qt = q_nat.T
    lanes = lax.broadcasted_iota(jnp.int32, (bq, 128), 1)
    queries, grads, q_pair, g_pair = [], [], [], []
    for h in range(heads):
        hs = slice(h * d, (h + 1) * d)
        delta = jnp.sum(grad_t[hs].astype(F32) * ot_ref[hs, :], axis=0, keepdims=True)
        queries.append(jnp.concatenate(
            [qt[hs], stack_rows((128 - d, bq), (1.0, 1.0, 1.0) + three(-lse_ref[0, h:h + 1, :]))], axis=0))
        grads.append(jnp.concatenate([grad_t[hs], stack_rows((128 - d, bq), three(-delta))], axis=0))
        pair = slice((h // 2) * 128, (h // 2) * 128 + 128)
        own = (lanes < d) if h % 2 == 0 else (lanes >= d)
        q_pair.append(jnp.where(own, q_nat[:, pair].astype(F32), 0.0).astype(BF))
        g_pair.append(jnp.where(own, grad_o[:, pair].astype(F32), 0.0).astype(BF))

    def block(j, carry, last):
        out = []
        kr = pl.ds(pl.multiple_of(j * bq, bq), bq)
        for h in range(heads):
            s = dot(ka_ref[h, kr, :], queries[h])
            if last:
                s = causal(s, bq, bq)
            p = jnp.exp(s)
            gs = (p * dot(va_ref[h, kr, :], grads[h])).astype(BF)
            pair = slice((h // 2) * 128, (h // 2) * 128 + 128)
            dv_ref[kr, pair] += dot(p.astype(BF), g_pair[h])
            dk_ref[kr, pair] += dot(gs, q_pair[h])
            out.append(carry[h] + dot(kt_ref[j, h * d:(h + 1) * d, :], gs))
        return tuple(out)

    carry = lax.fori_loop(0, i, lambda j, c: block(j, c, False), (jnp.zeros((d, bq), F32),) * heads)
    carry = block(i, carry, True)
    out_ref[:, 0:width] = jnp.concatenate(carry, axis=0).T.astype(BF)
    out_ref[:, width:2 * width] = dk_ref[rows_i, :].astype(BF)
    out_ref[:, 2 * width:] = dv_ref[rows_i, :].astype(BF)


def attend_back(qkv, wo, gh, ot, lse, heads, d, total_heads, bq=512):
    n, width = qkv.shape[0], heads * d
    bq = min(bq, n)
    nb = n // bq
    feats = wo.shape[1]
    back = lambda i: nb - 1 - i
    return pl.pallas_call(
        functools.partial(attend_back_kernel, heads, d, total_heads, bq),
        grid=(nb,),
        in_specs=[pl.BlockSpec(qkv.shape, lambda i: (0, 0)), pl.BlockSpec(wo.shape, lambda i: (0, 0)),
                  pl.BlockSpec((bq, feats), lambda i: (back(i), 0)), pl.BlockSpec((width, bq), lambda i: (0, back(i))),
                  pl.BlockSpec((1, heads, bq), lambda i: (back(i), 0, 0))],
        out_specs=pl.BlockSpec((bq, 3 * width), lambda i: (back(i), 0)),
        out_shape=jax.ShapeDtypeStruct((n, 3 * width), BF),
        scratch_shapes=[pltpu.VMEM((heads, n, 128), BF), pltpu.VMEM((nb, width, bq), BF),
                        pltpu.VMEM((heads, n, 128), BF), pltpu.VMEM((n, width), F32), pltpu.VMEM((n, width), F32)],
        compiler_params=pltpu.CompilerParams(vmem_limit_bytes=56 * 2**20),
        name="attend_back",
    )(qkv, wo, gh, ot, lse)


def normalize(values):
    centred = values - jnp.mean(values, axis=-1, keepdims=True)
    inverse = lax.rsqrt(jnp.mean(centred * centred, axis=-1, keepdims=True) + NORM_EPSILON)
    return (centred * inverse, inverse)


def normalize_back(incoming, normed, inverse, gain):
    scaled = incoming * gain
    return inverse * (
        scaled
        - jnp.mean(scaled, axis=-1, keepdims=True)
        - normed * jnp.mean(scaled * normed, axis=-1, keepdims=True)
    )


def over_rows(left, right):
    return lax.dot_general(
        left, right, (((0,), (0,)), ((), ())), preferred_element_type=jnp.float32
    )


def against_rows(left, right):
    return lax.dot_general(
        left, right, (((1,), (1,)), ((), ())), preferred_element_type=jnp.float32
    )


def gelu_tanh(values):
    return jax.nn.gelu(values, approximate=True)


def adam_step(master, moment, variance, gradient, rate, decay):
    moment_new = BETA_FIRST * moment + (1.0 - BETA_FIRST) * gradient
    variance_new = BETA_SECOND * variance + (1.0 - BETA_SECOND) * gradient * gradient
    moment_hat = moment_new / (1.0 - BETA_FIRST**STEP)
    variance_hat = variance_new / (1.0 - BETA_SECOND**STEP)
    master_new = master - rate * (
        moment_hat / (jnp.sqrt(variance_hat) + ADAM_EPSILON) + decay * master
    )
    return (master_new, moment_new, variance_new)


def on_device(
    tokens,
    cotangent,
    lengths,
    joint_weight,
    output_weight,
    widen_weight,
    narrow_weight,
    shared_vectors,
    split_vectors,
    joint_first,
    joint_second,
    output_first,
    output_second,
    widen_first,
    widen_second,
    narrow_first,
    narrow_second,
    shared_first,
    shared_second,
    split_first,
    split_second,
):
    gathered = (
        lax.all_gather(by_kind(joint_weight.astype(jnp.bfloat16)), "dp", axis=0, tiled=True),
        lax.all_gather(output_weight.astype(jnp.bfloat16), "dp", axis=1, tiled=True),
        lax.all_gather(widen_weight.astype(jnp.bfloat16), "dp", axis=0, tiled=True),
        lax.all_gather(narrow_weight.astype(jnp.bfloat16), "dp", axis=1, tiled=True),
        lax.all_gather(shared_vectors.astype(jnp.bfloat16), "dp", axis=1, tiled=True),
        lax.all_gather(split_vectors.astype(jnp.bfloat16), "dp", axis=1, tiled=True),
    )
    joint_work, output_work, widen_work, narrow_work, shared_work, split_work = gathered
    shared_float = shared_work.astype(jnp.float32)
    split_float = split_work.astype(jnp.float32)[0]
    head_size = D // HEADS
    head_cols = output_work.shape[0]
    local_heads = head_cols // head_size
    tensor_rank = lax.axis_index("tensor")
    widen_bias = split_float[2 * head_cols :]
    total_rows = tokens.shape[0]
    positions = jnp.arange(total_rows, dtype=jnp.int32)
    live_rows = (positions < lengths[0]).astype(jnp.float32)[:, None]
    scale = 1.0 / math.sqrt(head_size)
    qkv_bias = jnp.concatenate([split_float[:head_cols], jnp.zeros((head_cols,), F32), split_float[head_cols : 2 * head_cols]])
    qkv_scale = jnp.concatenate([jnp.full((head_cols,), scale, F32), jnp.ones((2 * head_cols,), F32)])

    inputs = tokens.astype(jnp.float32)
    normed_one, inverse_one = normalize(inputs)
    attn_input = (normed_one * shared_float[0] + shared_float[1]).astype(jnp.bfloat16)
    joint = jnp.dot(attn_input, joint_work, preferred_element_type=jnp.float32)
    qkv = ((joint + qkv_bias) * qkv_scale).astype(BF)
    attn_part, heads_out, lse = attend(qkv, output_work, local_heads, head_size, HEADS)
    attn_sum = lax.psum(attn_part, "tensor").astype(jnp.float32)
    hidden_one = inputs + attn_sum + shared_float[4]
    normed_two, inverse_two = normalize(hidden_one)
    mlp_input = (normed_two * shared_float[2] + shared_float[3]).astype(jnp.bfloat16)
    widened = jnp.dot(mlp_input, widen_work, preferred_element_type=jnp.float32) + widen_bias
    activated, gelu_pull = jax.vjp(gelu_tanh, widened)
    activated_low = activated.astype(jnp.bfloat16)
    mlp_sum = lax.psum(
        jnp.dot(activated_low, narrow_work, preferred_element_type=jnp.float32).astype(
            jnp.bfloat16
        ),
        "tensor",
    ).astype(jnp.float32)
    result = hidden_one + mlp_sum + shared_float[5]
    layer_output = (result * live_rows).astype(jnp.bfloat16)
    grad_out = cotangent.astype(jnp.float32) * live_rows
    grad_out_low = grad_out.astype(jnp.bfloat16)
    grad_narrow = over_rows(activated_low, grad_out_low)
    grad_widened = gelu_pull(against_rows(grad_out_low, narrow_work))[0].astype(jnp.bfloat16)
    grad_widen = over_rows(mlp_input, grad_widened)
    grad_mlp_in = lax.psum(
        against_rows(grad_widened, widen_work).astype(jnp.bfloat16), "tensor"
    ).astype(jnp.float32)
    grad_hidden = grad_out + normalize_back(grad_mlp_in, normed_two, inverse_two, shared_float[2])
    grad_hidden_low = grad_hidden.astype(jnp.bfloat16)
    grad_output = jnp.dot(heads_out.astype(BF), grad_hidden_low, preferred_element_type=F32)
    grad_joint_act = attend_back(
        qkv, output_work, grad_hidden_low, heads_out, lse, local_heads, head_size, HEADS
    )
    grad_qkv_bias = jnp.sum(grad_joint_act, axis=0, dtype=jnp.float32)
    grad_query_bias = grad_qkv_bias[:head_cols]
    grad_value_bias = grad_qkv_bias[2 * head_cols :]
    grad_joint = over_rows(attn_input, grad_joint_act)
    grad_attn_in = lax.psum(
        against_rows(grad_joint_act, joint_work).astype(jnp.bfloat16), "tensor"
    ).astype(jnp.float32)
    input_grad = (
        grad_hidden + normalize_back(grad_attn_in, normed_one, inverse_one, shared_float[0])
    ).astype(jnp.bfloat16)
    grad_shared = jnp.stack(
        [
            jnp.sum(grad_attn_in * normed_one, axis=0),
            jnp.sum(grad_attn_in, axis=0),
            jnp.sum(grad_mlp_in * normed_two, axis=0),
            jnp.sum(grad_mlp_in, axis=0),
            jnp.sum(grad_hidden, axis=0),
            jnp.sum(grad_out, axis=0),
        ]
    )
    grad_split = jnp.concatenate(
        [grad_query_bias, grad_value_bias, jnp.sum(grad_widened, axis=0, dtype=jnp.float32)]
    )[None]
    joint_sum, output_sum, widen_sum, narrow_sum, shared_sum, split_sum = (
        lax.psum_scatter(grad_joint.astype(BF), "dp", scatter_dimension=0, tiled=True),
        lax.psum_scatter(grad_output.astype(BF), "dp", scatter_dimension=1, tiled=True),
        lax.psum_scatter(grad_widen.astype(BF), "dp", scatter_dimension=0, tiled=True),
        lax.psum_scatter(grad_narrow.astype(BF), "dp", scatter_dimension=1, tiled=True),
        lax.psum_scatter(grad_shared, "dp", scatter_dimension=1, tiled=True),
        lax.psum_scatter(grad_split, "dp", scatter_dimension=1, tiled=True),
    )
    joint_sum, output_sum, widen_sum, narrow_sum = (
        by_head(joint_sum.astype(F32)), output_sum.astype(F32), widen_sum.astype(F32), narrow_sum.astype(F32)
    )
    local_square = jnp.sum(joint_sum * joint_sum) + jnp.sum(output_sum * output_sum)
    local_square = local_square + jnp.sum(widen_sum * widen_sum) + jnp.sum(narrow_sum * narrow_sum)
    local_square = local_square + jnp.sum(split_sum * split_sum)
    local_square = local_square + jnp.where(
        tensor_rank == 0, jnp.sum(shared_sum * shared_sum), jnp.float32(0.0)
    )
    total_square = lax.psum(local_square, ("dp", "tensor"))
    grad_norm = jnp.sqrt(total_square)
    factor = jnp.minimum(1.0, CLIP_LIMIT / (grad_norm + 1e-06))
    joint_new = adam_step(
        joint_weight, joint_first, joint_second, factor * joint_sum, MATRIX_RATE, MATRIX_DECAY
    )
    output_new = adam_step(
        output_weight, output_first, output_second, factor * output_sum, OUTPUT_RATE, MATRIX_DECAY
    )
    widen_new = adam_step(
        widen_weight, widen_first, widen_second, factor * widen_sum, MATRIX_RATE, MATRIX_DECAY
    )
    narrow_new = adam_step(
        narrow_weight, narrow_first, narrow_second, factor * narrow_sum, MATRIX_RATE, MATRIX_DECAY
    )
    shared_new = adam_step(
        shared_vectors, shared_first, shared_second, factor * shared_sum, VECTOR_RATE, 0.0
    )
    split_new = adam_step(
        split_vectors, split_first, split_second, factor * split_sum, VECTOR_RATE, 0.0
    )
    return (
        layer_output,
        input_grad,
        grad_norm,
        joint_new[0],
        joint_new[1],
        joint_new[2],
        output_new[0],
        output_new[1],
        output_new[2],
        widen_new[0],
        widen_new[1],
        widen_new[2],
        narrow_new[0],
        narrow_new[1],
        narrow_new[2],
        shared_new[0],
        shared_new[1],
        shared_new[2],
        split_new[0],
        split_new[1],
        split_new[2],
    )


def solution(mesh):
    in_specs = (
        P("dp", None),
        P("dp", None),
        P("dp"),
        P("dp", "tensor"),
        P("tensor", "dp"),
        P("dp", "tensor"),
        P("tensor", "dp"),
        P(None, "dp"),
        P("tensor", "dp"),
        P("dp", "tensor"),
        P("dp", "tensor"),
        P("tensor", "dp"),
        P("tensor", "dp"),
        P("dp", "tensor"),
        P("dp", "tensor"),
        P("tensor", "dp"),
        P("tensor", "dp"),
        P(None, "dp"),
        P(None, "dp"),
        P("tensor", "dp"),
        P("tensor", "dp"),
    )
    out_specs = (
        P("dp", None),
        P("dp", None),
        P(),
        P("dp", "tensor"),
        P("dp", "tensor"),
        P("dp", "tensor"),
        P("tensor", "dp"),
        P("tensor", "dp"),
        P("tensor", "dp"),
        P("dp", "tensor"),
        P("dp", "tensor"),
        P("dp", "tensor"),
        P("tensor", "dp"),
        P("tensor", "dp"),
        P("tensor", "dp"),
        P(None, "dp"),
        P(None, "dp"),
        P(None, "dp"),
        P("tensor", "dp"),
        P("tensor", "dp"),
        P("tensor", "dp"),
    )
    return jax.shard_map(
        on_device, mesh=mesh, in_specs=in_specs, out_specs=out_specs, check_vma=False
    )
```

time: 1440 us -> 1130 us (0.78)
  matrix products: 305 us -> 86.5 us
  other arithmetic: 173 us -> 81.9 us
  Pallas kernels: 0 us -> 61.3 us
  waiting for transfers between devices: 779 us -> 724 us
    dot_general x30 -> x2, matrix products: 216 us -> 10.4 us  [the longest x1 7 us: on_device(): joint = jnp.dot(attn_input, joint_work, preferred_element_type=jnp.float32)]
    reduce_scatter x4 -> x2, waiting for transfers between devices: 319 us -> 134 us  [the longest x1 68.5 us: on_device(): lax.psum_scatter(grad_widen.astype(BF), 'dp', scatter_dimension=0, tiled=...]
    unnamed x13 -> x15, waiting for transfers between devices: 27.2 us -> 141 us
    pallas_call x0 -> x2, Pallas kernels: none -> 61.3 us  [the longest x1 35.7 us: attend_back(): pl.pallas_call(functools.partial(attend_back_kernel, heads, d, total_head...]
    convert_element_type x14 -> x2, other arithmetic: 50.2 us -> 3.07 us  [the longest x1 3.07 us: on_device(): grad_hidden_low = grad_hidden.astype(jnp.bfloat16)]
    reduce_sum x6 -> x1, other arithmetic: 25.2 us -> 2.4 us  [on_device(): grad_qkv_bias = jnp.sum(grad_joint_act, axis=0, dtype=jnp.float32)]
    while x16 -> x0, local copies, waits for them, and re-layouts: 15.7 us -> none
    dot_general x4 -> x3, matrix products: 37.7 us -> 28.4 us  [over_rows(): lax.dot_general(left, right, (((0,), (0,)), ((), ())), preferred_element_...]
  transfers between devices with their start and end apart: 12 -> 12, of which waited for: 11 -> 11; matrix products, arithmetic and copies ran while one was open for 7% -> 9% of each run, Pallas kernels for 0% -> 0%
where the time goes in v1:
time: 1130 us; the launch traced here: 1120 us
  waiting for transfers between devices  724 us (64%)
  blocking collectives  117 us (10%)
  matrix products  86.5 us (8%)
  other arithmetic  81.9 us (7%)
  Pallas kernels  61.3 us (5%)
  local copies, waits for them, and re-layouts  23.1 us (2%)
  between operations  22 us (2%)
    psum x1, waiting for transfers between devices, on_device(): lax.psum(jnp.dot(activated_low, narrow_work, preferred_element_type=jnp.f...  151 us
    unnamed x15, waiting for transfers between devices  141 us
    psum x1, waiting for transfers between devices, on_device(): lax.psum(against_rows(grad_widened, widen_work).astype(jnp.bfloat16), 'te...  83.8 us
    psum x1, waiting for transfers between devices, on_device(): attn_sum = lax.psum(attn_part, 'tensor').astype(jnp.float32)  78.6 us
    reduce_scatter x1, waiting for transfers between devices, on_device(): lax.psum_scatter(grad_widen.astype(BF), 'dp', scatter_dimension=0, tiled=...  68.5 us
    reduce_scatter x1, waiting for transfers between devices, on_device(): lax.psum_scatter(grad_joint.astype(BF), 'dp', scatter_dimension=0, tiled=...  65.4 us
    reduce_scatter x1, waiting for transfers between devices, on_device(): lax.psum_scatter(grad_shared, 'dp', scatter_dimension=1, tiled=True)  53.8 us
    all_gather x1, waiting for transfers between devices, on_device(): lax.all_gather(narrow_weight.astype(jnp.bfloat16), 'dp', axis=1, tiled=True)  41.7 us
  transfers between devices with their start and end apart: 12, of which 11 were waited for; matrix products, arithmetic and copies ran while one was open for 9% of the time, Pallas kernels for 0%

profile of v1, /device:TPU:0, one launch (start us, length us, event | category | flops | bytes accessed | tf_op | source)
XLA Modules:
  0.0 1117.6 jit_solution(14263395474125043378)
XLA Ops:
  7.2 1.2 copy.54
  10.0 1.2 dynamic-slice
  12.8 23.1 %all-reduce = bf16[1536]{0:T(1024)(128)(2,1)S(1)} all-reduce(bf16[1536]{0:T(1024)(128)(2,1)S(1)} %dynamic-update-slice), channel_id=1, replica_groups=mesh['dp'=8,'tensor'=4] {'dp'}, use_global_device_ids=true, to_apply=%add | all-reduce | flops 1536 | bytes 6144
  36.0 0.9 convert_element_type.126
  36.9 26.2 %all_gather.18 = bf16[6,1024]{1,0:T(8,128)(2,1)S(1)} all-gather(bf16[6,128]{1,0:T(8,128)(2,1)S(1)} %convert_element_type.119), channel_id=1, replica_groups=mesh['dp'=8,'tensor'=4] {'dp'}, dimensions={1}, use_global_device_ids=true | all-gather | bytes 13824 | tf_op jit(solution)/shard_map/all_gather | solution.py:311
  63.1 2.8 convert_reduce_fusion.2
  65.9 3.0 fusion.16
  68.9 28.1 %all_gather.21.wo_ref = bf16[256,1024]{1,0:T(8,128)(2,1)} all-gather(bf16[256,128]{1,0:T(8,128)(2,1)S(1)} %convert_element_type.126), channel_id=1, replica_groups=mesh['dp'=8,'tensor'=4] {'dp'}, dimensions={1}, use_global_device_ids=true | all-gather | bytes 589824 | tf_op jit(solution)/shard_map/all_gather | solution.py:308
  97.0 7.0 multiply_convert_fusion.2.qkv_ref
  104.1 25.5 %attend.1 = (bf16[2048,1024]{1,0:T(8,128)(2,1)}, f32[256,2048]{1,0:T(8,128)S(1)}, f32[4,4,512]{2,1,0:T(4,128)S(1)}) custom-call(bf16[2048,768]{1,0:T(8,128)(2,1)S(1)} %multiply_convert_fusion.2.qkv_ref, bf16[256,1024]{1,0:T(8,128)(2,1)S(1)} %copy-done.1), custom_call_target="tpu_custom_call" | custom-call | tf_op jit(solution)/shard_map/attend/pallas_call | solution.py:143
  129.6 1.3 copy-done.2
  131.6 1.8 convert_element_type.129
  133.4 1.8 convert_element_type.131
  136.4 78.6 %all-reduce.6.cloned.1.call-done = bf16[2048,1024]{1,0:T(8,128)(2,1)} async-done(((bf16[2048,1024]{1,0:T(8,128)(2,1)}), bf16[2048,1024]{1,0:T(8,128)(2,1)}) %all-reduce.6.cloned.1.call-update) | async-done | bytes 4194320 | tf_op jit(solution)/shard_map/psum | solution.py:335
  215.0 5.0 fusion.34
  220.9 2.1 multiply_reduce_fusion
  223.0 3.7 add_convert_fusion
  226.7 40.6 %all-gather.6.cloned.1.call-done = bf16[1024,1024]{1,0:T(8,128)(2,1)} async-done(((bf16[128,1024]{1,0:T(8,128)(2,1)}), bf16[1024,1024]{1,0:T(8,128)(2,1)}) %all-gather.6.cloned.1.call-update) | async-done | bytes 2097168 | tf_op jit(solution)/shard_map/all_gather | solution.py:309
  267.4 10.6 fusion.76
  278.0 41.7 %all-gather.8.cloned.1.call-done = bf16[1024,1024]{1,0:T(8,128)(2,1)} async-done(((bf16[1024,128]{1,0:T(8,128)(2,1)}), bf16[1024,1024]{1,0:T(8,128)(2,1)}) %all-gather.8.cloned.1.call-update) | async-done | bytes 2097168 | tf_op jit(solution)/shard_map/all_gather | solution.py:310
  319.6 13.8 %convert_reduce_fusion.3 = (f32[1024]{0:T(1024)S(1)}, bf16[2048,1024]{1,0:T(8,128)(2,1)S(1)}) fusion(f32[2048,1024]{1,0:T(8,128)} %fusion.76, f32[1024]{0:T(1024)S(1)} %bitcast.83, bf16[1024,1024]{1,0:T(8,128)(2,1)} %all-gather.8.cloned.1.call-done, bf16[2048,1024]{1,0:T(8,128)(2,1)} %param.22, f32[2048]{0:T(1024)S(1)} %fusion.56), kind=kOutput, calls=%fused_computation.43 | convolution fusion | flops 4349492224 | bytes 18890752 | tf_op jit(solution)/shard_map/dot_general | solution.py:263
  333.5 2.0 copy-done.27
  335.5 6.3 convolution_convert_fusion.1
  341.8 83.8 %all-reduce.8.cloned.1.call-done = bf16[2048,1024]{1,0:T(8,128)(2,1)} async-done(((bf16[2048,1024]{1,0:T(8,128)(2,1)}), bf16[2048,1024]{1,0:T(8,128)(2,1)}) %all-reduce.8.cloned.1.call-update) | async-done | bytes 4194320 | tf_op jit(solution)/shard_map/psum | solution.py:355
  425.6 9.0 fusion.30
  434.7 7.2 fusion.71
  441.9 3.1 convert_element_type.141.gh_ref
  445.0 1.4 copy-done.9
  446.4 35.7 %attend_back.1 = bf16[2048,768]{1,0:T(8,128)(2,1)} custom-call(bf16[2048,768]{1,0:T(8,128)(2,1)} %copy-done, bf16[256,1024]{1,0:T(8,128)(2,1)} %all_gather.21.wo_ref, bf16[2048,1024]{1,0:T(8,128)(2,1)} %convert_element_type.141.gh_ref, f32[256,2048]{1,0:T(8,128)} %copy-done.2, f32[4,4,512]{2,1,0:T(4,128)} %copy-done.4), custom_call_target="tpu_custom_call" | custom-call | tf_op jit(solution)/shard_map/attend_back/pallas_call | solution.py:226
  482.1 2.4 convert_reduce_fusion.4
  484.5 1.2 reshape_bitcast_fusion
  485.8 3.4 convolution_convert_fusion.6
  489.2 1.0 copy.65
  490.5 11.4 %convolution_convert_fusion.3 = bf16[1024,1024]{1,0:T(8,128)(2,1)S(1)} fusion(bf16[2048,1024]{1,0:T(8,128)(2,1)} %param.22, f32[2048]{0:T(1024)S(1)} %fusion.56, f32[2048,1024]{1,0:T(8,128)} %fusion.76, f32[1024]{0:T(1024)S(1)} %bitcast.84), kind=kOutput, calls=%fused_computation.58 | convolution fusion | flops 4323278848 | bytes 14692352 | tf_op jit(solution)/shard_map/dot_general | solution.py:257
  501.9 2.6 copy.67
  504.6 9.6 convolution_convert_fusion.4
  514.7 7.4 convolution_convert_fusion.5
  522.2 12.0 %convolution_convert_fusion.2 = bf16[2048,1024]{1,0:T(8,128)(2,1)} fusion(bf16[1024,1024]{1,0:T(8,128)(2,1)} %all-gather.8.cloned.1.call-done, f32[2048,1024]{1,0:T(8,128)} %fusion.76, f32[1024]{0:T(1024)S(1)} %bitcast.85), kind=kOutput, calls=%fused_computation.56 | convolution fusion | flops 4318035968 | bytes 14684160 | tf_op jit(solution)/shard_map/dot_general | solution.py:343
  534.1 4.9 convolution_convert_fusion
  540.4 8.1 reduce-scatter.23.cloned.1.call-done
  548.5 1.0 copy.70
  550.1 63.7 %reduce-scatter.19.cloned.1.call-done = bf16[128,256]{1,0:T(8,128)(2,1)} async-done(((bf16[1024,256]{1,0:T(8,128)(2,1)}), bf16[128,256]{1,0:T(8,128)(2,1)}) %reduce-scatter.19.cloned.1.call-update) | async-done | bytes 65552
  613.8 0.9 copy.66
  615.4 68.8 %reduce-scatter.21.cloned.1.call-done = bf16[128,1024]{1,0:T(8,128)(2,1)} async-done(((bf16[1024,1024]{1,0:T(8,128)(2,1)}), bf16[128,1024]{1,0:T(8,128)(2,1)}) %reduce-scatter.21.cloned.1.call-update) | async-done | bytes 262160
  684.2 1.1 copy.68
  686.0 68.5 %reduce-scatter.15.cloned.1.call-done = bf16[128,1024]{1,0:T(8,128)(2,1)} async-done(((bf16[1024,1024]{1,0:T(8,128)(2,1)}), bf16[128,1024]{1,0:T(8,128)(2,1)}) %reduce-scatter.15.cloned.1.call-update) | async-done | bytes 262160 | tf_op jit(solution)/shard_map/reduce_scatter | solution.py:390
  754.5 1.7 fusion.45
  756.2 65.4 %reduce-scatter.13.cloned.1.call-done = bf16[128,768]{1,0:T(8,128)(2,1)} async-done(((bf16[1024,768]{1,0:T(8,128)(2,1)}), bf16[128,768]{1,0:T(8,128)(2,1)}) %reduce-scatter.13.cloned.1.call-update) | async-done | bytes 196624 | tf_op jit(solution)/shard_map/reduce_scatter | solution.py:388
  821.7 1.6 fusion.49
  826.5 150.6 %all-reduce.10.cloned.1.call-done = (bf16[2048,1024]{1,0:T(8,128)(2,1)}, bf16[2048,1024]{1,0:T(8,128)(2,1)}) async-done(((bf16[2048,1024]{1,0:T(8,128)(2,1)}, bf16[2048,1024]{1,0:T(8,128)(2,1)}), (bf16[2048,1024]{1,0:T(8,128)(2,1)}, bf16[2048,1024]{1,0:T(8,128)(2,1)})) %all-reduce.10.cloned.1.call-update) | async-done | bytes 8388624 | tf_op jit(solution)/shard_map/psum | solution.py:342
  977.2 6.1 fusion.31
  983.9 53.8 %reduce-scatter.17.cloned.1.call-done = f32[6,128]{1,0:T(8,128)} async-done(((f32[6,1024]{1,0:T(8,128)}), f32[6,128]{1,0:T(8,128)}) %reduce-scatter.17.cloned.1.call-update) | async-done | bytes 3088 | tf_op jit(solution)/shard_map/reduce_scatter | solution.py:392
  1037.7 1.3 multiply_reduce_fusion.1
  1039.7 14.2 %fusion.15 = (bf16[2048,1024]{1,0:T(8,128)(2,1)}, bf16[2048,1024]{1,0:T(8,128)(2,1)}) fusion(f32[2048,1024]{1,0:T(8,128)} %copy-done.9, bf16[2048,1024]{1,0:T(8,128)(2,1)} %param.21, bf16[2048,1024]{1,0:T(8,128)(2,1)} %get-tuple-element.78, f32[2048]{0:T(1024)S(1)} %broadcast_multiply_fusion, f32[2048]{0:T(1024)S(1)} %broadcast_multiply_fusion.1, ...), kind=kLoop, calls=%fused_computation.26 | loop fusion | flops 39845888 | bytes 33607680 | tf_op jit(solution)/shard_map/convert_element_type | solution.py:373
  1053.9 40.1 %psum.39 = f32[]{:T(128)} all-reduce(f32[]{:T(128)S(6)} %add.252), channel_id=1, replica_groups=mesh['dp'=8,'tensor'=4] {'dp','tensor'}, use_global_device_ids=true, to_apply=%region_32.33 | all-reduce | flops 1 | bytes 8 | tf_op jit(solution)/shard_map/psum | solution.py:404
  1095.0 1.1 multiply_subtract_fusion.2
  1096.0 1.9 copy.62
  1097.9 0.9 copy.63
  1098.9 0.9 copy.64
  1099.8 1.3 multiply_subtract_fusion.5
  1101.1 1.9 multiply_subtract_fusion.3
  1103.0 2.6 multiply_subtract_fusion
  1105.6 1.3 multiply_subtract_fusion.4
  1106.9 2.6 multiply_subtract_fusion.1
  (109 shorter events, 10.0 us)
Async XLA Ops:
  7.2 89.8 %copy-start.26 = (f32[768]{0:T(1024)S(1)}, f32[768]{0:T(1024)}, u32[]{:S(2)}) copy-start(f32[768]{0:T(1024)} %constant.26.clone.1) | copy-start | bytes 9220
  7.2 89.8 %all-gather.4.cloned.1.call-start = ((), (), s32[]{:S(2)}) async-start(), calls=%async_computation.6 | async-start | bytes 1769472 | tf_op jit(solution)/shard_map/all_gather | solution.py:307
  8.4 88.6 %copy-start.12 = (f32[128,768]{0,1:T(8,128)}, f32[128,768]{0,1:T(8,128)S(1)}, u32[]{:S(2)}) copy-start(f32[128,768]{0,1:T(8,128)S(1)} %copy.54) | copy-start | bytes 1179652
  9.2 205.8 %all-reduce.6.cloned.1.call-start = ((), (), s32[]{:S(2)}) async-start(), calls=%async_computation.7 | async-start | bytes 8388608 | tf_op jit(solution)/shard_map/psum | solution.py:335
  97.0 7.0 copy-start.1
  104.1 116.0 %copy-start = (bf16[2048,768]{1,0:T(8,128)(2,1)}, bf16[2048,768]{1,0:T(8,128)(2,1)S(1)}, u32[]{:S(2)}) copy-start(bf16[2048,768]{1,0:T(8,128)(2,1)S(1)} %multiply_convert_fusion.2.qkv_ref) | copy-start | bytes 9437188
  129.6 1.3 copy-start.2
  130.9 0.6 copy-start.4
  131.5 135.8 %all-gather.6.cloned.1.call-start = ((), (), s32[]{:S(2)}) async-start(), calls=%async_computation.8 | async-start | bytes 2359296 | tf_op jit(solution)/shard_map/all_gather | solution.py:309
  133.4 186.2 %all-gather.8.cloned.1.call-start = ((), (), s32[]{:S(2)}) async-start(), calls=%async_computation.9 | async-start | bytes 2359296 | tf_op jit(solution)/shard_map/all_gather | solution.py:310
  135.2 290.3 %all-reduce.8.cloned.1.call-start = ((), (), s32[]{:S(2)}) async-start(), calls=%async_computation.10 | async-start | bytes 8388608 | tf_op jit(solution)/shard_map/psum | solution.py:355
  215.0 5.1 copy-start.5
  215.0 5.9 copy-start.7
  319.6 15.8 %copy-start.24 = (bf16[1024,1024]{1,0:T(8,128)(2,1)S(1)}, bf16[1024,1024]{1,0:T(8,128)(2,1)}, u32[]{:S(2)}) copy-start(bf16[1024,1024]{1,0:T(8,128)(2,1)} %all-gather.6.cloned.1.call-done) | copy-start | bytes 6291460
  333.5 2.0 copy-start.27
  341.8 206.7 %reduce-scatter.23.cloned.1.call-start = ((), (), s32[]{:S(2)}) async-start(), calls=%async_computation.16 | async-start | bytes 884736
  425.6 9.0 copy-start.6
  425.6 9.0 copy-start.8
  425.6 9.1 copy-start.10
  441.9 4.5 copy-start.9
  446.4 39.4 %copy-start.3 = (f32[256,2048]{1,0:T(8,128)S(1)}, f32[256,2048]{1,0:T(8,128)}, u32[]{:S(2)}) copy-start(f32[256,2048]{1,0:T(8,128)} %copy-done.2) | copy-start | bytes 6291460
  485.7 128.0 %reduce-scatter.19.cloned.1.call-start = ((), (), s32[]{:S(2)}) async-start(), calls=%async_computation.14 | async-start | bytes 589824
  490.2 193.9 %reduce-scatter.21.cloned.1.call-start = ((), (), s32[]{:S(2)}) async-start(), calls=%async_computation.15 | async-start | bytes 2359296
  504.5 10.2 copy-start.11
  504.5 250.0 %reduce-scatter.15.cloned.1.call-start = ((), (), s32[]{:S(2)}) async-start(), calls=%async_computation.12 | async-start | bytes 2359296 | tf_op jit(solution)/shard_map/reduce_scatter | solution.py:390
  514.2 307.4 %reduce-scatter.13.cloned.1.call-start = ((), (), s32[]{:S(2)}) async-start(), calls=%async_computation.11 | async-start | bytes 1769472 | tf_op jit(solution)/shard_map/reduce_scatter | solution.py:388
  522.1 455.0 %all-reduce.10.cloned.1.call-start = ((), (), s32[]{:S(2)}) async-start(), calls=%async_computation.17 | async-start | bytes 16777216 | tf_op jit(solution)/shard_map/psum | solution.py:342
  522.2 12.0 %copy-start.25 = (bf16[1024,768]{0,1:T(8,128)(2,1)S(1)}, bf16[1024,768]{0,1:T(8,128)(2,1)}, u32[]{:S(2)}) copy-start(bf16[1024,768]{0,1:T(8,128)(2,1)} %all-gather.4.cloned.1.call-done) | copy-start | bytes 4718596
  539.1 1.0 copy-start.19
  539.1 1.2 copy-start.20
  539.1 498.6 %reduce-scatter.17.cloned.1.call-start = ((), (), s32[]{:S(2)}) async-start(), calls=%async_computation.13 | async-start | bytes 36864 | tf_op jit(solution)/shard_map/reduce_scatter | solution.py:392
  614.7 424.9 %copy-start.18 = (bf16[256,128]{1,0:T(8,128)(2,1)}, bf16[256,128]{1,0:T(8,128)(2,1)S(1)}, u32[]{:S(2)}) copy-start(bf16[256,128]{1,0:T(8,128)(2,1)S(1)} %copy.66) | copy-start | bytes 196612
  1039.6 55.1 %copy-start.17 = (bf16[128,768]{1,0:T(8,128)(2,1)S(1)}, bf16[128,768]{1,0:T(8,128)(2,1)}, u32[]{:S(2)}) copy-start(bf16[128,768]{1,0:T(8,128)(2,1)} %reduce-scatter.13.cloned.1.call-done) | copy-start | bytes 589828
  1039.7 55.3 %copy-start.13 = (f32[128,768]{0,1:T(8,128)S(1)}, f32[128,768]{0,1:T(8,128)}, u32[]{:S(2)}) copy-start(f32[128,768]{0,1:T(8,128)} %copy-done.12) | copy-start | bytes 1179652
  1053.8 49.1 %copy-start.14 = (f32[1024,128]{1,0:T(8,128)S(1)}, f32[1024,128]{1,0:T(8,128)}, u32[]{:S(2)}) copy-start(f32[1024,128]{1,0:T(8,128)} %param.27) | copy-start | bytes 1572868
  1053.8 51.7 %copy-start.21 = (f32[6,128]{1,0:T(8,128)S(1)}, f32[6,128]{1,0:T(8,128)}, u32[]{:S(2)}) copy-start(f32[6,128]{1,0:T(8,128)} %param.28) | copy-start | bytes 9220
  1053.8 51.7 %copy-start.22 = (f32[6,128]{1,0:T(8,128)S(1)}, f32[6,128]{1,0:T(8,128)}, u32[]{:S(2)}) copy-start(f32[6,128]{1,0:T(8,128)} %reduce-scatter.17.cloned.1.call-done) | copy-start | bytes 9220
  1053.9 51.7 %copy-start.23 = (f32[6,128]{1,0:T(8,128)S(1)}, f32[6,128]{1,0:T(8,128)}, u32[]{:S(2)}) copy-start(f32[6,128]{1,0:T(8,128)} %param.38) | copy-start | bytes 9220
  1053.9 53.0 %copy-start.15 = (f32[128,1024]{1,0:T(8,128)S(1)}, f32[128,1024]{1,0:T(8,128)}, u32[]{:S(2)}) copy-start(f32[128,1024]{1,0:T(8,128)} %param.26) | copy-start | bytes 1572868
  1053.9 53.0 %copy-start.16 = (bf16[128,1024]{1,0:T(8,128)(2,1)S(1)}, bf16[128,1024]{1,0:T(8,128)(2,1)}, u32[]{:S(2)}) copy-start(bf16[128,1024]{1,0:T(8,128)(2,1)} %reduce-scatter.15.cloned.1.call-done) | copy-start | bytes 786436
Sparse Core Ops, SparseCore 0:
  10.7 48.2 all-gather.3
  131.7 83.2 all-reduce.5
  217.9 49.4 all-gather.5
  270.0 49.5 all-gather.7
  341.9 83.6 all-reduce.7
  485.8 62.6 reduce-scatter.22
  552.8 60.9 reduce-scatter.18
  617.3 66.8 reduce-scatter.20
  687.7 66.7 reduce-scatter.14
  757.8 63.8 reduce-scatter.12
  825.0 152.0 all-reduce.9
  984.0 53.6 reduce-scatter.16

commit v2 on v1

--- a/solution.py
+++ b/solution.py
@@ -132,14 +132,14 @@
         m, l, acc = carry[h]
         ot_ref[h * d:(h + 1) * d, :] = acc / l
         lse_ref[0, h:h + 1, :] = m + jnp.log(l)
-    part_ref[...] = dot(ot_ref[...].astype(BF), wo_ref[...], TN).astype(BF)
+    part_ref[...] = dot(ot_ref[...].astype(BF).T, wo_ref[...], NT).astype(BF)
 
 
 def attend(qkv, wo, heads, d, total_heads, bq=512):
     n, width = qkv.shape[0], heads * d
     bq = min(bq, n)
     nb = n // bq
-    feats = wo.shape[1]
+    feats = wo.shape[0]
     return pl.pallas_call(
         functools.partial(attend_kernel, heads, d, total_heads, bq),
         grid=(nb,),
@@ -178,7 +178,7 @@
         lax.fori_loop(0, nb, fill, 0)
 
     rows_i = pl.ds(pl.multiple_of(i * bq, bq), bq)
-    grad_o = dot(gh_ref[...], wo_ref[...], NT).astype(BF)
+    grad_o = dot(gh_ref[...], wo_ref[...]).astype(BF)
     grad_t = grad_o.T
     q_nat = qkv_ref[rows_i, 0:width]
     qt = q_nat.T
@@ -221,7 +221,7 @@
     n, width = qkv.shape[0], heads * d
     bq = min(bq, n)
     nb = n // bq
-    feats = wo.shape[1]
+    feats = wo.shape[0]
     back = lambda i: nb - 1 - i
     return pl.pallas_call(
         functools.partial(attend_back_kernel, heads, d, total_heads, bq),
@@ -236,6 +236,249 @@
         compiler_params=pltpu.CompilerParams(vmem_limit_bytes=56 * 2**20),
         name="attend_back",
     )(qkv, wo, gh, ot, lse)
+
+
+def at_dp(index):
+    return {"dp": index}
+
+
+def at_tensor(index):
+    return {"tensor": index}
+
+
+def remote(src, dst, send, recv, where):
+    return pltpu.make_async_remote_copy(
+        src_ref=src, dst_ref=dst, send_sem=send, recv_sem=recv, device_id=where, device_id_type=pl.DeviceIdType.MESH
+    )
+
+
+def greet(n_dp, n_tensor):
+    me, rank = lax.axis_index("dp"), lax.axis_index("tensor")
+    barrier = pltpu.get_barrier_semaphore()
+
+    def along_dp(k, c):
+        pl.semaphore_signal(barrier, inc=1, device_id=at_dp(lax.rem(me + k, n_dp)), device_id_type=pl.DeviceIdType.MESH)
+        return c
+
+    lax.fori_loop(1, n_dp, along_dp, 0)
+    for k in range(1, n_tensor):
+        pl.semaphore_signal(
+            barrier, inc=1, device_id=at_tensor(lax.rem(rank + k, n_tensor)), device_id_type=pl.DeviceIdType.MESH
+        )
+    pl.semaphore_wait(barrier, n_dp + n_tensor - 2)
+
+
+def gather_kernel(n_dp, n_tensor, cuts, shard_ref, vec_ref, out_ref, vecs_ref, own_sem, xs, xr, zs, zr, vs, vr):
+    me = lax.axis_index("dp")
+    lines = n_dp // 2
+    z, x = me // 2, lax.rem(me, 2)
+    other = at_dp(z * 2 + 1 - x)
+    rows = shard_ref.shape[0]
+
+    def place(index, cut):
+        first, count = cut
+        return out_ref.at[pl.ds(pl.multiple_of(index * rows, rows), rows), pl.ds(first, count)]
+
+    def own(cut):
+        first, count = cut
+        return shard_ref.at[:, pl.ds(first, count)]
+
+    def to_x(s, zz, src):
+        return remote(src, place(zz * 2 + x, cuts[s]), xs.at[s, zz], xr.at[s, zz], other)
+
+    def to_z(s, k):
+        return remote(own(cuts[s]), place(me, cuts[s]), zs.at[s, k], zr.at[s, z], at_dp(lax.rem(z + k, lines) * 2 + x))
+
+    def from_z(s, zz):
+        spot = place(zz * 2 + x, cuts[s])
+        return remote(spot, spot, zs.at[s, 0], zr.at[s, zz], other)
+
+    def vec_to(k):
+        return remote(vec_ref, vecs_ref.at[me], vs.at[k], vr.at[me], at_dp(lax.rem(me + k, n_dp)))
+
+    def vec_from(source):
+        return remote(vec_ref, vecs_ref.at[source], vs.at[0], vr.at[source], other)
+
+    mine = pltpu.make_async_copy(shard_ref, out_ref.at[pl.ds(pl.multiple_of(me * rows, rows), rows)], own_sem.at[0])
+    mine.start()
+    mine_vec = pltpu.make_async_copy(vec_ref, vecs_ref.at[me], own_sem.at[1])
+    mine_vec.start()
+    greet(n_dp, n_tensor)
+    count = len(cuts)
+
+    def loop(body, first, last):
+        lax.fori_loop(first, last, lambda k, c: (body(k), c)[1], 0)
+
+    loop(lambda k: vec_to(k).start(), 1, n_dp)
+
+    def begin(s):
+        loop(lambda k: to_z(s, k).start(), 1, lines)
+        to_x(s, z, own(cuts[s])).start()
+
+    def forward(s):
+        def step(k):
+            zz = lax.rem(z + k, lines)
+            from_z(s, zz).wait_recv()
+            to_x(s, zz, place(zz * 2 + x, cuts[s])).start()
+        loop(step, 1, lines)
+
+    def sent(s):
+        loop(lambda k: to_z(s, k).wait_send(), 1, lines)
+        loop(lambda zz: to_x(s, zz, own(cuts[s])).wait_send(), 0, lines)
+
+    for s in range(count):
+        begin(s)
+        if s:
+            forward(s - 1)
+    forward(count - 1)
+    for s in range(count):
+        sent(s)
+        loop(lambda zz: to_x(s, zz, own(cuts[s])).wait_recv(), 0, lines)
+    loop(lambda k: vec_to(k).wait_send(), 1, n_dp)
+    loop(lambda k: vec_from(lax.rem(me + k, n_dp)).wait_recv(), 1, n_dp)
+    mine.wait()
+    mine_vec.wait()
+
+
+def gather_weights(shard, vec, n_dp, n_tensor, cuts, collective_id):
+    rows, cols = shard.shape
+    lines, count = n_dp // 2, len(cuts)
+    anywhere = pl.BlockSpec(memory_space=pl.ANY)
+    vmem = pl.BlockSpec(memory_space=pltpu.VMEM)
+    dma = pltpu.SemaphoreType.DMA
+    return pl.pallas_call(
+        functools.partial(gather_kernel, n_dp, n_tensor, cuts),
+        in_specs=[anywhere, vmem],
+        out_specs=[anywhere, vmem],
+        out_shape=[jax.ShapeDtypeStruct((n_dp * rows, cols), BF), jax.ShapeDtypeStruct((n_dp,) + vec.shape, BF)],
+        scratch_shapes=[dma((2,))] + [dma((count, lines))] * 4 + [dma((n_dp,))] * 2,
+        compiler_params=pltpu.CompilerParams(collective_id=collective_id, has_side_effects=True),
+        name="gather_weights",
+    )(shard, vec)
+
+
+def scatter_kernel(n_dp, n_tensor, parts, ahead, g_ref, vec_ref, total_ref, vec_out, square_out,
+                   x_buf, z_buf, v_buf, q_buf, t_buf, xs, xr, zs, zr, vs, vr, qs, qr, ts, tr):
+    me, rank = lax.axis_index("dp"), lax.axis_index("tensor")
+    lines = n_dp // 2
+    z, x = me // 2, lax.rem(me, 2)
+    rows, cols = total_ref.shape
+    wide = cols // parts
+    items = parts * lines
+
+    def loop(body, first, last):
+        lax.fori_loop(first, last, lambda k, c: (body(k), c)[1], 0)
+
+    def chunk(dest, part):
+        return (pl.ds(pl.multiple_of(dest * rows, rows), rows), pl.ds(pl.multiple_of(part * wide, wide), wide))
+
+    def which(item):
+        return item // lines, lax.rem(z + 1 + lax.rem(item, lines), lines)
+
+    def to_x(item):
+        part, dz = which(item)
+        return remote(g_ref.at[chunk(dz * 2 + 1 - x, part)], x_buf.at[part, dz], xs.at[part, dz], xr.at[part, dz],
+                      at_dp(z * 2 + 1 - x))
+
+    def to_z(part, dz):
+        return remote(x_buf.at[part, dz], z_buf.at[part, z], zs.at[part, dz], zr.at[part, z], at_dp(dz * 2 + x))
+
+    def from_z(part, zz):
+        return remote(z_buf.at[part, zz], z_buf.at[part, zz], zs.at[part, zz], zr.at[part, zz], at_dp(zz * 2 + x))
+
+    def vec_to(k):
+        dest = lax.rem(me + k, n_dp)
+        return remote(vec_ref.at[dest], v_buf.at[me], vs.at[k], vr.at[me], at_dp(dest))
+
+    def square_to(k):
+        return remote(q_buf.at[me], q_buf.at[me], qs.at[k], qr.at[me], at_dp(lax.rem(me + k, n_dp)))
+
+    def tensor_to(k):
+        return remote(t_buf.at[rank], t_buf.at[rank], ts.at[k], tr.at[rank], at_tensor(lax.rem(rank + k, n_tensor)))
+
+    greet(n_dp, n_tensor)
+    for item in range(min(ahead, items)):
+        to_x(item).start()
+    loop(lambda k: vec_to(k).start(), 1, n_dp)
+
+    def step(item):
+        part, dz = which(item)
+        to_x(item).wait()
+        if items > ahead:
+            @pl.when(item + ahead < items)
+            def _():
+                to_x(item + ahead).start()
+        summed = x_buf[part, dz].astype(F32) + g_ref[chunk(dz * 2 + x, part)].astype(F32)
+
+        @pl.when(dz != z)
+        def _():
+            x_buf[part, dz] = summed.astype(BF)
+            to_z(part, dz).start()
+
+        @pl.when(dz == z)
+        def _():
+            total_ref[:, pl.ds(pl.multiple_of(part * wide, wide), wide)] = summed
+
+    loop(step, 0, items)
+
+    def finish(part):
+        def add(k):
+            zz = lax.rem(z + k, lines)
+            from_z(part, zz).wait_recv()
+            total_ref[:, pl.ds(pl.multiple_of(part * wide, wide), wide)] += z_buf[part, zz].astype(F32)
+            to_z(part, zz).wait_send()
+        loop(add, 1, lines)
+
+    loop(finish, 0, parts)
+
+    v_buf[me] = vec_ref[me]
+    def vec_arrived(k):
+        source = lax.rem(me + k, n_dp)
+        remote(v_buf.at[source], v_buf.at[source], vs.at[0], vr.at[source], at_dp(source)).wait_recv()
+        vec_to(k).wait_send()
+    loop(vec_arrived, 1, n_dp)
+    vec_total = lax.fori_loop(0, n_dp, lambda k, acc: acc + v_buf[k], jnp.zeros(vec_out.shape, F32))
+    vec_out[...] = vec_total
+
+    counted = lax.broadcasted_iota(jnp.int32, vec_out.shape, 0) >= jnp.where(rank == 0, 0, 6)
+    vec_kept = jnp.where(counted, vec_total, 0.0)
+    square = jnp.sum(total_ref[...] * total_ref[...]) + jnp.sum(vec_kept * vec_kept)
+    q_buf[me] = jnp.full(q_buf.shape[1:], square, F32)
+    loop(lambda k: square_to(k).start(), 1, n_dp)
+    def square_arrived(k):
+        source = lax.rem(me + k, n_dp)
+        remote(q_buf.at[source], q_buf.at[source], qs.at[0], qr.at[source], at_dp(source)).wait_recv()
+        square_to(k).wait_send()
+    loop(square_arrived, 1, n_dp)
+    t_buf[rank] = lax.fori_loop(0, n_dp, lambda k, acc: acc + q_buf[k], jnp.zeros(q_buf.shape[1:], F32))
+    for k in range(1, n_tensor):
+        tensor_to(k).start()
+    for k in range(1, n_tensor):
+        source = lax.rem(rank + k, n_tensor)
+        remote(t_buf.at[source], t_buf.at[source], ts.at[0], tr.at[source], at_tensor(source)).wait_recv()
+        tensor_to(k).wait_send()
+    square_out[...] = lax.fori_loop(0, n_tensor, lambda k, acc: acc + t_buf[k], jnp.zeros(q_buf.shape[1:], F32))
+
+
+def scatter_gradients(grads, vec, n_dp, n_tensor, collective_id, parts=4, ahead=3):
+    rows, cols = grads.shape[0] // n_dp, grads.shape[1]
+    lines = n_dp // 2
+    vmem = pl.BlockSpec(memory_space=pltpu.VMEM)
+    dma = pltpu.SemaphoreType.DMA
+    wide = cols // parts
+    tile = (8, 128)
+    return pl.pallas_call(
+        functools.partial(scatter_kernel, n_dp, n_tensor, parts, ahead),
+        in_specs=[vmem, vmem],
+        out_specs=[vmem, vmem, vmem],
+        out_shape=[jax.ShapeDtypeStruct((rows, cols), F32), jax.ShapeDtypeStruct(vec.shape[1:], F32),
+                   jax.ShapeDtypeStruct(tile, F32)],
+        scratch_shapes=[pltpu.VMEM((parts, lines, rows, wide), BF), pltpu.VMEM((parts, lines, rows, wide), BF),
+                        pltpu.VMEM(vec.shape, F32), pltpu.VMEM((n_dp,) + tile, F32), pltpu.VMEM((n_tensor,) + tile, F32)]
+        + [dma((parts, lines))] * 4 + [dma((n_dp,))] * 4 + [dma((n_tensor,))] * 2,
+        compiler_params=pltpu.CompilerParams(collective_id=collective_id, has_side_effects=True, vmem_limit_bytes=48 * 2**20),
+        name="scatter_gradients",
+    )(grads, vec)
 
 
 def normalize(values):
@@ -303,19 +546,29 @@
     split_first,
     split_second,
 ):
-    gathered = (
-        lax.all_gather(by_kind(joint_weight.astype(jnp.bfloat16)), "dp", axis=0, tiled=True),
-        lax.all_gather(output_weight.astype(jnp.bfloat16), "dp", axis=1, tiled=True),
-        lax.all_gather(widen_weight.astype(jnp.bfloat16), "dp", axis=0, tiled=True),
-        lax.all_gather(narrow_weight.astype(jnp.bfloat16), "dp", axis=1, tiled=True),
-        lax.all_gather(shared_vectors.astype(jnp.bfloat16), "dp", axis=1, tiled=True),
-        lax.all_gather(split_vectors.astype(jnp.bfloat16), "dp", axis=1, tiled=True),
-    )
-    joint_work, output_work, widen_work, narrow_work, shared_work, split_work = gathered
-    shared_float = shared_work.astype(jnp.float32)
-    split_float = split_work.astype(jnp.float32)[0]
+    n_dp, n_tensor = lax.axis_size("dp"), lax.axis_size("tensor")
+    sizes = (joint_weight.shape[1], widen_weight.shape[1], output_weight.shape[0], narrow_weight.shape[0])
+    starts = (0, sizes[0], sizes[0] + sizes[1], sum(sizes[:3]), sum(sizes))
+    spans = [slice(first, last) for first, last in zip(starts[:-1], starts[1:])]
+    shard = jnp.concatenate(
+        [by_kind(joint_weight), widen_weight, output_weight.T, narrow_weight.T], axis=1
+    ).astype(BF)
+    shared_cols, split_cols = shared_vectors.shape[1], split_vectors.shape[1]
+    vec_cols = -(-max(shared_cols, split_cols) // 128) * 128
+    vec_shard = jnp.concatenate(
+        [
+            jnp.pad(shared_vectors, ((0, 0), (0, vec_cols - shared_cols))),
+            jnp.pad(split_vectors, ((0, 9), (0, vec_cols - split_cols))),
+        ],
+        axis=0,
+    ).astype(BF)
+    cuts = tuple((first, last - first) for first, last in zip(starts[:-1], starts[1:]))
+    work, vecs = gather_weights(shard, vec_shard, n_dp, n_tensor, cuts, 0)
+    joint_work, widen_work, output_t, narrow_t = [work[:, span] for span in spans]
+    shared_float = jnp.swapaxes(vecs[:, :6, :shared_cols], 0, 1).reshape(6, D).astype(F32)
+    split_float = vecs[:, 6, :split_cols].reshape(-1).astype(F32)
     head_size = D // HEADS
-    head_cols = output_work.shape[0]
+    head_cols = sizes[2]
     local_heads = head_cols // head_size
     tensor_rank = lax.axis_index("tensor")
     widen_bias = split_float[2 * head_cols :]
@@ -331,7 +584,7 @@
     attn_input = (normed_one * shared_float[0] + shared_float[1]).astype(jnp.bfloat16)
     joint = jnp.dot(attn_input, joint_work, preferred_element_type=jnp.float32)
     qkv = ((joint + qkv_bias) * qkv_scale).astype(BF)
-    attn_part, heads_out, lse = attend(qkv, output_work, local_heads, head_size, HEADS)
+    attn_part, heads_out, lse = attend(qkv, output_t, local_heads, head_size, HEADS)
     attn_sum = lax.psum(attn_part, "tensor").astype(jnp.float32)
     hidden_one = inputs + attn_sum + shared_float[4]
     normed_two, inverse_two = normalize(hidden_one)
@@ -340,7 +593,7 @@
     activated, gelu_pull = jax.vjp(gelu_tanh, widened)
     activated_low = activated.astype(jnp.bfloat16)
     mlp_sum = lax.psum(
-        jnp.dot(activated_low, narrow_work, preferred_element_type=jnp.float32).astype(
+        against_rows(activated_low, narrow_t).astype(
             jnp.bfloat16
         ),
         "tensor",
@@ -349,17 +602,19 @@
     layer_output = (result * live_rows).astype(jnp.bfloat16)
     grad_out = cotangent.astype(jnp.float32) * live_rows
     grad_out_low = grad_out.astype(jnp.bfloat16)
-    grad_narrow = over_rows(activated_low, grad_out_low)
-    grad_widened = gelu_pull(against_rows(grad_out_low, narrow_work))[0].astype(jnp.bfloat16)
+    grad_narrow = over_rows(grad_out_low, activated_low)
+    grad_widened = gelu_pull(jnp.dot(grad_out_low, narrow_t, preferred_element_type=F32))[0].astype(jnp.bfloat16)
     grad_widen = over_rows(mlp_input, grad_widened)
     grad_mlp_in = lax.psum(
         against_rows(grad_widened, widen_work).astype(jnp.bfloat16), "tensor"
     ).astype(jnp.float32)
     grad_hidden = grad_out + normalize_back(grad_mlp_in, normed_two, inverse_two, shared_float[2])
     grad_hidden_low = grad_hidden.astype(jnp.bfloat16)
-    grad_output = jnp.dot(heads_out.astype(BF), grad_hidden_low, preferred_element_type=F32)
+    grad_output = lax.dot_general(
+        grad_hidden_low, heads_out.astype(BF), (((0,), (1,)), ((), ())), preferred_element_type=F32
+    )
     grad_joint_act = attend_back(
-        qkv, output_work, grad_hidden_low, heads_out, lse, local_heads, head_size, HEADS
+        qkv, output_t, grad_hidden_low, heads_out, lse, local_heads, head_size, HEADS
     )
     grad_qkv_bias = jnp.sum(grad_joint_act, axis=0, dtype=jnp.float32)
     grad_query_bias = grad_qkv_bias[:head_cols]
@@ -383,26 +638,28 @@
     )
     grad_split = jnp.concatenate(
         [grad_query_bias, grad_value_bias, jnp.sum(grad_widened, axis=0, dtype=jnp.float32)]
-    )[None]
-    joint_sum, output_sum, widen_sum, narrow_sum, shared_sum, split_sum = (
-        lax.psum_scatter(grad_joint.astype(BF), "dp", scatter_dimension=0, tiled=True),
-        lax.psum_scatter(grad_output.astype(BF), "dp", scatter_dimension=1, tiled=True),
-        lax.psum_scatter(grad_widen.astype(BF), "dp", scatter_dimension=0, tiled=True),
-        lax.psum_scatter(grad_narrow.astype(BF), "dp", scatter_dimension=1, tiled=True),
-        lax.psum_scatter(grad_shared, "dp", scatter_dimension=1, tiled=True),
-        lax.psum_scatter(grad_split, "dp", scatter_dimension=1, tiled=True),
-    )
-    joint_sum, output_sum, widen_sum, narrow_sum = (
-        by_head(joint_sum.astype(F32)), output_sum.astype(F32), widen_sum.astype(F32), narrow_sum.astype(F32)
-    )
-    local_square = jnp.sum(joint_sum * joint_sum) + jnp.sum(output_sum * output_sum)
-    local_square = local_square + jnp.sum(widen_sum * widen_sum) + jnp.sum(narrow_sum * narrow_sum)
-    local_square = local_square + jnp.sum(split_sum * split_sum)
-    local_square = local_square + jnp.where(
-        tensor_rank == 0, jnp.sum(shared_sum * shared_sum), jnp.float32(0.0)
-    )
-    total_square = lax.psum(local_square, ("dp", "tensor"))
-    grad_norm = jnp.sqrt(total_square)
+    )
+    grads = jnp.concatenate(
+        [part.astype(BF) for part in (grad_joint, grad_widen, grad_output, grad_narrow)], axis=1
+    )
+    grad_vecs = jnp.concatenate(
+        [
+            jnp.pad(
+                jnp.swapaxes(grad_shared.reshape(6, n_dp, shared_cols), 0, 1),
+                ((0, 0), (0, 0), (0, vec_cols - shared_cols)),
+            ),
+            jnp.pad(grad_split.reshape(n_dp, 1, split_cols), ((0, 0), (0, 1), (0, vec_cols - split_cols))),
+        ],
+        axis=1,
+    )
+    grad_sum, vec_sum, square = scatter_gradients(grads, grad_vecs, n_dp, n_tensor, 1)
+    joint_sum = by_head(grad_sum[:, spans[0]])
+    widen_sum = grad_sum[:, spans[1]]
+    output_sum = grad_sum[:, spans[2]].T
+    narrow_sum = grad_sum[:, spans[3]].T
+    shared_sum = vec_sum[:6, :shared_cols]
+    split_sum = vec_sum[6:7, :split_cols]
+    grad_norm = jnp.sqrt(square[0, 0])
     factor = jnp.minimum(1.0, CLIP_LIMIT / (grad_norm + 1e-06))
     joint_new = adam_step(
         joint_weight, joint_first, joint_second, factor * joint_sum, MATRIX_RATE, MATRIX_DECAY

time: 1130 us -> 743 us (0.66)
  waiting for transfers between devices: 724 us -> 274 us
  Pallas kernels: 61.3 us -> 239 us
  blocking collectives: 117 us -> 0 us
  local copies, waits for them, and re-layouts: 23.1 us -> 46.6 us
    reduce_scatter x3 -> x0, waiting for transfers between devices: 188 us -> none  [the longest x1 68.5 us: on_device(): lax.psum_scatter(grad_widen.astype(BF), 'dp', scatter_dimension=0, tiled=...]
    pallas_call x0 -> x2, Pallas kernels: none -> 177 us  [the longest x1 90.2 us: scatter_gradients(): pl.pallas_call(functools.partial(scatter_kernel, n_dp, n_tensor, parts, a...]
    unnamed x15 -> x3, waiting for transfers between devices: 141 us -> 0.05 us
    all_gather x3 -> x0, waiting for transfers between devices: 82.3 us -> none  [the longest x1 41.7 us: on_device(): lax.all_gather(narrow_weight.astype(jnp.bfloat16), 'dp', axis=1, tiled=True)]
    all_gather x2 -> x0, blocking collectives: 54.3 us -> none  [the longest x1 28.1 us: on_device(): lax.all_gather(output_weight.astype(jnp.bfloat16), 'dp', axis=1, tiled=True)]
    psum x1 -> x0, blocking collectives: 40.1 us -> none  [on_device(): total_square = lax.psum(local_square, ('dp', 'tensor'))]
    psum x1, waiting for transfers between devices: 151 us -> 127 us  [on_device(): lax.psum(against_rows(activated_low, narrow_t).astype(jnp.bfloat16), 'ten...]
    unnamed x1 -> x0, blocking collectives: 23.1 us -> none
  transfers between devices with their start and end apart: 12 -> 3, of which waited for: 11 -> 3; matrix products, arithmetic and copies ran while one was open for 9% -> 8% of each run, Pallas kernels for 0% -> 0%
where the time goes in v2:
time: 743 us; the launch traced here: 734 us
  waiting for transfers between devices  274 us (37%)
  Pallas kernels  239 us (32%)
  matrix products  79.3 us (11%)
  other arithmetic  77.6 us (10%)
  local copies, waits for them, and re-layouts  46.6 us (6%)
  between operations  17.1 us (2%)
    psum x1, waiting for transfers between devices, on_device(): lax.psum(against_rows(activated_low, narrow_t).astype(jnp.bfloat16), 'ten...  127 us
    pallas_call x1, Pallas kernels, scatter_gradients(): pl.pallas_call(functools.partial(scatter_kernel, n_dp, n_tensor, parts, a...  90.2 us
    pallas_call x1, Pallas kernels, gather_weights(): pl.pallas_call(functools.partial(gather_kernel, n_dp, n_tensor, cuts), in...  86.9 us
    psum x1, waiting for transfers between devices, on_device(): attn_sum = lax.psum(attn_part, 'tensor').astype(jnp.float32)  82.2 us
    psum x1, waiting for transfers between devices, on_device(): lax.psum(against_rows(grad_widened, widen_work).astype(jnp.bfloat16), 'te...  64.5 us
    unnamed x104, local copies, waits for them, and re-layouts  39.8 us
    pallas_call x1, Pallas kernels, attend_back(): pl.pallas_call(functools.partial(attend_back_kernel, heads, d, total_head...  35.9 us
    dot_general x3, matrix products, over_rows(): lax.dot_general(left, right, (((0,), (0,)), ((), ())), preferred_element_...  28.3 us
  transfers between devices with their start and end apart: 3, of which 3 were waited for; matrix products, arithmetic and copies ran while one was open for 8% of the time, Pallas kernels for 0%

profile of v2, /device:TPU:0, one launch (start us, length us, event | category | flops | bytes accessed | tf_op | source)
XLA Modules:
  0.0 733.7 jit_solution(8250249015488467496)
XLA Ops:
  8.6 1.0 copy.66
  10.3 1.1 convert.30
  11.4 1.2 copy.64
  13.4 1.2 copy.67
  15.4 0.9 pad_maximum_fusion.1.shard_ref
  16.4 86.9 %gather_weights.1 = (bf16[1024,3072]{1,0:T(8,128)(2,1)}, bf16[8,16,256]{2,1,0:T(8,128)(2,1)}) custom-call(bf16[128,3072]{1,0:T(8,128)(2,1)} %pad_maximum_fusion.1.shard_ref, bf16[16,256]{1,0:T(8,128)(2,1)} %fusion.57.vec_ref), custom_call_target="tpu_custom_call" | custom-call | tf_op jit(solution)/shard_map/gather_weights/pallas_call | solution.py:349
  103.3 0.8 convert_reduce_fusion.5
  104.8 2.8 convert_reduce_fusion.2
  107.6 3.0 fusion.16
  111.4 1.1 slice.87.wo_ref
  112.5 7.0 multiply_convert_fusion.2.qkv_ref
  119.6 25.6 %attend.1 = (bf16[2048,1024]{1,0:T(8,128)(2,1)}, f32[256,2048]{1,0:T(8,128)S(1)}, f32[4,4,512]{2,1,0:T(4,128)S(1)}) custom-call(bf16[2048,768]{1,0:T(8,128)(2,1)S(1)} %multiply_convert_fusion.2.qkv_ref, bf16[1024,256]{1,0:T(8,128)(2,1)S(1)} %slice.87.wo_ref), custom_call_target="tpu_custom_call" | custom-call | tf_op jit(solution)/shard_map/attend/pallas_call | solution.py:143
  145.2 1.3 copy-done.2
  147.6 1.3 slice.111
  149.6 1.7 copy.79
  151.2 1.7 copy.80
  152.9 0.9 copy.73
  153.8 1.9 copy.76
  155.7 2.0 copy.83
  157.7 2.0 copy.84
  159.8 82.2 %all-reduce.9.cloned.1.call-done = bf16[2048,1024]{1,0:T(8,128)(2,1)} async-done(((bf16[2048,1024]{1,0:T(8,128)(2,1)}), bf16[2048,1024]{1,0:T(8,128)(2,1)}) %all-reduce.9.cloned.1.call-update) | async-done | bytes 4194320 | tf_op jit(solution)/shard_map/psum | solution.py:588
  242.0 5.0 fusion.34
  247.0 0.8 copy-done.7
  247.9 2.1 multiply_reduce_fusion
  250.0 2.4 add_convert_fusion
  252.4 2.0 copy-done.15
  254.5 4.6 fusion.41
  259.1 9.8 %convert_reduce_fusion.3 = (f32[1024]{0:T(1024)S(1)}, bf16[2048,1024]{1,0:T(8,128)(2,1)S(1)}) fusion(f32[2048,1024]{1,0:T(8,128)S(1)} %fusion.41, f32[1024]{0:T(1024)S(1)} %copy-done.37, bf16[1024,3072]{1,0:T(8,128)(2,1)S(1)} %bitcast.71, bf16[2048,1024]{1,0:T(8,128)(2,1)S(1)} %copy-done.14, f32[2048]{0:T(1024)S(1)} %fusion.58), kind=kOutput, calls=%fused_computation.43 | convolution fusion | flops 4349492224 | bytes 18890752 | tf_op jit(solution)/shard_map/dot_general | solution.py:606
  269.0 2.0 copy-done.39
  270.9 6.4 convolution_convert_fusion.1
  277.4 9.4 %convolution_convert_fusion.4 = bf16[1024,1024]{1,0:T(8,128)(2,1)} fusion(bf16[2048,1024]{1,0:T(8,128)(2,1)} %copy-done.15, bf16[2048,1024]{1,0:T(8,128)(2,1)} %copy-done.39), kind=kOutput, calls=%fused_computation.60 | convolution fusion | flops 4296015872 | bytes 10485760 | tf_op jit(solution)/shard_map/dot_general | solution.py:500
  286.8 11.9 %convolution_convert_fusion.2 = bf16[2048,1024]{1,0:T(8,128)(2,1)} fusion(bf16[1024,3072]{1,0:T(8,128)(2,1)} %get-tuple-element.30, f32[2048,1024]{1,0:T(8,128)} %copy-done.40, f32[1024]{0:T(1024)S(1)} %copy-done.37), kind=kOutput, calls=%fused_computation.57 | convolution fusion | flops 4318035968 | bytes 14684160 | tf_op jit(solution)/shard_map/dot_general | solution.py:506
  298.7 64.5 %all-reduce.11.cloned.1.call-done = bf16[2048,1024]{1,0:T(8,128)(2,1)} async-done(((bf16[2048,1024]{1,0:T(8,128)(2,1)}), bf16[2048,1024]{1,0:T(8,128)(2,1)}) %all-reduce.11.cloned.1.call-update) | async-done | bytes 4194320 | tf_op jit(solution)/shard_map/psum | solution.py:608
  363.2 8.9 %fusion.30 = (f32[1024]{0:T(1024)S(1)}, f32[2048]{0:T(1024)S(1)}, f32[2048]{0:T(1024)S(1)}, f32[1024]{0:T(1024)S(1)}) fusion(bf16[2048,1024]{1,0:T(8,128)(2,1)} %all-reduce.11.cloned.1.call-done, f32[2048]{0:T(1024)S(1)} %add_rsqrt_fusion, f32[2048]{0:T(1024)S(1)} %broadcast_multiply_fusion.4, f32[1024]{0:T(1024)S(1)} %bitcast.63, ...), kind=kLoop, calls=%fused_computation.41 | loop fusion | flops 29353984 | bytes 12632064 | tf_op jit(solution)/shard_map/reduce_sum | solution.py:633
  372.1 7.2 fusion.72
  379.4 3.2 copy-done.9
  382.6 2.7 convert_element_type.124.gh_ref
  385.3 35.9 %attend_back.1 = bf16[2048,768]{1,0:T(8,128)(2,1)} custom-call(bf16[2048,768]{1,0:T(8,128)(2,1)} %copy-done, bf16[1024,256]{1,0:T(8,128)(2,1)} %copy-done.1, bf16[2048,1024]{1,0:T(8,128)(2,1)} %convert_element_type.124.gh_ref, f32[256,2048]{1,0:T(8,128)} %copy-done.2, f32[4,4,512]{2,1,0:T(4,128)} %copy-done.4), custom_call_target="tpu_custom_call" | custom-call | tf_op jit(solution)/shard_map/attend_back/pallas_call | solution.py:226
  421.2 7.8 %convolution_convert_fusion = bf16[2048,1024]{1,0:T(8,128)(2,1)} fusion(bf16[2048,768]{1,0:T(8,128)(2,1)} %attend_back.1, bf16[1024,3072]{1,0:T(8,128)(2,1)} %get-tuple-element.30), kind=kOutput, calls=%fused_computation.55 | convolution fusion | flops 3223322624 | bytes 8912896 | tf_op jit(solution)/shard_map/dot_general | solution.py:506
  429.0 11.3 %convolution_convert_fusion.3 = bf16[1024,1024]{1,0:T(8,128)(2,1)} fusion(bf16[2048,1024]{1,0:T(8,128)(2,1)} %param.22, f32[2048]{0:T(1024)S(1)} %fusion.58, f32[2048,1024]{1,0:T(8,128)} %copy-done.40, f32[1024]{0:T(1024)S(1)} %copy-done.37), kind=kOutput, calls=%fused_computation.59 | convolution fusion | flops 4323278848 | bytes 14692352 | tf_op jit(solution)/shard_map/dot_general | solution.py:500
  440.9 3.5 convolution_convert_fusion.6
  444.5 7.6 %convolution_convert_fusion.5 = bf16[1024,768]{1,0:T(8,128)(2,1)S(1)} fusion(bf16[2048,768]{1,0:T(8,128)(2,1)} %attend_back.1, bf16[2048,1024]{1,0:T(8,128)(2,1)} %param.21, f32[1024]{0:T(1024)S(1)} %bitcast.85, f32[1024]{0:T(1024)S(1)} %bitcast.73, f32[2048]{0:T(1024)S(1)} %copy-done.30, f32[2048]{0:T(1024)S(1)} %broadcast_multiply_fusion.5), kind=kOutput, calls=%fused_computation.67 | convolution fusion | flops 3234594816 | bytes 8937472 | tf_op jit(solution)/shard_map/dot_general | solution.py:500
  452.1 3.2 pad_maximum_fusion.g_ref
  455.3 127.2 %all-reduce.13.cloned.1.call-done = (bf16[2048,1024]{1,0:T(8,128)(2,1)}, bf16[2048,1024]{1,0:T(8,128)(2,1)}) async-done(((bf16[2048,1024]{1,0:T(8,128)(2,1)}, bf16[2048,1024]{1,0:T(8,128)(2,1)}), (bf16[2048,1024]{1,0:T(8,128)(2,1)}, bf16[2048,1024]{1,0:T(8,128)(2,1)})) %all-reduce.13.cloned.1.call-update) | async-done | bytes 8388624 | tf_op jit(solution)/shard_map/psum | solution.py:595
  582.5 6.1 fusion.31
  589.9 90.2 %scatter_gradients.1 = (f32[128,3072]{1,0:T(8,128)S(1)}, f32[8,256]{1,0:T(8,128)S(1)}, f32[8,128]{1,0:T(8,128)S(1)}) custom-call(bf16[1024,3072]{1,0:T(8,128)(2,1)} %pad_maximum_fusion.g_ref, f32[8,8,256]{2,1,0:T(8,128)S(1)} %select_maximum_fusion.vec_ref), custom_call_target="tpu_custom_call" | custom-call | tf_op jit(solution)/shard_map/scatter_gradients/pallas_call | solution.py:470
  682.1 2.5 multiply_subtract_fusion
  684.6 2.1 copy.93
  686.7 1.8 multiply_subtract_fusion.3
  688.6 1.7 copy.90
  690.2 1.7 copy.91
  691.9 1.7 copy.92
  693.5 1.9 copy.74
  695.4 1.0 copy.75
  696.5 2.3 multiply_subtract_fusion.2
  698.8 1.9 copy.87
  700.7 1.9 copy.88
  702.6 1.9 copy.89
  704.6 1.0 copy.94
  705.5 1.0 copy.95
  706.5 1.3 multiply_subtract_fusion.5
  707.8 1.3 multiply_subtract_fusion.4
  709.2 2.6 multiply_subtract_fusion.1
  711.8 14.1 %fusion.15 = (bf16[2048,1024]{1,0:T(8,128)(2,1)}, bf16[2048,1024]{1,0:T(8,128)(2,1)}) fusion(f32[2048,1024]{1,0:T(8,128)} %copy-done.9, bf16[2048,1024]{1,0:T(8,128)(2,1)} %param.21, bf16[2048,1024]{1,0:T(8,128)(2,1)} %get-tuple-element.88, f32[2048]{0:T(1024)} %broadcast_multiply_fusion, f32[2048]{0:T(1024)} %broadcast_multiply_fusion.1, ...), kind=kLoop, calls=%fused_computation.26 | loop fusion | flops 39845888 | bytes 33607680 | tf_op jit(solution)/shard_map/convert_element_type | solution.py:628
  (118 shorter events, 9.6 us)
Async XLA Ops:
  7.2 234.8 %all-reduce.9.cloned.1.call-start = ((), (), s32[]{:S(2)}) async-start(), calls=%async_computation | async-start | bytes 8388608 | tf_op jit(solution)/shard_map/psum | solution.py:588
  9.6 0.7 copy-start.24
  10.3 102.3 %copy-start.38 = (f32[768]{0:T(1024)S(1)}, f32[768]{0:T(1024)}, u32[]{:S(2)}) copy-start(f32[768]{0:T(1024)} %constant.28.clone.1) | copy-start | bytes 9220
  12.5 0.8 copy-start.16
  14.7 97.8 %copy-start.12 = (f32[1024,128]{0,1:T(8,128)}, f32[1024,128]{0,1:T(8,128)S(1)}, u32[]{:S(2)}) copy-start(f32[1024,128]{0,1:T(8,128)S(1)} %copy.67) | copy-start | bytes 1572868
  107.6 336.8 %copy-start.26 = (f32[2048]{0:T(1024)}, f32[2048]{0:T(1024)S(1)}, u32[]{:S(2)}) copy-start(f32[2048]{0:T(1024)S(1)} %broadcast_multiply_fusion.5) | copy-start | bytes 24580
  110.6 1.8 copy-start.29
  111.3 1.2 copy-start.31
  111.3 1.2 copy-start.35
  111.4 1.2 copy-start.33
  112.4 7.1 copy-start.1
  119.6 127.4 %copy-start = (bf16[2048,768]{1,0:T(8,128)(2,1)}, bf16[2048,768]{1,0:T(8,128)(2,1)S(1)}, u32[]{:S(2)}) copy-start(bf16[2048,768]{1,0:T(8,128)(2,1)S(1)} %multiply_convert_fusion.2.qkv_ref) | copy-start | bytes 9437188
  119.6 33.3 %copy-start.25 = (f32[128,768]{1,0:T(8,128)S(1)}, f32[128,768]{1,0:T(8,128)}, u32[]{:S(2)}) copy-start(f32[128,768]{1,0:T(8,128)} %param.30) | copy-start | bytes 1179652
  145.2 1.3 copy-start.2
  146.5 0.6 copy-start.4
  147.1 216.1 %all-reduce.11.cloned.1.call-start = ((), (), s32[]{:S(2)}) async-start(), calls=%async_computation.1 | async-start | bytes 8388608 | tf_op jit(solution)/shard_map/psum | solution.py:608
  159.8 269.2 %copy-start.28 = (f32[2048]{0:T(1024)}, f32[2048]{0:T(1024)S(1)}, u32[]{:S(2)}) copy-start(f32[2048]{0:T(1024)S(1)} %fusion.58) | copy-start | bytes 24580
  242.0 5.1 copy-start.5
  242.0 5.9 copy-start.7
  242.0 8.1 %copy-start.34 = (f32[1,8,128]{2,0,1:T(1,128)S(1)}, f32[1,8,128]{2,0,1:T(1,128)}, u32[]{:S(2)}) copy-start(f32[1,8,128]{2,0,1:T(1,128)} %get-tuple-element.113) | copy-start | bytes 12292
  250.0 4.5 slice-start
  250.0 4.4 slice-start.1
  252.4 2.0 copy-start.15
  254.5 4.7 copy-start.14
  254.5 4.7 copy-start.37
  259.1 9.8 %copy-start.40 = (f32[2048,1024]{1,0:T(8,128)}, f32[2048,1024]{1,0:T(8,128)S(1)}, u32[]{:S(2)}) copy-start(f32[2048,1024]{1,0:T(8,128)S(1)} %fusion.41) | copy-start | bytes 25165828
  269.0 2.0 copy-start.39
  277.4 305.1 %all-reduce.13.cloned.1.call-start = ((), (), s32[]{:S(2)}) async-start(), calls=%async_computation.2 | async-start | bytes 16777216 | tf_op jit(solution)/shard_map/psum | solution.py:595
  363.2 8.9 %copy-start.6 = (bf16[2048,1024]{1,0:T(8,128)(2,1)S(1)}, bf16[2048,1024]{1,0:T(8,128)(2,1)}, u32[]{:S(2)}) copy-start(bf16[2048,1024]{1,0:T(8,128)(2,1)} %param.21) | copy-start | bytes 12582916
  363.2 8.9 %copy-start.8 = (bf16[2048,1024]{1,0:T(8,128)(2,1)S(1)}, bf16[2048,1024]{1,0:T(8,128)(2,1)}, u32[]{:S(2)}) copy-start(bf16[2048,1024]{1,0:T(8,128)(2,1)} %all-reduce.9.cloned.1.call-done) | copy-start | bytes 12582916
  363.2 9.0 %copy-start.10 = (bf16[2048,1024]{1,0:T(8,128)(2,1)S(1)}, bf16[2048,1024]{1,0:T(8,128)(2,1)}, u32[]{:S(2)}) copy-start(bf16[2048,1024]{1,0:T(8,128)(2,1)} %all-reduce.11.cloned.1.call-done) | copy-start | bytes 12582916
  379.4 3.2 copy-start.9
  429.0 11.3 %copy-start.11 = (bf16[2048,768]{1,0:T(8,128)(2,1)S(1)}, bf16[2048,768]{1,0:T(8,128)(2,1)}, u32[]{:S(2)}) copy-start(bf16[2048,768]{1,0:T(8,128)(2,1)} %attend_back.1) | copy-start | bytes 9437188
  429.0 11.9 %copy-start.3 = (f32[256,2048]{1,0:T(8,128)S(1)}, f32[256,2048]{1,0:T(8,128)}, u32[]{:S(2)}) copy-start(f32[256,2048]{1,0:T(8,128)} %copy-done.2) | copy-start | bytes 6291460
  440.3 4.2 copy-start.30
  440.3 4.2 copy-start.32
  440.3 4.2 copy-start.36
  444.5 7.6 %copy-start.22 = (bf16[1024,1024]{1,0:T(8,128)(2,1)S(1)}, bf16[1024,1024]{1,0:T(8,128)(2,1)}, u32[]{:S(2)}) copy-start(bf16[1024,1024]{1,0:T(8,128)(2,1)} %convolution_convert_fusion.4) | copy-start | bytes 6291460
  444.5 7.6 %copy-start.23 = (bf16[1024,1024]{1,0:T(8,128)(2,1)S(1)}, bf16[1024,1024]{1,0:T(8,128)(2,1)}, u32[]{:S(2)}) copy-start(bf16[1024,1024]{1,0:T(8,128)(2,1)} %convolution_convert_fusion.3) | copy-start | bytes 6291460
  452.1 130.4 %copy-start.27 = (f32[2048]{0:T(1024)S(1)}, f32[2048]{0:T(1024)}, u32[]{:S(2)}) copy-start(f32[2048]{0:T(1024)} %copy-done.26) | copy-start | bytes 24580
  455.3 226.8 %copy-start.13 = (f32[1024,128]{0,1:T(8,128)S(1)}, f32[1024,128]{0,1:T(8,128)}, u32[]{:S(2)}) copy-start(f32[1024,128]{0,1:T(8,128)} %copy-done.12) | copy-start | bytes 1572868
  455.3 226.8 %copy-start.19 = (f32[1024,128]{0,1:T(8,128)S(1)}, f32[1024,128]{0,1:T(8,128)}, u32[]{:S(2)}) copy-start(f32[1024,128]{0,1:T(8,128)} %copy.83) | copy-start | bytes 1572868
  588.6 107.9 %copy-start.17 = (f32[128,768]{0,1:T(8,128)S(1)}, f32[128,768]{0,1:T(8,128)}, u32[]{:S(2)}) copy-start(f32[128,768]{0,1:T(8,128)} %copy-done.16) | copy-start | bytes 1179652
  680.1 29.1 %copy-start.18 = (f32[128,1024]{1,0:T(8,128)S(1)}, f32[128,1024]{1,0:T(8,128)}, u32[]{:S(2)}) copy-start(f32[128,1024]{1,0:T(8,128)} %param.26) | copy-start | bytes 1572868
  684.6 20.0 %copy-start.21 = (f32[1024,128]{0,1:T(8,128)S(1)}, f32[1024,128]{0,1:T(8,128)}, u32[]{:S(2)}) copy-start(f32[1024,128]{0,1:T(8,128)} %get-tuple-element.96) | copy-start | bytes 1572868
  684.6 20.9 %copy-start.20 = (f32[1024,128]{0,1:T(8,128)S(1)}, f32[1024,128]{0,1:T(8,128)}, u32[]{:S(2)}) copy-start(f32[1024,128]{0,1:T(8,128)} %get-tuple-element.97) | copy-start | bytes 1572868
Sparse Core Ops, SparseCore 0:
  147.2 94.6 all-reduce.8
  277.5 85.6 all-reduce.10
  429.1 153.3 all-reduce.12

commit v3 on v1

v3 whole, which is shorter than its diff:
```python
import functools
import math

import jax
import jax.numpy as jnp
from jax import lax
from jax.experimental import pallas as pl
from jax.experimental.pallas import tpu as pltpu
from jax.sharding import PartitionSpec as P

F32, BF = jnp.float32, jnp.bfloat16

D = 1024
HEADS = 16
STEP = 10


NORM_EPSILON = 1e-05
CLIP_LIMIT = 1.0
BETA_FIRST = 0.9
BETA_SECOND = 0.95
ADAM_EPSILON = 1e-08
MATRIX_RATE = 0.05
OUTPUT_RATE = 0.2
VECTOR_RATE = 0.6
MATRIX_DECAY = 0.1


def by_kind(values):
    rows, cols = values.shape
    size = D // HEADS
    return jnp.swapaxes(values.reshape(rows, cols // (3 * size), 3, size), 1, 2).reshape(rows, cols)


NN = (((1,), (0,)), ((), ()))
NT = (((1,), (1,)), ((), ()))
TN = (((0,), (0,)), ((), ()))
LOW = -1e30


def dot(left, right, dims=NN):
    return lax.dot_general(left, right, dims, preferred_element_type=F32)


def three(values):
    high = values.astype(BF).astype(F32)
    rest = values - high
    middle = rest.astype(BF).astype(F32)
    return high, middle, rest - middle


def stack_rows(shape, rows):
    ids = lax.broadcasted_iota(jnp.int32, shape, 0)
    out = jnp.zeros(shape, F32)
    for at, row in enumerate(rows):
        out = jnp.where(ids == at, row, out)
    return out.astype(BF)


def head_tile(ref, rows, col, head, d):
    lane = col + (head // 2) * 128
    tile = ref[rows, lane:lane + 128].astype(F32)
    if head % 2:
        tile = pltpu.roll(tile, 64, 1)
    return tile


def fill_keys(qkv_ref, ka_ref, heads, d, slope_of, first, count):
    rows = pl.ds(first, count)
    lanes = lax.broadcasted_iota(jnp.int32, (count, 128), 1)
    position = (lax.broadcasted_iota(jnp.int32, (count, 128), 0) + first).astype(F32)
    for head in range(heads):
        high, middle, low = three(position * slope_of(head))
        tile = head_tile(qkv_ref, rows, heads * d, head, d)
        for at, part in enumerate((high, middle, low, 1.0, 1.0, 1.0)):
            tile = jnp.where(lanes == d + at, part, tile)
        ka_ref[head, rows, :] = jnp.where(lanes < d + 6, tile, 0.0).astype(BF)


def causal(scores, bk, bq):
    kid = lax.broadcasted_iota(jnp.int32, (bk, bq), 0)
    qid = lax.broadcasted_iota(jnp.int32, (bk, bq), 1)
    return jnp.where(kid <= qid, scores, LOW)


def slope_fn(heads, total_heads):
    rank = lax.axis_index("tensor")
    def slope_of(head):
        index = jnp.full((1, 128), rank * heads + head + 1, jnp.int32).astype(F32)
        return jnp.exp2(index * (-8.0 / total_heads))
    return slope_of


def at_dp(index):
    return {"dp": index}


def at_tensor(index):
    return {"tensor": index}


def remote(src, dst, send, recv, where):
    return pltpu.make_async_remote_copy(
        src_ref=src, dst_ref=dst, send_sem=send, recv_sem=recv, device_id=where, device_id_type=pl.DeviceIdType.MESH
    )


def greet(n_dp, n_tensor):
    me, rank = lax.axis_index("dp"), lax.axis_index("tensor")
    barrier = pltpu.get_barrier_semaphore()

    def along_dp(k, c):
        pl.semaphore_signal(barrier, inc=1, device_id=at_dp(lax.rem(me + k, n_dp)), device_id_type=pl.DeviceIdType.MESH)
        return c

    lax.fori_loop(1, n_dp, along_dp, 0)
    for k in range(1, n_tensor):
        pl.semaphore_signal(
            barrier, inc=1, device_id=at_tensor(lax.rem(rank + k, n_tensor)), device_id_type=pl.DeviceIdType.MESH
        )
    pl.semaphore_wait(barrier, n_dp + n_tensor - 2)


def over(body, first, last):
    lax.fori_loop(first, last, lambda k, c: (body(k), c)[1], 0)


def greet_tensor(n_tensor):
    rank = lax.axis_index("tensor")
    barrier = pltpu.get_barrier_semaphore()
    for k in range(1, n_tensor):
        pl.semaphore_signal(
            barrier, inc=1, device_id=at_tensor(lax.rem(rank + k, n_tensor)), device_id_type=pl.DeviceIdType.MESH
        )
    pl.semaphore_wait(barrier, n_tensor - 1)


class Gather:
    def __init__(self, lines, rows, pieces, sems):
        me = lax.axis_index("dp")
        self.me, self.z, self.x = me, me // 2, lax.rem(me, 2)
        self.lines, self.rows, self.pieces, self.sems = lines, rows, pieces, sems
        self.other = at_dp(self.z * 2 + 1 - self.x)

    def own(self, s):
        shard, first, _, cols = self.pieces[s][:4]
        return shard.at[:, pl.ds(first, cols)]

    def spot(self, s, device):
        _, _, first, cols, out = self.pieces[s]
        return out.at[pl.ds(pl.multiple_of(device * self.rows, self.rows), self.rows), pl.ds(first, cols)]

    def to_x(self, s, zz, src):
        return remote(src, self.spot(s, zz * 2 + self.x), self.sems.at[0, s, zz], self.sems.at[1, s, zz], self.other)

    def from_x(self, s, zz):
        spot = self.spot(s, zz * 2 + 1 - self.x)
        return remote(spot, spot, self.sems.at[0, s, zz], self.sems.at[1, s, zz], self.other)

    def to_z(self, s, k):
        target = lax.rem(self.z + k, self.lines) * 2 + self.x
        return remote(self.own(s), self.spot(s, self.me), self.sems.at[2, s, k], self.sems.at[3, s, self.z], at_dp(target))

    def from_z(self, s, zz):
        spot = self.spot(s, zz * 2 + self.x)
        return remote(spot, spot, self.sems.at[2, s, 0], self.sems.at[3, s, zz], self.other)

    def keep(self, s):
        return pltpu.make_async_copy(self.own(s), self.spot(s, self.me), self.sems.at[2, s, 0])

    def begin_z(self, s):
        over(lambda k: self.to_z(s, k).start(), 1, self.lines)
        self.keep(s).start()

    def begin_x(self, s):
        self.to_x(s, self.z, self.own(s)).start()

    def begin(self, s):
        self.begin_z(s)
        self.begin_x(s)

    def forward(self, s):
        def step(k):
            zz = lax.rem(self.z + k, self.lines)
            self.from_z(s, zz).wait_recv()
            self.to_x(s, zz, self.spot(s, zz * 2 + self.x)).start()

        over(step, 1, self.lines)

    def finish(self, s):
        self.keep(s).wait()
        over(lambda k: self.to_z(s, k).wait_send(), 1, self.lines)
        over(lambda zz: self.to_x(s, zz, self.own(s)).wait_send(), 0, self.lines)
        over(lambda zz: self.from_x(s, zz).wait_recv(), 0, self.lines)


class Place:
    def __init__(self):
        rank = lax.axis_index("tensor")
        self.far, self.near = rank // 2, lax.rem(rank, 2)
        self.near_device = at_tensor(self.far * 2 + 1 - self.near)
        self.far_device = at_tensor((1 - self.far) * 2 + self.near)


class BlockSum:
    def __init__(self, place, quarter, part, slot, near_buf, send_buf, far_buf, sems):
        self.place, self.quarter, self.part, self.slot = place, quarter, part, slot
        self.near_buf, self.send_buf, self.far_buf, self.sems = near_buf, send_buf, far_buf, sems

    def rows(self, near, far):
        first = (near * 2 + far) * self.quarter
        return pl.ds(pl.multiple_of(first, self.quarter), self.quarter)

    def half(self, near):
        first = near * 2 * self.quarter
        return pl.ds(pl.multiple_of(first, self.quarter), 2 * self.quarter)

    def to_near(self, b):
        return remote(self.part.at[self.slot(b), self.half(1 - self.place.near)], self.near_buf.at[b],
                      self.sems.at[0, b], self.sems.at[1, b], self.place.near_device)

    def to_far(self, b):
        return remote(self.send_buf.at[b], self.far_buf.at[b], self.sems.at[2, b], self.sems.at[3, b],
                      self.place.far_device)

    def pair(self, b, far):
        own = self.part[self.slot(b), self.rows(self.place.near, far)].astype(F32)
        return own + self.near_buf[b, self.rows(0, far)].astype(F32)

    def begin(self, b):
        self.to_near(b).start()

    def stage(self, b):
        self.to_near(b).wait_recv()
        self.send_buf[b] = self.pair(b, 1 - self.place.far).astype(BF)

    def pass_on(self, b):
        self.stage(b)
        self.to_far(b).start()

    def total(self, b):
        self.to_far(b).wait()
        self.to_near(b).wait_send()
        return self.pair(b, self.place.far) + self.far_buf[b].astype(F32)

    def stage_all(self, b):
        self.stage(b)
        rows = self.rows(0, self.place.far)
        self.near_buf[b, rows] = self.pair(b, self.place.far).astype(BF)
        self.to_near(b).wait_send()

    def late_total(self, b):
        self.to_far(b).wait()
        return self.near_buf[b, self.rows(0, self.place.far)].astype(F32) + self.far_buf[b].astype(F32)


class BlockSpread:
    def __init__(self, place, quarter, out, sems, own=None):
        self.place, self.quarter, self.out, self.sems, self.own = place, quarter, out, sems, own

    def rows(self, b, near, far):
        first = (b * 4 + near * 2 + far) * self.quarter
        return pl.ds(pl.multiple_of(first, self.quarter), self.quarter)

    def spot(self, b, near, far):
        return self.out.at[self.rows(b, near, far)]

    def mine(self, b):
        return self.spot(b, self.place.near, self.place.far)

    def source(self, b):
        return self.mine(b) if self.own is None else self.own.at[b]

    def put(self, b, values):
        if self.own is None:
            self.out[self.rows(b, self.place.near, self.place.far), :] = values
        else:
            self.own[b] = values
        self.to_far(b).start()
        self.to_near(b).start()
        if self.own is not None:
            self.keep(b).start()

    def to_far(self, b):
        return remote(self.source(b), self.mine(b), self.sems.at[0, b], self.sems.at[1, b], self.place.far_device)

    def to_near(self, b):
        return remote(self.source(b), self.mine(b), self.sems.at[2, b], self.sems.at[3, b], self.place.near_device)

    def arrival(self, near, far, b, at):
        spot = self.spot(b, near, far)
        return remote(spot, spot, self.sems.at[at - 1, b], self.sems.at[at, b], self.place.near_device)

    def pass_far(self, b):
        spot = self.spot(b, self.place.near, 1 - self.place.far)
        return remote(spot, spot, self.sems.at[4, b], self.sems.at[5, b], self.place.near_device)

    def keep(self, b):
        return pltpu.make_async_copy(self.own.at[b], self.mine(b), self.sems.at[6, b])

    def relay(self, b):
        self.arrival(self.place.near, 1 - self.place.far, b, 1).wait_recv()
        self.pass_far(b).start()

    def finish(self, b):
        self.to_far(b).wait_send()
        self.to_near(b).wait_send()
        self.pass_far(b).wait_send()
        if self.own is not None:
            self.keep(b).wait()
        self.arrival(1 - self.place.near, self.place.far, b, 3).wait_recv()
        self.arrival(1 - self.place.near, 1 - self.place.far, b, 5).wait_recv()


def normalize(values):
    centred = values - jnp.mean(values, axis=-1, keepdims=True)
    inverse = lax.rsqrt(jnp.mean(centred * centred, axis=-1, keepdims=True) + NORM_EPSILON)
    return (centred * inverse, inverse)


def normalize_back(incoming, normed, inverse, gain):
    scaled = incoming * gain
    return inverse * (
        scaled
        - jnp.mean(scaled, axis=-1, keepdims=True)
        - normed * jnp.mean(scaled * normed, axis=-1, keepdims=True)
    )


def column_sum(values):
    return jnp.sum(values, axis=0, keepdims=True)


def params(collective_id, megabytes):
    return pltpu.CompilerParams(
        collective_id=collective_id, has_side_effects=True, vmem_limit_bytes=megabytes * 2**20
    )


ANYWHERE = pl.BlockSpec(memory_space=pl.ANY)


def fixed(shape):
    return pl.BlockSpec(shape, lambda i: (0,) * len(shape), pipeline_mode=pl.Buffered(1))


def whole(array):
    return fixed(array.shape)


class Scatter:
    def __init__(self, lines, rows, source, first, cols, x_buf, z_buf, total, at, sems, part):
        me = lax.axis_index("dp")
        self.z, self.x = me // 2, lax.rem(me, 2)
        self.lines, self.rows, self.source = lines, rows, source
        self.cols, self.total_cols = pl.ds(first, cols), pl.ds(at, cols)
        self.x_buf, self.z_buf, self.total, self.sems, self.part = x_buf, z_buf, total, sems, part

    def dest(self, k):
        return lax.rem(self.z + 1 + k, self.lines)

    def chunk(self, device):
        return (pl.ds(pl.multiple_of(device * self.rows, self.rows), self.rows), self.cols)

    def sem(self, kind, index):
        return self.sems.at[kind, self.part, index]

    def to_x(self, dz):
        return remote(self.source.at[self.chunk(dz * 2 + 1 - self.x)], self.x_buf.at[dz], self.sem(0, dz),
                      self.sem(1, dz), at_dp(self.z * 2 + 1 - self.x))

    def to_z(self, dz):
        return remote(self.x_buf.at[dz], self.z_buf.at[self.z], self.sem(2, dz), self.sem(3, self.z),
                      at_dp(dz * 2 + self.x))

    def from_z(self, zz):
        return remote(self.z_buf.at[zz], self.z_buf.at[zz], self.sem(2, zz), self.sem(3, zz), at_dp(zz * 2 + self.x))

    def begin(self):
        over(lambda k: self.to_x(self.dest(k)).start(), 0, self.lines)

    def summed(self, dz):
        self.to_x(dz).wait()
        return self.x_buf[dz].astype(F32) + self.source[self.chunk(dz * 2 + self.x)].astype(F32)

    def pass_on(self):
        def step(k):
            dz = self.dest(k)
            self.x_buf[dz] = self.summed(dz).astype(BF)
            self.to_z(dz).start()

        over(step, 0, self.lines - 1)
        self.total[:, self.total_cols] = self.summed(self.z)

    def finish(self):
        def add(k):
            zz = lax.rem(self.z + k, self.lines)
            self.from_z(zz).wait_recv()
            self.total[:, self.total_cols] += self.z_buf[zz].astype(F32)
            self.to_z(zz).wait_send()

        over(add, 1, self.lines)


class Exchange:
    def __init__(self, buf, index, count, where, send, recv):
        self.buf, self.index, self.count, self.where = buf, index, count, where
        self.send, self.recv = send, recv

    def to(self, k):
        other = lax.rem(self.index + k, self.count)
        return remote(self.buf.at[self.index], self.buf.at[self.index], self.send.at[k], self.recv.at[self.index],
                      self.where(other))

    def begin(self, values):
        self.buf[self.index] = values
        over(lambda k: self.to(k).start(), 1, self.count)

    def total(self):
        def arrived(k):
            other = lax.rem(self.index + k, self.count)
            remote(self.buf.at[other], self.buf.at[other], self.send.at[0], self.recv.at[other],
                   self.where(other)).wait_recv()
            self.to(k).wait_send()

        over(arrived, 1, self.count)
        zero = jnp.zeros(self.buf.shape[1:], F32)
        return lax.fori_loop(0, self.count, lambda k, acc: acc + self.buf[k].astype(F32), zero)


def layer_kernel(dims, len_ref, tok_ref, cot_ref, near_shard, far_shard, vec_shard,
                 total_ref, vec_out, square_out, in_out, lay_out, a_hbm, *scratch):
    heads, d, total_heads, bq, nb, n_dp, n_tensor, near_cuts, far_cuts, sum_cuts = dims
    (qkv, ka, big, wj, wo, ac, low, ot, lse, h1, gh1, acc, hid_buf, gu_buf, cot_buf,
     part, near_buf, send_buf, far_buf, part2, near2_buf, send2_buf, far2_buf, x_far, z_far, x_near, z_near,
     vec_buf, vec, vpart, v_buf, s_buf, q_buf, t_buf,
     gn_sems, gf_sems, sum_sems, spread_sems, sf_sems, sn_sems, copy_sems, vs, vr, vs2, vr2, qs, qr, ss, sr, ts, tr) = scratch
    s = pl.program_id(0)
    place = Place()
    me, rank = lax.axis_index("dp"), lax.axis_index("tensor")
    width, feats, hidden = heads * d, ac.shape[1], big.shape[1] // 2
    quarter, lines, rows = bq // 4, n_dp // 2, total_ref.shape[0]
    last = nb - 1
    halves = (slice(0, feats // 2), slice(feats // 2, feats))
    small = n_dp <= 8

    def slot_from(base):
        return lambda b: lax.rem(base + last - b, 3)

    sum1, sum3, sum4 = (
        BlockSum(place, quarter, part, slot_from(k * nb), near_buf, send_buf, far_buf, sum_sems.at[k]) for k in range(3)
    )
    sum2 = BlockSum(place, quarter, part2, lambda b: lax.rem(last - b, 2), near2_buf, send2_buf, far2_buf, sum_sems.at[3])
    spread_c = BlockSpread(place, quarter, ac, spread_sems.at[0])
    spread_low = BlockSpread(place, quarter, low, spread_sems.at[1])
    spread_lay = BlockSpread(place, quarter, lay_out, spread_sems.at[2], send2_buf)
    spread_in = BlockSpread(place, quarter, in_out, spread_sems.at[3], send_buf)
    near_gather = Gather(lines, rows, [(near_shard, first, at, cols, (wj, wo)[index]) for index, first, at, cols in near_cuts],
                         gn_sems)
    far_gather = Gather(lines, rows, [(far_shard, first, first, cols, big) for first, cols in far_cuts], gf_sems)
    grads_near = part2.reshape(2 * bq, feats)
    far_parts = [
        Scatter(lines, rows, big, first, cols, x_far.at[p], z_far.at[p], total_ref, feats + first, sf_sems, p)
        for p, (first, cols) in enumerate(sum_cuts[0])
    ]
    near_parts = [
        Scatter(lines, rows, grads_near, first, cols, x_near.at[p], z_near.at[p], total_ref, first, sn_sems, p)
        for p, (first, cols) in enumerate(sum_cuts[1])
    ]
    vec_gather = Exchange(vec_buf, me, n_dp, at_dp, vs, vr)
    vec_sum = Exchange(v_buf, me, n_dp, at_dp, vs2, vr2)
    vec_tensor = Exchange(s_buf, rank, n_tensor, at_tensor, ss, sr)
    square_sum = Exchange(q_buf, me, n_dp, at_dp, qs, qr)
    square_tensor = Exchange(t_buf, rank, n_tensor, at_tensor, ts, tr)

    def block_rows(b):
        return pl.ds(pl.multiple_of(b * bq, bq), bq)

    def turned_spot(b, first=0, count=None):
        row = pl.multiple_of(lax.rem(b, 2) * width + first, d)
        return (pl.ds(row, width if count is None else count), pl.ds(pl.multiple_of(b // 2 * bq, bq), bq))

    def value_spot(h, b):
        lane = pl.multiple_of(((h % 2) * nb + b) * 128, 128)
        return (h // 2, slice(None), pl.ds(lane, 128))

    def own_rows(b):
        return spread_c.rows(b, place.near, place.far)

    def copy_tokens():
        return pltpu.make_async_copy(tok_ref, low, copy_sems.at[0])

    def copy_a(b):
        return pltpu.make_async_copy(ac.at[block_rows(b)], a_hbm.at[block_rows(b)], copy_sems.at[1 + b])

    def copy_back():
        return pltpu.make_async_copy(a_hbm, ac, copy_sems.at[0])

    def copy_cot(b):
        return pltpu.make_async_copy(cot_ref.at[block_rows(b)], cot_buf, copy_sems.at[0])

    def own_spot(b):
        return pl.ds(pl.multiple_of(b * quarter, quarter), quarter)

    def copy_own(b):
        return pltpu.make_async_copy(tok_ref.at[own_rows(b)], cot_buf.at[own_spot(b)], copy_sems.at[1 + b])

    def norm1(b):
        hidden_one = h1[b] + sum1.total(b)
        h1[b] = hidden_one
        normed, _ = normalize(hidden_one)
        spread_c.put(b, (normed * vec[2:3, :feats] + vec[3:4, :feats]).astype(BF))

    def norm3(b):
        grad_c = sum3.total(b)
        normed, inverse = normalize(h1[b])
        grad_out = gh1[b]
        grad_h = grad_out + normalize_back(grad_c, normed, inverse, vec[2:3, :feats])
        gh1[b] = grad_h
        spread_low.put(b, grad_h.astype(BF))
        vpart[2:3, :feats] += column_sum(grad_c * normed)
        vpart[3:4, :feats] += column_sum(grad_c)
        vpart[4:5, :feats] += column_sum(grad_h)
        vpart[5:6, :feats] += column_sum(grad_out)

    def norm4(b):
        grad_a = sum4.total(b)
        copy_own(b).wait()
        normed, inverse = normalize(cot_buf[own_spot(b), :].astype(F32))
        spread_in.put(b, (gh1[b] + normalize_back(grad_a, normed, inverse, vec[0:1, :feats])).astype(BF))
        vpart[0:1, :feats] += column_sum(grad_a * normed)
        vpart[1:2, :feats] += column_sum(grad_a)

    def layer_block(b):
        ids = lax.broadcasted_iota(jnp.int32, (quarter, 1), 0) + (b * 4 + place.near * 2 + place.far) * quarter
        result = h1[b] + sum2.late_total(b) + vec[5:6, :feats]
        spread_lay.put(b, jnp.where(ids < len_ref[0], result, 0.0).astype(BF))

    forward, middle, backward = 1, 1 + nb, 1 + 2 * nb
    end = 3 * nb
    plan = {}

    def at(step, point, action, *args):
        plan.setdefault((step, point), []).append((action, args))

    for k in range(nb):
        b = last - k
        if k + 1 < nb:
            at(forward + k + 1, "early", sum1.pass_on, b)
            at(middle + k + 1, "early", sum3.pass_on, b)
            at(backward + k + 1, "early", sum4.pass_on, b)
        at(middle + k + 1, "early" if k + 1 < nb else "start", sum2.stage_all, b)
    at(forward + 1, "late", norm1, last)
    at(forward + 2, "late", spread_c.relay, last)
    at(forward + 3, "late", norm1, last - 1)
    at(forward, "late", far_gather.forward, 0)
    at(forward, "late", far_gather.begin_x, 1)
    at(forward + 1, "late", far_gather.begin, 2)
    at(forward + 2, "late", far_gather.forward, 1)
    at(forward + 2, "late", far_gather.begin, 3)
    at(forward + 3, "late", far_gather.begin, 4)
    at(forward + 3, "early", copy_cot(last).start)
    at(middle, "start", sum1.pass_on, 0)
    at(middle, "start", norm1, last - 2)
    at(middle, "start", far_gather.forward, 2)
    at(middle, "start", spread_c.relay, last - 1)
    at(middle, "start", norm1, last - 3)
    at(middle, "start", far_gather.forward, 3)
    at(middle, "start", spread_c.relay, last - 2)
    at(middle, "start", far_gather.forward, 4)
    for piece in range(len(far_cuts)):
        at(middle, "start", far_gather.finish, piece)
    at(middle, "mid", spread_c.relay, last - 3)
    at(middle + 1, "late", norm3, last)
    at(middle + 2, "mid", spread_low.relay, last)
    at(middle + 2, "late", norm3, last - 1)
    at(middle + 3, "mid", spread_low.relay, last - 1)
    at(middle + 3, "late", norm3, last - 2)
    at(backward, "early", sum3.pass_on, 0)
    for k in range(nb):
        at(backward, "early", sum2.to_far(last - k).start)
    at(backward, "mid", norm3, last - 3)
    at(backward, "mid", spread_low.relay, last - 2)
    at(backward, "mid", far_parts[0].pass_on)
    at(backward, "mid", far_parts[2].begin)
    at(backward, "late", spread_low.relay, last - 3)
    at(backward, "late", far_parts[1].pass_on)
    at(backward, "late", far_parts[3].begin)
    at(backward + 1, "mid", far_parts[2].pass_on)
    at(backward + 1, "late", far_parts[3].pass_on)
    at(backward + 1, "late", layer_block, last)
    at(backward + 2, "mid", norm4, last)
    at(backward + 2, "mid", layer_block, last - 1)
    at(backward + 2, "late", layer_block, last - 2)
    at(backward + 3, "mid", norm4, last - 1)
    at(backward + 3, "mid", layer_block, last - 3)

    def run(phase, point):
        for step in range(phase, phase + nb):
            actions = plan.get((step, point), ())
            if actions:
                @pl.when(s == step)
                def _(actions=actions):
                    for action, args in actions:
                        action(*args)

    @pl.when(s == 0)
    def _():
        copy_tokens().start()
        greet(n_dp, n_tensor)
        if small:
            vec_gather.begin(vec_shard[...])
        near_gather.begin(0)
        near_gather.begin(1)
        vpart[...] = jnp.zeros_like(vpart)
        copy_tokens().wait()
        vec[...] = vec_gather.total() if small else vec_shard[...].astype(F32)

        def norm(b):
            span = block_rows(b)
            normed, _ = normalize(low[span, :].astype(F32))
            ac[span, :] = (normed * vec[0:1, :feats] + vec[1:2, :feats]).astype(BF)
            copy_a(b).start()
            h1[b] = low[own_rows(b), :].astype(F32) + vec[4:5, :feats]

        over(norm, 0, nb)
        scale = 1.0 / d**0.5

        def project(kind):
            near_gather.finish(kind)
            cols = slice(kind * width, (kind + 1) * width)

            def step(b):
                span = block_rows(b)
                out = dot(ac[span, :], wj[:, cols])
                if kind == 0:
                    out = (out + vec[6:7, 0:width]) * scale
                if kind == 2:
                    out = out + vec[6:7, width:2 * width]
                qkv[span, cols] = out.astype(BF)

            over(step, 0, nb)

        near_gather.forward(0)
        near_gather.begin(2)
        near_gather.forward(1)
        near_gather.begin(3)
        project(0)
        near_gather.forward(2)
        far_gather.begin_z(0)
        project(1)
        near_gather.forward(3)
        far_gather.begin_z(1)
        project(2)
        far_gather.begin_x(0)

        def fill(b):
            first = pl.multiple_of(b * bq, bq)
            fill_keys(qkv, ka, heads, d, slope_fn(heads, total_heads), first, bq)
            gu_buf[turned_spot(b)] = qkv[pl.ds(first, bq), 2 * width:3 * width].T

        over(fill, 0, nb)
        near_gather.finish(3)
        over(lambda b: copy_a(b).wait(), 0, nb)

    @pl.when((s >= forward) & (s < middle))
    def _():
        i = middle - 1 - s
        qt = qkv[block_rows(i), 0:width].T
        ones = stack_rows((128 - d, bq), (1.0, 1.0, 1.0))
        queries = [jnp.concatenate([qt[h * d:(h + 1) * d], ones], axis=0) for h in range(heads)]
        run(forward, "early")

        def block(j, carry, diagonal):
            out = []
            kr = block_rows(j)
            for h in range(heads):
                m, l, total = carry[h]
                scores = dot(ka[h, kr, :], queries[h])
                if diagonal:
                    scores = causal(scores, bq, bq)
                top = jnp.maximum(m, jnp.max(scores, axis=0, keepdims=True))
                p = jnp.exp(scores - top)
                scale = jnp.exp(m - top)
                l = l * scale + jnp.sum(p, axis=0, keepdims=True)
                total = total * scale + dot(gu_buf[turned_spot(j, h * d, d)], p.astype(BF))
                out.append((top, l, total))
            return tuple(out)

        start = (jnp.full((1, bq), LOW, F32), jnp.zeros((1, bq), F32), jnp.zeros((d, bq), F32))
        carry = lax.fori_loop(0, i, lambda j, c: block(j, c, False), (start,) * heads)
        carry = block(i, carry, True)
        for h in range(heads):
            m, l, total = carry[h]
            ot[i, h * d:(h + 1) * d, :] = total / l
            lse[i, h:h + 1, :] = m + jnp.log(l)
        out_nat = ot[i].astype(BF).T
        for half_cols in halves:
            part[sum1.slot(i), :, half_cols] = dot(out_nat, wo[half_cols, :], NT).astype(BF)
        sum1.begin(i)
        run(forward, "late")

    @pl.when((s >= middle) & (s < backward))
    def _():
        i = backward - 1 - s
        run(middle, "start")

        @pl.when(s == middle)
        def _():
            acc[...] = jnp.zeros_like(acc)

        spread_c.finish(i)
        copy_cot(i).wait()
        row_ids = lax.broadcasted_iota(jnp.int32, (bq, 128), 0) + i * bq
        live = jnp.where(row_ids < len_ref[0], 1.0, 0.0).astype(BF)
        cot_buf[...] = cot_buf[...] * jnp.concatenate([live] * (feats // 128), axis=1)
        gh1[i] = cot_buf[sum1.rows(place.near, place.far), :].astype(F32)
        run(middle, "early")
        root = math.sqrt(2.0 / math.pi)
        step = 256
        for first in range(0, hidden, step):
            cols = slice(first, first + step)
            u = dot(ac[block_rows(i), :], big[:, cols]) + vec[6:7, 2 * width + first:2 * width + first + step]
            square = u * u
            bent = jnp.tanh(root * (u + 0.044715 * (square * u)))
            half = 0.5 * (1.0 + bent)
            hid_buf[:, cols] = (u * half).astype(BF)
            slope = half + 0.5 * u * (1.0 - bent * bent) * (root * (1.0 + 3 * 0.044715 * square))
            grad_u = (dot(cot_buf[...], big[:, hidden + first:hidden + first + step]) * slope).astype(BF)
            gu_buf[:, cols] = grad_u
            vpart[6:7, 2 * width + first:2 * width + first + step] += column_sum(grad_u.astype(F32))
        for half_cols in halves:
            part[sum3.slot(i), :, half_cols] = dot(gu_buf[...], big[half_cols, :hidden], NT).astype(BF)
        sum3.begin(i)
        run(middle, "mid")
        for half_cols in halves:
            part2[sum2.slot(i), :, half_cols] = dot(hid_buf[...], big[half_cols, hidden:], NT).astype(BF)
        sum2.begin(i)
        for r in range(2):
            cols = slice(r * bq, (r + 1) * bq)
            for half_cols in halves:
                acc[r, :, half_cols] += dot(ac[block_rows(i), cols], gu_buf[:, half_cols], TN)
                acc[2 + r, :, half_cols] += dot(cot_buf[:, cols], hid_buf[:, half_cols], TN)

        @pl.when(i > 0)
        def _():
            copy_cot(i - 1).start()

        run(middle, "late")

        @pl.when(s == backward - 1)
        def _():
            for r in range(2):
                span = slice(r * bq, (r + 1) * bq)
                big[span, :hidden] = acc[r].astype(BF)
                big[span, hidden:] = acc[2 + r].astype(BF)
            far_parts[0].begin()
            far_parts[1].begin()
            copy_back().start()
            over(lambda b: copy_own(b).start(), 0, nb)

    @pl.when(s >= backward)
    def _():
        i = end - s
        lanes = lax.broadcasted_iota(jnp.int32, (bq, 128), 1)
        run(backward, "start")

        @pl.when(s == backward)
        def _():
            acc[...] = jnp.zeros_like(acc)

            def fill(b):
                span = block_rows(b)
                gu_buf[turned_spot(b)] = (qkv[span, width:2 * width].astype(F32) * (1.0 / d**0.5)).astype(BF).T
                for h in range(heads):
                    tile = head_tile(qkv, span, 2 * width, h, d)
                    part2[value_spot(h, b)] = jnp.where(lanes < d, tile, jnp.where(lanes < d + 3, 1.0, 0.0)).astype(BF)

            over(fill, 0, nb)

        spread_low.finish(i)
        grad_o = dot(low[block_rows(i), :], wo[...]).astype(BF)
        grad_t = grad_o.T
        q_nat = qkv[block_rows(i), 0:width]
        qt = q_nat.T
        queries, grads, q_pair, g_pair = [], [], [], []
        for h in range(heads):
            hs = slice(h * d, (h + 1) * d)
            delta = jnp.sum(grad_t[hs].astype(F32) * ot[i, hs, :], axis=0, keepdims=True)
            queries.append(jnp.concatenate(
                [qt[hs], stack_rows((128 - d, bq), (1.0, 1.0, 1.0) + three(-lse[i, h:h + 1, :]))], axis=0))
            grads.append(jnp.concatenate([grad_t[hs], stack_rows((128 - d, bq), three(-delta))], axis=0))
            pair = slice((h // 2) * 128, (h // 2) * 128 + 128)
            mine = (lanes < d) if h % 2 == 0 else (lanes >= d)
            q_pair.append(jnp.where(mine, q_nat[:, pair].astype(F32), 0.0).astype(BF))
            g_pair.append(jnp.where(mine, grad_o[:, pair].astype(F32), 0.0).astype(BF))
        run(backward, "early")

        def block(j, carry, diagonal):
            out = []
            kr = block_rows(j)
            for h in range(heads):
                scores = dot(ka[h, kr, :], queries[h])
                if diagonal:
                    scores = causal(scores, bq, bq)
                p = jnp.exp(scores)
                gs = (p * dot(part2[value_spot(h, j)], grads[h])).astype(BF)
                at_k = slice((h // 2) * 128, (h // 2) * 128 + 128)
                at_v = slice(width + (h // 2) * 128, width + (h // 2) * 128 + 128)
                acc[j, :, at_v] += dot(p.astype(BF), g_pair[h])
                acc[j, :, at_k] += dot(gs, q_pair[h])
                out.append(carry[h] + dot(gu_buf[turned_spot(j, h * d, d)], gs))
            return tuple(out)

        carry = lax.fori_loop(0, i, lambda j, c: block(j, c, False), (jnp.zeros((d, bq), F32),) * heads)
        run(backward, "mid")
        carry = block(i, carry, True)
        hid_buf[:, 0:width] = jnp.concatenate(carry, axis=0).T.astype(BF)
        hid_buf[:, width:3 * width] = acc[i, :, 0:2 * width].astype(BF)
        gqkv = hid_buf[:, 0:3 * width]
        for half_cols in halves:
            part[sum4.slot(i), :, half_cols] = dot(gqkv, wj[half_cols, :], NT).astype(BF)
        sum4.begin(i)
        sums = column_sum(gqkv.astype(F32))
        vpart[6:7, 0:width] += sums[:, 0:width]
        vpart[6:7, width:2 * width] += sums[:, 2 * width:]

        @pl.when(s == backward)
        def _():
            copy_back().wait()

        out_nat = ot[i].astype(BF).T
        for r in range(2):
            cols = slice(r * bq, (r + 1) * bq)
            left = ac[block_rows(i), cols]
            acc[2 * r, :, 2 * width:] += dot(left, hid_buf[:, 0:2 * width], TN)
            acc[2 * r + 1, :, 2 * width:3 * width] += dot(left, hid_buf[:, 2 * width:3 * width], TN)
            acc[2 * r + 1, :, 3 * width:] += dot(low[block_rows(i), cols], out_nat, TN)
        run(backward, "late")

    @pl.when(s == end)
    def _():
        sum4.pass_on(0)
        for r in range(2):
            for c in range(2):
                grads_near[r * bq:(r + 1) * bq, c * 2 * width:(c + 1) * 2 * width] = acc[2 * r + c, :, 2 * width:].astype(BF)
        near_parts[0].begin()
        near_parts[1].begin()
        norm4(last - 2)
        near_parts[0].pass_on()
        near_parts[2].begin()
        over(spread_lay.relay, 0, nb)
        norm4(last - 3)
        if small:
            vec_sum.begin(vpart[...])
        near_parts[1].pass_on()
        near_parts[3].begin()
        for part_far in far_parts:
            part_far.finish()
        near_parts[2].pass_on()
        for b in range(last, 0, -1):
            spread_in.relay(b)
        square = jnp.sum(total_ref[:, feats:] * total_ref[:, feats:])
        if small:
            vec_tensor.begin(vec_sum.total())
            near_parts[3].pass_on()
            shared_total = vec_tensor.total()
            row_ids = lax.broadcasted_iota(jnp.int32, vec_out.shape, 0)
            vec_total = jnp.where(row_ids < 6, shared_total, s_buf[rank])
            vec_out[...] = vec_total
            first_row = jnp.where(me == 0, jnp.where(rank == 0, 0, 6), 8)
            vec_kept = jnp.where(row_ids >= first_row, vec_total, 0.0)
            square = square + jnp.sum(vec_kept * vec_kept)
        else:
            near_parts[3].pass_on()
            vec_out[...] = vpart[...]
        for part_near in near_parts:
            part_near.finish()
        square = square + jnp.sum(total_ref[:, :feats] * total_ref[:, :feats])
        square_sum.begin(jnp.full(q_buf.shape[1:], square, F32))
        spread_in.relay(0)
        square_tensor.begin(square_sum.total())
        square_out[...] = square_tensor.total()
        over(spread_lay.finish, 0, nb)
        over(spread_in.finish, 0, nb)


def layer(lengths, tokens, cot, near_shard, far_shard, vec_shard, heads, d, total_heads, bq, n_dp, n_tensor, collective_id):
    n, feats = tokens.shape
    rows = near_shard.shape[0]
    width = heads * d
    hidden = far_shard.shape[1] // 2
    nb, quarter, lines = n // bq, bq // 4, n_dp // 2
    wide = vec_shard.shape[1]
    near_cuts = [(0, k * width, k * width, width) for k in range(3)] + [(1, 3 * width, 0, width)]
    step = hidden // 2
    far_cuts = [(0, step), (step, step), (2 * step, step), (3 * step, step // 2), (3 * step + step // 2, step // 2)]
    sum_far = [(k * step, step) for k in range(4)]
    sum_near = [(k * width, width) for k in range(4)]
    dims = (heads, d, total_heads, bq, nb, n_dp, n_tensor, near_cuts, far_cuts, (sum_far, sum_near))
    vm, dma = pltpu.VMEM, pltpu.SemaphoreType.DMA
    own = (nb, quarter, feats)
    sums = [vm((nb, 2 * quarter, feats), BF), vm(own, BF), vm(own, BF)]
    tile = (8, 128)
    scratch = [
        vm((n, 3 * width), BF), vm((heads, n, 128), BF),
        vm((feats, 2 * hidden), BF), vm((feats, 3 * width), BF), vm((feats, width), BF), vm((n, feats), BF),
        vm((n, feats), BF), vm((nb, width, bq), F32), vm((nb, heads, bq), F32), vm(own, F32), vm(own, F32),
        vm((4, bq, hidden), F32), vm((bq, hidden), BF), vm((bq, hidden), BF), vm((bq, feats), BF),
        vm((3, bq, feats), BF), *sums, vm((2, bq, feats), BF), *sums,
        vm((4, lines, rows, step), BF), vm((4, lines, rows, step), BF),
        vm((4, lines, rows, width), BF), vm((4, lines, rows, width), BF),
        vm((n_dp if n_dp <= 8 else 1,) + vec_shard.shape, BF), vm(vec_shard.shape, F32), vm((8, wide), F32),
        vm((n_dp if n_dp <= 8 else 1, 8, wide), F32), vm((n_tensor, 8, wide), F32), vm((n_dp,) + tile, F32), vm((n_tensor,) + tile, F32),
        dma((4, len(near_cuts), lines)), dma((4, len(far_cuts), lines)), dma((4, 4, nb)), dma((4, 7, nb)),
        dma((4, 4, lines)), dma((4, 4, lines)), dma((1 + nb,)), dma((n_dp,)), dma((n_dp,)), dma((n_dp,)), dma((n_dp,)),
        dma((n_dp,)), dma((n_dp,)), dma((n_tensor,)), dma((n_tensor,)), dma((n_tensor,)), dma((n_tensor,)),
    ]
    shape = jax.ShapeDtypeStruct
    return pl.pallas_call(
        functools.partial(layer_kernel, dims),
        grid=(1 + 3 * nb,),
        in_specs=[pl.BlockSpec(memory_space=pltpu.SMEM)] + [ANYWHERE] * 4 + [whole(vec_shard)],
        out_specs=[fixed((rows, feats + 2 * hidden)), fixed((8, wide)), fixed(tile), ANYWHERE, ANYWHERE, ANYWHERE],
        out_shape=[shape((rows, feats + 2 * hidden), F32), shape((8, wide), F32), shape(tile, F32),
                   shape((n, feats), BF), shape((n, feats), BF), shape((n, feats), BF)],
        scratch_shapes=scratch,
        compiler_params=params(collective_id, 63),
        name="layer",
    )(lengths, tokens, cot, near_shard, far_shard, vec_shard)


def adam_step(master, moment, variance, gradient, rate, decay):
    moment_new = BETA_FIRST * moment + (1.0 - BETA_FIRST) * gradient
    variance_new = BETA_SECOND * variance + (1.0 - BETA_SECOND) * gradient * gradient
    moment_hat = moment_new / (1.0 - BETA_FIRST**STEP)
    variance_hat = variance_new / (1.0 - BETA_SECOND**STEP)
    master_new = master - rate * (
        moment_hat / (jnp.sqrt(variance_hat) + ADAM_EPSILON) + decay * master
    )
    return (master_new, moment_new, variance_new)


def update_kernel(head_size, square_ref, joint_sum, output_sum, widen_sum, narrow_sum, shared_sum, split_sum, *refs):
    ins, outs = refs[:18], refs[18:]
    norm = jnp.sqrt(square_ref[0:1, 0:1])
    factor = jnp.minimum(1.0, CLIP_LIMIT / (norm + 1e-06))

    def step(at, gradient, rate, decay, cols=slice(None)):
        new = adam_step(*[ref[:, cols] for ref in ins[3 * at:3 * at + 3]], factor * gradient, rate, decay)
        for ref, value in zip(outs[3 * at:3 * at + 3], new):
            ref[:, cols] = value

    joint = ins[0].shape[1]
    heads = joint // (3 * head_size)

    def source(piece):
        head, kind = piece // 3, piece % 3
        first = (kind * heads + head) * head_size
        return joint_sum[:, first:first + head_size]

    for piece in range(0, joint // head_size, 2):
        cols = slice(piece * head_size, (piece + 2) * head_size)
        step(0, jnp.concatenate([source(piece), source(piece + 1)], axis=1), MATRIX_RATE, MATRIX_DECAY, cols)
    step(1, output_sum[...].T, OUTPUT_RATE, MATRIX_DECAY)
    step(2, widen_sum[...], MATRIX_RATE, MATRIX_DECAY)
    step(3, narrow_sum[...].T, MATRIX_RATE, MATRIX_DECAY)

    @pl.when(pl.program_id(0) == 0)
    def _():
        step(4, shared_sum[...], VECTOR_RATE, 0.0)
        step(5, split_sum[...], VECTOR_RATE, 0.0)


def update(square, sums, shared, split, states, head_size):
    count = 2
    joint, output, widen, narrow = [states[3 * k].shape for k in range(4)]
    rows = joint[0]

    def halves(shape):
        return pl.BlockSpec((shape[0] // count, shape[1]), lambda i: (i, 0))

    def all_of(shape):
        return pl.BlockSpec(shape, lambda i: (0, 0))

    def columns(first, cols):
        wide = cols // count
        return pl.BlockSpec((rows, wide), lambda i: (0, first // wide + i))

    states_specs = [halves(state.shape) for state in states[:12]] + [all_of(state.shape) for state in states[12:]]
    widen_at, narrow_at = joint[1] + output[0], joint[1] + output[0] + widen[1]
    return pl.pallas_call(
        functools.partial(update_kernel, head_size),
        grid=(count,),
        in_specs=[all_of(square.shape), halves(joint), columns(joint[1], output[0]),
                  pl.BlockSpec((rows // count, widen[1]), lambda i: (i, widen_at // widen[1])),
                  columns(narrow_at, narrow[0]), all_of(shared.shape), all_of(split.shape)] + states_specs,
        out_specs=states_specs,
        out_shape=[jax.ShapeDtypeStruct(state.shape, F32) for state in states],
        compiler_params=pltpu.CompilerParams(vmem_limit_bytes=48 * 2**20),
        name="update",
    )(square, sums, sums, sums, sums, shared, split, *states)


def on_device(
    tokens,
    cotangent,
    lengths,
    joint_weight,
    output_weight,
    widen_weight,
    narrow_weight,
    shared_vectors,
    split_vectors,
    joint_first,
    joint_second,
    output_first,
    output_second,
    widen_first,
    widen_second,
    narrow_first,
    narrow_second,
    shared_first,
    shared_second,
    split_first,
    split_second,
):
    n_dp, n_tensor = lax.axis_size("dp"), lax.axis_size("tensor")
    me = lax.axis_index("dp")
    head_cols = output_weight.shape[0]
    near_shard = jnp.concatenate([by_kind(joint_weight), output_weight.T], axis=1).astype(BF)
    far_shard = jnp.concatenate([widen_weight, narrow_weight.T], axis=1).astype(BF)
    shared_cols, split_cols = shared_vectors.shape[1], split_vectors.shape[1]
    vec_cols = n_dp * max(shared_cols, split_cols)

    def placed(values, cols):
        here = lax.broadcasted_iota(jnp.int32, (1, n_dp * cols), 1) // cols == me
        wide = jnp.where(here, jnp.tile(values, (1, n_dp)), 0.0)
        return jnp.pad(wide, ((0, 0), (0, vec_cols - n_dp * cols)))

    vec_shard = jnp.pad(
        jnp.concatenate([placed(shared_vectors, shared_cols), placed(split_vectors, split_cols)], axis=0),
        ((0, 9), (0, 0)),
    ).astype(BF)
    if n_dp > 8:
        vec_shard = lax.psum(vec_shard, "dp")
    head_size = D // HEADS
    local_heads = head_cols // head_size
    total_rows = tokens.shape[0]
    block = min(512, total_rows)
    sums, vec_sum, square, input_grad, layer_output, _ = layer(
        lengths, tokens, cotangent, near_shard, far_shard, vec_shard, local_heads, head_size, HEADS, block, n_dp,
        n_tensor, 0,
    )
    if n_dp > 8:
        split_all = lax.psum(vec_sum[6:], "dp")
        shared_all = lax.psum(vec_sum[:6], ("dp", "tensor"))
        vec_sum = jnp.concatenate([shared_all, split_all], axis=0)
        square = square + jnp.sum(shared_all * shared_all) + lax.psum(jnp.sum(split_all * split_all), "tensor")
    shared_sum = lax.dynamic_slice(vec_sum, (0, me * shared_cols), (6, shared_cols))
    split_sum = lax.dynamic_slice(vec_sum, (6, me * split_cols), (1, split_cols))
    states = (
        joint_weight, joint_first, joint_second, output_weight, output_first, output_second,
        widen_weight, widen_first, widen_second, narrow_weight, narrow_first, narrow_second,
        shared_vectors, shared_first, shared_second, split_vectors, split_first, split_second,
    )
    updated = update(square, sums, shared_sum, split_sum, states, head_size)
    return (layer_output, input_grad, jnp.sqrt(square[0, 0]), *updated)


def solution(mesh):
    in_specs = (
        P("dp", None),
        P("dp", None),
        P("dp"),
        P("dp", "tensor"),
        P("tensor", "dp"),
        P("dp", "tensor"),
        P("tensor", "dp"),
        P(None, "dp"),
        P("tensor", "dp"),
        P("dp", "tensor"),
        P("dp", "tensor"),
        P("tensor", "dp"),
        P("tensor", "dp"),
        P("dp", "tensor"),
        P("dp", "tensor"),
        P("tensor", "dp"),
        P("tensor", "dp"),
        P(None, "dp"),
        P(None, "dp"),
        P("tensor", "dp"),
        P("tensor", "dp"),
    )
    out_specs = (
        P("dp", None),
        P("dp", None),
        P(),
        P("dp", "tensor"),
        P("dp", "tensor"),
        P("dp", "tensor"),
        P("tensor", "dp"),
        P("tensor", "dp"),
        P("tensor", "dp"),
        P("dp", "tensor"),
        P("dp", "tensor"),
        P("dp", "tensor"),
        P("tensor", "dp"),
        P("tensor", "dp"),
        P("tensor", "dp"),
        P(None, "dp"),
        P(None, "dp"),
        P(None, "dp"),
        P("tensor", "dp"),
        P("tensor", "dp"),
        P("tensor", "dp"),
    )
    return jax.shard_map(
        on_device, mesh=mesh, in_specs=in_specs, out_specs=out_specs, check_vma=False
    )
```

time: 1130 us -> 333 us (0.29)
  waiting for transfers between devices: 724 us -> 0 us
  Pallas kernels: 61.3 us -> 303 us
  blocking collectives: 117 us -> 0 us
  matrix products: 86.5 us -> 0 us
  other arithmetic: 81.9 us -> 2.69 us
  between operations: 22 us -> 3.34 us
    psum x3 -> x0, waiting for transfers between devices: 313 us -> none  [the longest x1 151 us: on_device(): lax.psum(jnp.dot(activated_low, narrow_work, preferred_element_type=jnp.f...]
    pallas_call x2, Pallas kernels: 61.3 us -> 303 us  [the longest x1 298 us: layer(): pl.pallas_call(functools.partial(layer_kernel, dims), grid=(1 + 3 * nb,),...]
    reduce_scatter x3 -> x0, waiting for transfers between devices: 188 us -> none  [the longest x1 68.5 us: on_device(): lax.psum_scatter(grad_widen.astype(BF), 'dp', scatter_dimension=0, tiled=...]
    unnamed x15 -> x0, waiting for transfers between devices: 141 us -> none
    dot_general x10 -> x0, matrix products: 86.5 us -> none  [the longest x3 28.4 us: over_rows(): lax.dot_general(left, right, (((0,), (0,)), ((), ())), preferred_element_...]
    all_gather x3 -> x0, waiting for transfers between devices: 82.3 us -> none  [the longest x1 41.7 us: on_device(): lax.all_gather(narrow_weight.astype(jnp.bfloat16), 'dp', axis=1, tiled=True)]
    all_gather x2 -> x0, blocking collectives: 54.3 us -> none  [the longest x1 28.1 us: on_device(): lax.all_gather(output_weight.astype(jnp.bfloat16), 'dp', axis=1, tiled=True)]
    reduce_sum x14 -> x0, other arithmetic: 44.2 us -> none  [the longest x1 9.01 us: on_device(): jnp.sum(grad_mlp_in * normed_two, axis=0)]
  transfers between devices with their start and end apart: 12 -> 0, of which waited for: 11 -> 0; matrix products, arithmetic and copies ran while one was open for 9% -> 0% of each run, Pallas kernels for 0% -> 0%
where the time goes in v3:
time: 333 us; the launch traced here: 332 us
  Pallas kernels  303 us (91%)
  local copies, waits for them, and re-layouts  23.2 us (7%)
  between operations  3.34 us (1%)
    pallas_call x1, Pallas kernels, layer(): pl.pallas_call(functools.partial(layer_kernel, dims), grid=(1 + 3 * nb,),...  298 us
    unnamed x48, local copies, waits for them, and re-layouts  19.7 us

profile of v3, /device:TPU:0, one launch (start us, length us, event | category | flops | bytes accessed | tf_op | source)
XLA Modules:
  0.0 331.9 jit_solution(12611851402177244712)
XLA Ops:
  0.7 0.0 copy-start.12
  0.7 0.0 copy-start.16
  1.3 1.0 copy.47
  2.4 1.2 copy.45
  3.5 0.1 copy.48
  3.7 0.7 pad_maximum_fusion.1.near_shard
  4.4 1.2 copy.49
  5.6 1.1 convert.29
  6.7 0.8 pad_maximum_fusion.far_shard
  7.5 0.0 copy-done.12
  7.5 0.0 copy-done.16
  7.6 0.1 tile.24
  7.7 0.6 pad.11.vec_shard
  8.3 0.0 copy-start
  8.3 0.0 copy-start.2
  8.3 0.0 copy-start.13
  8.3 0.0 copy-start.14
  8.3 0.0 copy-start.17
  8.4 0.0 copy-start.18
  8.4 297.9 %layer.1 = (f32[128,3072]{1,0:T(8,128)}, f32[8,1536]{1,0:T(8,128)}, f32[8,128]{1,0:T(8,128)}, bf16[2048,1024]{1,0:T(8,128)(2,1)}, bf16[2048,1024]{1,0:T(8,128)(2,1)}, /*index=5*/bf16[2048,1024]{1,0:T(8,128)(2,1)}) custom-call(s32[1]{0:T(128)S(6)} %copy.54.len_ref, bf16[2048,1024]{1,0:T(8,128)(2,1)} %tok_ref.1, bf16[2048,1024]{1,0:T(8,128)(2,1)} %cot_ref.1, ...), custom_call_target="tpu_custom_call" | custom-call | tf_op jit(solution)/shard_map/layer/pallas_call | solution.py:920
  306.2 1.2 slice.3
  308.1 0.7 constant_dynamic-slice_fusion.1.shared_sum
  308.8 0.8 constant_dynamic-slice_fusion.split_sum
  309.6 0.0 copy-done
  309.6 0.0 copy-done.2
  309.6 0.0 copy-done.13
  309.6 0.0 copy-done.14
  309.6 0.0 copy-done.17
  309.6 0.0 copy-done.18
  309.6 0.0 copy-start.1
  309.6 1.0 copy-done.1
  310.7 0.0 copy-start.3
  310.7 0.9 copy-done.3
  311.6 0.0 copy-start.4
  311.6 1.0 copy-done.4
  312.6 0.0 copy-start.5
  312.6 1.0 copy-done.5
  313.7 0.0 copy-start.6
  313.7 1.0 copy-done.6
  314.7 0.0 copy-start.7
  314.7 1.0 copy-done.7
  315.7 0.0 copy-start.8
  315.8 1.0 copy-done.8
  316.7 0.0 copy-start.9
  316.7 1.0 copy-done.9
  317.7 0.0 copy-start.10
  317.7 0.9 copy-done.10
  318.6 0.0 copy-start.11
  318.6 0.9 copy-done.11
  319.6 0.0 copy-start.15
  319.6 0.7 copy-done.15
  320.2 0.0 copy-start.20
  320.2 4.8 %update.1 = (f32[128,768]{1,0:T(8,128)}, f32[128,768]{1,0:T(8,128)}, f32[128,768]{1,0:T(8,128)}, f32[256,128]{1,0:T(8,128)}, f32[256,128]{1,0:T(8,128)}, /*index...) custom-call(f32[8,128]{1,0:T(8,128)S(1)} %copy-done.15, ...), custom_call_target="tpu_custom_call" | custom-call | tf_op jit(solution)/shard_map/update/pallas_call | solution.py:992
  325.0 0.0 copy-done.20
  325.0 0.0 copy-start.19
  325.0 2.1 copy.55
  327.2 1.6 copy-done.19
  328.7 2.0 copy.56
  (7 shorter events, 0.1 us)
Async XLA Ops:
  0.7 6.9 %copy-start.12 = (f32[6,128]{1,0:T(8,128)S(1)}, f32[6,128]{1,0:T(8,128)}, u32[]{:S(2)}) copy-start(f32[6,128]{1,0:T(8,128)} %refs_12_.1) | copy-start | bytes 9220
  0.7 6.9 %copy-start.16 = (f32[1,192]{1,0:T(1,128)S(1)}, f32[1,192]{1,0:T(1,128)}, u32[]{:S(2)}) copy-start(f32[1,192]{1,0:T(1,128)} %refs_15_.1) | copy-start | bytes 2308
  8.3 301.3 %copy-start = (f32[1024,128]{1,0:T(8,128)S(1)}, f32[1024,128]{1,0:T(8,128)}, u32[]{:S(2)}) copy-start(f32[1024,128]{1,0:T(8,128)} %refs_9_.1) | copy-start | bytes 1572868
  8.3 301.3 %copy-start.2 = (f32[128,768]{1,0:T(8,128)S(1)}, f32[128,768]{1,0:T(8,128)}, u32[]{:S(2)}) copy-start(f32[128,768]{1,0:T(8,128)} %refs_0_.1) | copy-start | bytes 1179652
  8.3 301.3 %copy-start.13 = (f32[6,128]{1,0:T(8,128)S(1)}, f32[6,128]{1,0:T(8,128)}, u32[]{:S(2)}) copy-start(f32[6,128]{1,0:T(8,128)} %refs_13_.1) | copy-start | bytes 9220
  8.3 301.3 %copy-start.14 = (f32[6,128]{1,0:T(8,128)S(1)}, f32[6,128]{1,0:T(8,128)}, u32[]{:S(2)}) copy-start(f32[6,128]{1,0:T(8,128)} %refs_14_.1) | copy-start | bytes 9220
  8.3 301.3 %copy-start.17 = (f32[1,192]{1,0:T(1,128)S(1)}, f32[1,192]{1,0:T(1,128)}, u32[]{:S(2)}) copy-start(f32[1,192]{1,0:T(1,128)} %refs_16_.1) | copy-start | bytes 2308
  8.4 301.3 %copy-start.18 = (f32[1,192]{1,0:T(1,128)S(1)}, f32[1,192]{1,0:T(1,128)}, u32[]{:S(2)}) copy-start(f32[1,192]{1,0:T(1,128)} %refs_17_.1) | copy-start | bytes 2308
  309.6 1.0 copy-start.1
  310.7 0.9 copy-start.3
  311.6 1.0 copy-start.4
  312.6 1.0 copy-start.5
  313.7 1.0 copy-start.6
  314.7 1.0 copy-start.7
  315.7 1.0 copy-start.8
  316.7 1.0 copy-start.9
  317.7 0.9 copy-start.10
  318.6 0.9 copy-start.11
  319.6 0.7 copy-start.15
  320.2 4.8 %copy-start.20 = (bf16[2048,1024]{1,0:T(8,128)(2,1)S(1)}, bf16[2048,1024]{1,0:T(8,128)(2,1)}, u32[]{:S(2)}) copy-start(bf16[2048,1024]{1,0:T(8,128)(2,1)} %get-tuple-element.88) | copy-start | bytes 12582916
  325.0 3.7 %copy-start.19 = (bf16[2048,1024]{1,0:T(8,128)(2,1)S(1)}, bf16[2048,1024]{1,0:T(8,128)(2,1)}, u32[]{:S(2)}) copy-start(bf16[2048,1024]{1,0:T(8,128)(2,1)} %get-tuple-element.89) | copy-start | bytes 12582916
